TPU v7x, 32 devices: a whole 2x2x4 slice. The times are simulated.
32 devices in a mesh: tok: 8 (over y, x, core), head: 4 (over z).
Axes of the slice: x: 2, y: 2, z: 4, core: 2. Of those that a mesh axis runs over, the one named last changes fastest.
Arguments:
- hidden: float32 [4096, 5376], P('tok', 'head'), may hold values from -8 to 8
- queries: float32 [4096, 2048], P('tok', 'head'), may hold values from -4000 to 4000
- out_grad: float32 [4096, 2048], P('tok', 'head'), may hold values from -6 to 6
- w_key: float32 [5376, 1024], P('head', 'tok'), may hold values from -1 to 1
- w_value: float32 [5376, 1024], P('head', 'tok'), may hold values from -0.078125 to 0.078125
- fork_tile: int32 [7], replicated, may hold values from 0 to 25, as said below
- live_len: int32 [8], replicated, may hold values from 257 to 512, as said below
Outputs:
- grad_query: float32 [4096, 2048], P('tok', 'head')
- grad_key: float32 [4096, 1024], P('tok', 'head')
- grad_value: float32 [4096, 1024], P('tok', 'head')
- grad_w_key: float32 [5376, 1024], P('head', 'tok')
- grad_w_value: float32 [5376, 1024], P('head', 'tok')
Inputs may be any that keep to these rules, and one draw needn't show every extreme that they name: fork_tile[b - 1] lies in branch b - 1 or b - 2 (branch 0 counts), among that branch's first 2 tiles, and those tiles are live. `live_len`: branch 0 is fully live.
All inputs are finite; a program needn't handle non-finite values.
Results may differ from a plain program's by a relative error of at most 0.0005.
Values sent between devices are 32-bit elements; how exact they have to be, the bound alone decides.
No kernel may reach another device: no remote copies, remote signals or barrier semaphores. Data moves between devices by JAX's collectives and lax.ppermute only.
A program may use at most 128 MiB of HBM per device.

v0:
```python
import jax
import jax.numpy as jnp
from jax import lax
from jax.sharding import PartitionSpec as P

HEAD_DIM = 128
TILE = 128
CAP = 2
TOK_DEV = 512


logit_scale = 168.0 ** (-0.5)
highest = lax.Precision.HIGHEST


def path_table(fork_tile, owners, tile_count):
    initial = jnp.full((owners, owners), -1, jnp.int32)

    def visit_branch(branch, path_rows):
        fork_at = fork_tile[branch - 1]
        parent = fork_at // tile_count
        inherited = path_rows[parent].at[parent].set(fork_at % tile_count)
        return path_rows.at[branch].set(inherited)

    return lax.fori_loop(1, owners, visit_branch, initial)


def visible_mask(entries_row, live_count, row_count, owners):
    slot_index = jnp.arange(owners * CAP * TILE)
    owner_of = slot_index // (CAP * TILE)
    tile_of = slot_index % (CAP * TILE) // TILE
    remote = (tile_of <= entries_row[owner_of])[None, :]
    positions = jnp.arange(row_count)
    local_part = (positions[None, :] <= positions[:, None]) & (positions[None, :] < live_count)
    return jnp.concatenate(
        [jnp.broadcast_to(remote, (row_count, remote.shape[1])), local_part], axis=1
    )


def attend(query_rows, grad_rows, key_rows, value_rows, visible):
    query_heads = query_rows.shape[1] // HEAD_DIM
    kv_heads = key_rows.shape[1] // HEAD_DIM
    group_size = query_heads // kv_heads
    query_grads = []
    key_grads = [jnp.zeros((key_rows.shape[0], HEAD_DIM), jnp.float32) for _ in range(kv_heads)]
    value_grads = [jnp.zeros((key_rows.shape[0], HEAD_DIM), jnp.float32) for _ in range(kv_heads)]
    for head_index in range(query_heads):
        kv_index = head_index // group_size
        query_head = query_rows[:, head_index * HEAD_DIM : (head_index + 1) * HEAD_DIM]
        grad_head = grad_rows[:, head_index * HEAD_DIM : (head_index + 1) * HEAD_DIM]
        key_head = key_rows[:, kv_index * HEAD_DIM : (kv_index + 1) * HEAD_DIM]
        value_head = value_rows[:, kv_index * HEAD_DIM : (kv_index + 1) * HEAD_DIM]
        scores = jnp.dot(query_head, key_head.T, precision=highest) * logit_scale
        scores = jnp.where(visible, scores, -1e30)
        largest = jnp.max(scores, axis=1, keepdims=True)
        weights = jnp.where(visible, jnp.exp(scores - largest), 0.0)
        weights = weights / jnp.sum(weights, axis=1, keepdims=True)
        output = jnp.dot(weights, value_head, precision=highest)
        delta_row = jnp.sum(grad_head * output, axis=1, keepdims=True)
        grad_prob = jnp.dot(grad_head, value_head.T, precision=highest)
        grad_score = weights * (grad_prob - delta_row)
        query_grads.append(jnp.dot(grad_score, key_head, precision=highest) * logit_scale)
        key_grads[kv_index] = (
            key_grads[kv_index] + jnp.dot(grad_score.T, query_head, precision=highest) * logit_scale
        )
        value_grads[kv_index] = value_grads[kv_index] + jnp.dot(
            weights.T, grad_head, precision=highest
        )
    return (
        jnp.concatenate(query_grads, axis=1),
        jnp.concatenate(key_grads, axis=1),
        jnp.concatenate(value_grads, axis=1),
    )


def shards(hidden, queries, out_grad, w_key, w_value, fork_tile, live_len):
    owners = lax.axis_size("tok")
    branch = lax.axis_index("tok")
    stacked = jnp.stack([w_key, w_value])
    partials = jnp.einsum(
        "td,sdc->stc", hidden, lax.all_gather(stacked, "tok", axis=2, tiled=True), precision=highest
    )
    projected = lax.psum_scatter(partials, "head", scatter_dimension=2, tiled=True)
    fork_span = CAP * TILE
    remote_count = owners * fork_span
    fork_rows = lax.all_gather(projected[:, :fork_span], "tok", axis=1, tiled=True)
    path_rows = path_table(fork_tile, owners, TOK_DEV // TILE)
    visible = visible_mask(path_rows[branch], live_len[branch], TOK_DEV, owners)
    live_rows = (jnp.arange(TOK_DEV) < live_len[branch]).astype(jnp.float32)[:, None]
    key_rows = jnp.concatenate([fork_rows[0], projected[0]], axis=0)
    value_rows = jnp.concatenate([fork_rows[1], projected[1]], axis=0)
    grad_query, grad_keys, grad_values = attend(
        queries, out_grad * live_rows, key_rows, value_rows, visible
    )
    remote = jnp.stack([grad_keys[:remote_count], grad_values[:remote_count]])
    returned = lax.psum_scatter(remote, "tok", scatter_dimension=1, tiled=True)
    own_grads = jnp.stack([grad_keys[remote_count:], grad_values[remote_count:]])
    own_grads = own_grads.at[:, :fork_span].add(returned)
    every_column = lax.all_gather(own_grads, "head", axis=2, tiled=True)
    summed = lax.psum_scatter(
        jnp.einsum("stc,td->csd", every_column, hidden, precision=highest),
        "tok",
        scatter_dimension=0,
        tiled=True,
    )
    grad_w_key = summed[:, 0, :].T
    grad_w_value = summed[:, 1, :].T
    return (grad_query, own_grads[0], own_grads[1], grad_w_key, grad_w_value)


def solution(mesh):
    placed = (
        P("tok", "head"),
        P("tok", "head"),
        P("tok", "head"),
        P("head", "tok"),
        P("head", "tok"),
        P(),
        P(),
    )
    return jax.shard_map(
        shards,
        mesh=mesh,
        in_specs=placed,
        out_specs=(
            P("tok", "head"),
            P("tok", "head"),
            P("tok", "head"),
            P("head", "tok"),
            P("head", "tok"),
        ),
        check_vma=False,
    )
```

profile of v0, /device:TPU:0, one launch (start us, length us, event | category | flops | bytes accessed | tf_op | source)
XLA Modules:
  0.0 622.9 jit_solution(1389625070493020375)
XLA Ops:
  9.9 70.4 %all-gather.4.cloned.1.call-done = f32[2,1344,1024]{2,1,0:T(8,128)} async-done(((f32[2,1344,128]{2,1,0:T(8,128)}), f32[2,1344,1024]{2,1,0:T(8,128)}) %all-gather.4.cloned.1.call-update) | async-done | bytes 11010064 | tf_op jit(solution)/shard_map/all_gather | solution.py:81
  80.3 24.0 %fusion.13 = f32[2,512,1024]{1,2,0:T(8,128)} fusion(f32[2,1344,1024]{2,1,0:T(8,128)} %all-gather.4.cloned.1.call-done, f32[512,1344]{0,1:T(8,128)S(1)} %copy-done), kind=kOutput, calls=%fused_computation.39 | convolution fusion | flops 16911433728 | bytes 17956864 | tf_op jit(solution)/shard_map/td,sdc->stc/dot_general | solution.py:80
  104.3 76.9 %reduce-scatter.4.cloned.1.call-done = f32[2,512,256]{1,2,0:T(8,128)} async-done(((f32[2,512,1024]{1,2,0:T(8,128)}), f32[2,512,256]{1,2,0:T(8,128)}) %reduce-scatter.4.cloned.1.call-update) | async-done | bytes 1048592 | tf_op jit(solution)/shard_map/reduce_scatter | solution.py:83
  186.3 42.4 %while.22 = (s32[]{:T(128)}, s32[8,8]{1,0:T(8,128)S(1)}, s32[7]{0:T(128)S(1)}, s32[]{:T(128)}, s32[]{:T(128)}, /*index=5*/s32[]{:T(128)}, s32[]{:T(128)}, s32[]{...) while((s32[]{:T(128)}, s32[8,8]{1,0:T(8,128)S(1)}, ...), condition=%wide.region_2.3_spmd, body=%wide.region_0.2_spmd.sunk | while | flops 49 | bytes 736 | solution.py:25
  243.8 5.8 fusion.68
  249.6 6.2 fusion.67
  255.8 5.8 fusion.66
  261.6 7.8 %fusion.65 = (f32[512]{0:T(512)S(1)}, f32[512,2560]{0,1:T(8,128)}) fusion(f32[2560,128]{0,1:T(8,128)S(1)} %get-tuple-element.292, f32[512,512]{1,0:T(8,128)S(1)} %copy-done.19, pred[512,512]{0,1:T(32,128)(4,1)S(1)} %fusion.24, pred[2560]{0:T(1024)(128)(4,1)S(1)} %pad.30.clone), kind=kOutput, calls=%fused_computation.131 | convolution fusion | flops 2018508288 | bytes 7083008 | tf_op jit(solution)/shard_map/dot_general | solution.py:53
  269.4 7.4 %fusion.3 = (f32[512]{0:T(512)S(1)}, f32[512]{0:T(512)S(1)}, f32[512]{0:T(512)S(1)}, f32[512]{0:T(512)S(1)}) fusion(f32[512,2560]{0,1:T(8,128)} %get-tuple-element.284, f32[512]{0:T(512)S(1)} %get-tuple-element.283, pred[512,512]{0,1:T(32,128)(4,1)S(1)} %fusion.24, pred[2560]{0:T(1024)(128)(4,1)S(1)} %pad.30.clone, f32[512,2560]{0,1:T(8,128)S(1)} %get-tuple-element.286, ...), kind=kLoop, calls=%fused_computation.25 | loop fusion | flops 17037312 | bytes 21252608 | tf_op jit(solution)/shard_map/reduce_sum | solution.py:57
  276.9 6.5 %fusion.45 = f32[2560,128]{0,1:T(8,128)S(1)} fusion(f32[512,512]{0,1:T(8,128)S(1)} %copy-done.16, f32[512,2560]{0,1:T(8,128)S(1)} %copy-done.13, f32[512]{0:T(512)S(1)} %get-tuple-element.253, f32[512]{0:T(512)S(1)} %get-tuple-element.283, pred[512,512]{0,1:T(32,128)(4,1)S(1)} %fusion.24, pred[2560]{0:T(1024)(128)(4,1)S(1)} %pad.30.clone), kind=kOutput, calls=%fused_computation.98 | convolution fusion | flops 2018508800 | bytes 7085056 | tf_op jit(solution)/shard_map/dot_general | solution.py:66
  292.1 8.8 %fusion.40 = f32[2560,128]{0,1:T(8,128)} fusion(f32[512,512]{0,1:T(8,128)S(1)} %copy-done.16, f32[512,2560]{0,1:T(8,128)S(1)} %get-tuple-element.288, f32[512]{0:T(512)S(1)} %get-tuple-element.255, f32[512]{0:T(512)S(1)} %get-tuple-element.287, pred[512,512]{0,1:T(32,128)(4,1)S(1)} %fusion.24, pred[2560]{0:T(1024)(128)(4,1)S(1)} %pad.30.clone), kind=kOutput, calls=%fused_computation.93 | convolution fusion | flops 2018508800 | bytes 7085056 | tf_op jit(solution)/shard_map/dot_general | solution.py:66
  309.3 5.7 subtract_multiply_fusion.3
  315.0 6.5 %convolution_add_fusion.1 = f32[2560,128]{0,1:T(8,128)S(1)} fusion(f32[2560,128]{0,1:T(8,128)S(1)} %fusion.45, f32[512,512]{0,1:T(8,128)S(1)} %copy-done.16, f32[512,2560]{0,1:T(8,128)S(1)} %get-tuple-element.286, f32[512]{0:T(512)S(1)} %get-tuple-element.254, f32[512]{0:T(512)S(1)} %get-tuple-element.285, pred[512,512]{0,1:T(32,128)(4,1)S(1)} %fusion.24, ...), kind=kOutput, calls=%fused_computation.19 | convolution fusion | flops 2018836480 | bytes 8395776 | tf_op jit(solution)/shard_map/dot_general | solution.py:66
  321.6 5.8 subtract_multiply_fusion.2
  327.4 6.7 %fusion.35 = f32[2560,128]{0,1:T(8,128)S(1)} fusion(f32[512,2560]{0,1:T(8,128)S(1)} %subtract_multiply_fusion.3, f32[512,512]{1,0:T(8,128)} %param.16), kind=kOutput, calls=%fused_computation.88 | convolution fusion | flops 2013265920 | bytes 6815744 | tf_op jit(solution)/shard_map/dot_general | solution.py:64
  339.8 6.9 %convolution_add_fusion = f32[2560,128]{0,1:T(8,128)S(1)} fusion(f32[2560,128]{0,1:T(8,128)S(1)} %copy-done.24, f32[512,512]{0,1:T(8,128)S(1)} %copy-done.17, f32[512,2560]{0,1:T(8,128)S(1)} %get-tuple-element.290, f32[512]{0:T(512)S(1)} %get-tuple-element.256, f32[512]{0:T(512)S(1)} %get-tuple-element.289, pred[512,512]{0,1:T(32,128)(4,1)S(1)} %fusion.24, ...), kind=kOutput, calls=%fused_computation.18 | convolution fusion | flops 2018836480 | bytes 8395776 | tf_op jit(solution)/shard_map/dot_general | solution.py:66
  352.3 5.8 fusion.30
  377.2 48.0 %reduce-scatter.6.cloned.1.call-done = f32[2,256,256]{1,2,0:T(8,128)} async-done(((f32[2,2048,256]{1,2,0:T(8,128)}), f32[2,256,256]{1,2,0:T(8,128)}) %reduce-scatter.6.cloned.1.call-update) | async-done | bytes 524304 | tf_op jit(solution)/shard_map/reduce_scatter | solution.py:96
  427.2 80.9 %all-gather.8.cloned.1.call-done = f32[2,512,1024]{1,2,0:T(8,128)} async-done(((f32[2,512,256]{1,2,0:T(8,128)}), f32[2,512,1024]{1,2,0:T(8,128)}) %all-gather.8.cloned.1.call-update) | async-done | bytes 4194320 | tf_op jit(solution)/shard_map/all_gather | solution.py:99
  508.1 22.4 %convolution_bitcast_fusion = f32[1024,2,1344]{0,2,1:T(8,128)} fusion(f32[2,512,1024]{1,2,0:T(8,128)} %all-gather.8.cloned.1.call-done, f32[512,1344]{0,1:T(8,128)S(1)} %copy-done), kind=kOutput, calls=%fused_computation.3 | convolution fusion | flops 16911433728 | bytes 17956864 | tf_op jit(solution)/shard_map/stc,td->csd/dot_general | solution.py:101
  530.5 6.0 convolution_multiply_fusion.4
  536.5 7.0 %convolution_multiply_fusion.6 = f32[512,128]{0,1:T(8,128)S(1)} fusion(f32[512,2560]{0,1:T(8,128)} %copy-done.1, f32[2560,128]{0,1:T(8,128)S(1)} %copy-done.10), kind=kOutput, calls=%fused_computation.60 | convolution fusion | flops 2013331456 | bytes 6815744 | tf_op jit(solution)/shard_map/dot_general | solution.py:62
  543.6 6.4 %convolution_multiply_fusion = f32[512,128]{0,1:T(8,128)S(1)} fusion(f32[512,2560]{0,1:T(8,128)} %copy-done.4, f32[2560,128]{0,1:T(8,128)S(1)} %copy-done.8), kind=kOutput, calls=%fused_computation.54 | convolution fusion | flops 2013331456 | bytes 6815744 | tf_op jit(solution)/shard_map/dot_general | solution.py:62
  561.8 51.4 %reduce-scatter.8.cloned.1.call-done = f32[128,2,1344]{0,2,1:T(8,128)} async-done(((f32[1024,2,1344]{0,2,1:T(8,128)}), f32[128,2,1344]{0,2,1:T(8,128)}) %reduce-scatter.8.cloned.1.call-update) | async-done | bytes 1376272 | tf_op jit(solution)/shard_map/reduce_scatter | solution.py:100
  (156 shorter events, 105.5 us)
Async XLA Ops:
  7.2 73.1 %copy-start = (f32[512,1344]{0,1:T(8,128)S(1)}, f32[512,1344]{0,1:T(8,128)}, u32[]{:S(2)}) copy-start(f32[512,1344]{0,1:T(8,128)} %param.15) | copy-start | bytes 8257540
  7.2 73.1 %all-gather.4.cloned.1.call-start = ((), (), s32[]{:S(2)}) async-start(), calls=%async_computation.3 | async-start | bytes 12386304 | tf_op jit(solution)/shard_map/all_gather | solution.py:81
  9.9 171.3 %reduce-scatter.4.cloned.1.call-start = ((), (), s32[]{:S(2)}) async-start(), calls=%async_computation.4 | async-start | bytes 5242880 | tf_op jit(solution)/shard_map/reduce_scatter | solution.py:83
  104.3 81.4 %copy-start.22 = (s32[8]{0:T(128)S(1)}, s32[8]{0:T(128)}, u32[]{:S(2)}) copy-start(s32[8]{0:T(128)} %param.21) | copy-start | bytes 100
  104.3 82.1 %copy-start.21 = (s32[2]{0:T(128)S(1)}, s32[2]{0:T(128)}, u32[]{:S(2)}) copy-start(s32[2]{0:T(128)} %constant.373.clone.1) | copy-start | bytes 28
  104.3 82.1 %copy-start.23 = (s32[7]{0:T(128)S(1)}, s32[7]{0:T(128)}, u32[]{:S(2)}) copy-start(s32[7]{0:T(128)} %param.20) | copy-start | bytes 88
  104.3 135.5 %all-gather.6.cloned.1.call-start = ((), (), s32[]{:S(2)}) async-start(), calls=%async_computation.5 | async-start | bytes 4718592 | tf_op jit(solution)/shard_map/all_gather | solution.py:86
  183.1 242.0 %reduce-scatter.6.cloned.1.call-start = ((), (), s32[]{:S(2)}) async-start(), calls=%async_computation.6 | async-start | bytes 4718592 | tf_op jit(solution)/shard_map/reduce_scatter | solution.py:96
  243.1 12.7 %copy-start.7 = (f32[2560,128]{0,1:T(8,128)}, f32[2560,128]{0,1:T(8,128)S(1)}, u32[]{:S(2)}) copy-start(f32[2560,128]{0,1:T(8,128)S(1)} %get-tuple-element.291) | copy-start | bytes 3932164
  243.1 18.5 %copy-start.9 = (f32[2560,128]{0,1:T(8,128)}, f32[2560,128]{0,1:T(8,128)S(1)}, u32[]{:S(2)}) copy-start(f32[2560,128]{0,1:T(8,128)S(1)} %get-tuple-element.292) | copy-start | bytes 3932164
  269.4 7.4 %copy-start.13 = (f32[512,2560]{0,1:T(8,128)S(1)}, f32[512,2560]{0,1:T(8,128)}, u32[]{:S(2)}) copy-start(f32[512,2560]{0,1:T(8,128)} %get-tuple-element.284) | copy-start | bytes 15728644
  269.4 7.4 %copy-start.16 = (f32[512,512]{0,1:T(8,128)S(1)}, f32[512,512]{0,1:T(8,128)}, u32[]{:S(2)}) copy-start(f32[512,512]{0,1:T(8,128)} %broadcast_multiply_fusion) | copy-start | bytes 3145732
  315.0 12.3 %copy-start.1 = (f32[512,2560]{0,1:T(8,128)}, f32[512,2560]{0,1:T(8,128)S(1)}, u32[]{:S(2)}) copy-start(f32[512,2560]{0,1:T(8,128)S(1)} %subtract_multiply_fusion.3) | copy-start | bytes 15728644
  321.6 49.2 %copy-start.11 = (f32[2560,128]{0,1:T(8,128)}, f32[2560,128]{0,1:T(8,128)S(1)}, u32[]{:S(2)}) copy-start(f32[2560,128]{0,1:T(8,128)S(1)} %convolution_add_fusion.1) | copy-start | bytes 3932164
  327.4 30.7 %copy-start.3 = (f32[512,2560]{0,1:T(8,128)}, f32[512,2560]{0,1:T(8,128)S(1)}, u32[]{:S(2)}) copy-start(f32[512,2560]{0,1:T(8,128)S(1)} %subtract_multiply_fusion.2) | copy-start | bytes 15728644
  339.8 12.5 %copy-start.2 = (f32[512,2560]{0,1:T(8,128)}, f32[512,2560]{0,1:T(8,128)S(1)}, u32[]{:S(2)}) copy-start(f32[512,2560]{0,1:T(8,128)S(1)} %subtract_multiply_fusion.1) | copy-start | bytes 15728644
  346.6 24.1 %copy-start.12 = (f32[2560,128]{0,1:T(8,128)}, f32[2560,128]{0,1:T(8,128)S(1)}, u32[]{:S(2)}) copy-start(f32[2560,128]{0,1:T(8,128)S(1)} %convolution_add_fusion) | copy-start | bytes 3932164
  352.3 11.5 %copy-start.4 = (f32[512,2560]{0,1:T(8,128)}, f32[512,2560]{0,1:T(8,128)S(1)}, u32[]{:S(2)}) copy-start(f32[512,2560]{0,1:T(8,128)S(1)} %subtract_multiply_fusion) | copy-start | bytes 15728644
  363.8 6.9 %copy-start.5 = (f32[2560,128]{0,1:T(8,128)}, f32[2560,128]{0,1:T(8,128)S(1)}, u32[]{:S(2)}) copy-start(f32[2560,128]{0,1:T(8,128)S(1)} %fusion) | copy-start | bytes 3932164
  373.2 134.9 %all-gather.8.cloned.1.call-start = ((), (), s32[]{:S(2)}) async-start(), calls=%async_computation.7 | async-start | bytes 5242880 | tf_op jit(solution)/shard_map/all_gather | solution.py:99
  427.2 186.0 %reduce-scatter.8.cloned.1.call-start = ((), (), s32[]{:S(2)}) async-start(), calls=%async_computation.8 | async-start | bytes 12386304 | tf_op jit(solution)/shard_map/reduce_scatter | solution.py:100
  530.5 13.1 %copy-start.8 = (f32[2560,128]{0,1:T(8,128)S(1)}, f32[2560,128]{0,1:T(8,128)}, u32[]{:S(2)}) copy-start(f32[2560,128]{0,1:T(8,128)} %copy-done.7) | copy-start | bytes 3932164
  530.5 19.5 %slice-start = ((s8[5242880]{0:T(1024)(128)(4,1)}), s8[4194304]{0:T(1024)(128)(4,1)S(1)}, s32[]{:S(2)}) async-start(s8[5242880]{0:T(1024)(128)(4,1)} %bitcast.103), calls=%async_computation.9 | async-start | bytes 8388608
  536.5 13.5 %slice-start.1 = ((s8[5242880]{0:T(1024)(128)(4,1)}), s8[1048576]{0:T(1024)(128)(4,1)S(1)}, s32[]{:S(2)}) async-start(s8[5242880]{0:T(1024)(128)(4,1)} %bitcast.103), calls=%async_computation.10 | async-start | bytes 2097152
  (9 other events, 34.9 us)
Sparse Core Ops, SparseCore 0:
  10.0 70.2 all-gather.3
  104.4 76.7 reduce-scatter.3
  183.8 38.0 all-gather.5
  373.3 51.8 reduce-scatter.5
  427.3 80.7 all-gather.7
  530.6 82.5 reduce-scatter.7
where the time goes:
time: 632 us; the launch traced here: 623 us
  waiting for transfers between devices  328 us (52%)
  matrix products  187 us (30%)
  other arithmetic  37.1 us (6%)
  local copies, waits for them, and re-layouts  32.9 us (5%)
  loops' own time  23.3 us (4%)
  between operations  15.2 us (2%)
    all_gather x1, waiting for transfers between devices, shards(): every_column = lax.all_gather(own_grads, 'head', axis=2, tiled=True)  80.9 us
    reduce_scatter x1, waiting for transfers between devices, shards(): lax.psum_scatter(partials, 'head', scatter_dimension=2, tiled=True)  76.9 us
    all_gather x1, waiting for transfers between devices, shards(): lax.all_gather(stacked, 'tok', axis=2, tiled=True)  70.4 us
    reduce_scatter x1, waiting for transfers between devices, shards(): lax.psum_scatter(jnp.einsum('stc,td->csd', every_column, hidden, precisio...  51.4 us
    reduce_scatter x1, waiting for transfers between devices, shards(): returned = lax.psum_scatter(remote, 'tok', scatter_dimension=1, tiled=True)  48 us
    dot_general x4, matrix products, attend(): jnp.dot(weights.T, grad_head, precision=highest)  28.7 us
    dot_general x4, matrix products, attend(): scores = jnp.dot(query_head, key_head.T, precision=highest) * logit_scale  25.6 us
    dot_general x1, matrix products, shards(): jnp.einsum('td,sdc->stc', hidden, lax.all_gather(stacked, 'tok', axis=2,...  24 us
  transfers between devices with their start and end apart: 6, of which 5 were waited for; matrix products, arithmetic and copies ran while one was open for 11% of the time, Pallas kernels for 0%

commit v1 on v0

v1 whole, which is shorter than its diff:
```python
import functools

import jax
import jax.numpy as jnp
from jax import lax
from jax.experimental import pallas as pl
from jax.experimental.pallas import tpu as pltpu
from jax.sharding import PartitionSpec as P

HEAD_DIM = 128
TILE = 128
CAP = 2
SPAN = CAP * TILE

logit_scale = 168.0 ** (-0.5)
f32 = jnp.float32
bf16 = jnp.bfloat16
VMEM_LIMIT = 56 * 1024 * 1024


def split(rows):
    high = rows.astype(bf16)
    return high, (rows - high.astype(f32)).astype(bf16)


def pair_cat(rows, axis):
    return jnp.concatenate(split(rows), axis=axis)


def dot(left, right):
    return jnp.dot(left, right, preferred_element_type=f32)


def dot_first(left, right):
    return lax.dot_general(left, right, (((0,), (0,)), ((), ())), preferred_element_type=f32)


def whole_spec(array):
    return pl.BlockSpec(array.shape, lambda *_: (0,) * len(array.shape))


smem_spec = pl.BlockSpec(memory_space=pltpu.SMEM)


def project_body(place_ref, *refs, row_inputs, parts, steps_each):
    x_refs = refs[:row_inputs]
    w_refs = refs[row_inputs : row_inputs + parts]
    out_ref, high_ref, low_ref = refs[row_inputs + parts :]
    step = pl.program_id(0)

    @pl.when(step == 0)
    def _():
        for part in range(parts):
            high, low = split(w_refs[part][...])
            high_ref[:, part * HEAD_DIM : (part + 1) * HEAD_DIM] = high
            low_ref[:, part * HEAD_DIM : (part + 1) * HEAD_DIM] = low

    for source in range(row_inputs):

        @pl.when(step // steps_each == source)
        def _():
            x_high, x_low = split(x_refs[source][...])
            total = dot(x_high, high_ref[...]) + dot(x_high, low_ref[...]) + dot(x_low, high_ref[...])
            for part in range(parts):
                out_ref[place_ref[part]] = total[:, part * HEAD_DIM : (part + 1) * HEAD_DIM]


def project(place, xs, ws):
    rows, depth = xs[0].shape
    parts = len(ws)
    block = 256
    steps_each = rows // block
    steps = steps_each * len(xs)

    def x_map(source):
        return lambda step: (jnp.clip(step - source * steps_each, 0, steps_each - 1), 0)

    return pl.pallas_call(
        functools.partial(project_body, row_inputs=len(xs), parts=parts, steps_each=steps_each),
        grid=(steps,),
        in_specs=[smem_spec]
        + [pl.BlockSpec((block, depth), x_map(source)) for source in range(len(xs))]
        + [whole_spec(w) for w in ws],
        out_specs=pl.BlockSpec((parts, block, HEAD_DIM), lambda step: (0, step, 0)),
        out_shape=jax.ShapeDtypeStruct((parts, rows * len(xs), HEAD_DIM), f32),
        scratch_shapes=[pltpu.VMEM((depth, parts * HEAD_DIM), bf16)] * 2,
        compiler_params=pltpu.CompilerParams(vmem_limit_bytes=VMEM_LIMIT),
        cost_estimate=pl.CostEstimate(
            flops=6 * rows * len(xs) * depth * parts * HEAD_DIM, bytes_accessed=4 * rows * len(xs) * depth, transcendentals=0
        ),
    )(place, *xs, *ws)


def weight_grad_body(place_ref, *refs, row_inputs, parts):
    x_refs = refs[:row_inputs]
    g_ref = refs[row_inputs]
    out_refs = refs[row_inputs + 1 : row_inputs + 1 + parts]
    high_ref, low_ref = refs[row_inputs + 1 + parts :]
    rows = x_refs[0].shape[0]

    @pl.when(pl.program_id(0) == 0)
    def _():
        for part in range(parts):
            high, low = split(g_ref[place_ref[part]])
            high_ref[:, part * HEAD_DIM : (part + 1) * HEAD_DIM] = high
            low_ref[:, part * HEAD_DIM : (part + 1) * HEAD_DIM] = low

    total = jnp.zeros((x_refs[0].shape[1], parts * HEAD_DIM), f32)
    for source in range(row_inputs):
        x_high, x_low = split(x_refs[source][...])
        g_high = high_ref[source * rows : (source + 1) * rows]
        g_low = low_ref[source * rows : (source + 1) * rows]
        total += dot_first(x_high, g_high) + dot_first(x_high, g_low) + dot_first(x_low, g_high)
    for part in range(parts):
        out_refs[part][...] = total[:, part * HEAD_DIM : (part + 1) * HEAD_DIM]


def weight_grad(place, xs, grads):
    rows, depth = xs[0].shape
    parts = grads.shape[0]
    block = 256
    return pl.pallas_call(
        functools.partial(weight_grad_body, row_inputs=len(xs), parts=parts),
        grid=(pl.cdiv(depth, block),),
        in_specs=[smem_spec] + [pl.BlockSpec((rows, block), lambda step: (0, step))] * len(xs) + [whole_spec(grads)],
        out_specs=[pl.BlockSpec((block, HEAD_DIM), lambda step: (step, 0))] * parts,
        out_shape=[jax.ShapeDtypeStruct((depth, HEAD_DIM), f32)] * parts,
        scratch_shapes=[pltpu.VMEM((rows * len(xs), parts * HEAD_DIM), bf16)] * 2,
        compiler_params=pltpu.CompilerParams(vmem_limit_bytes=VMEM_LIMIT),
        cost_estimate=pl.CostEstimate(
            flops=6 * rows * len(xs) * depth * parts * HEAD_DIM, bytes_accessed=4 * rows * len(xs) * depth, transcendentals=0
        ),
    )(place, *xs, grads)


def list_blocks(own_ref, fork_ref, offset_ref, limit_ref, step, tok, owners, halves, tiles, paired):
    branch_slot = step // halves
    half = step % halves
    branch = tok ^ branch_slot
    for block in range(halves):
        offset_ref[block] = (owners + branch_slot * halves + block) * SPAN
        limit_ref[block] = -1
    own_count = half + 1

    def climb(_, carry):
        current, count = carry
        fork_at = fork_ref[jnp.maximum(current - 1, 0)]
        parent = lax.div(fork_at, jnp.int32(tiles))
        inside = lax.rem(fork_at, jnp.int32(tiles))

        @pl.when(current > 0)
        def _():
            offset_ref[count] = ((tok ^ parent) if paired else parent) * SPAN
            limit_ref[count] = (inside + 1) * TILE - 1

        return jnp.where(current > 0, parent, 0), count + (current > 0).astype(jnp.int32)

    _, count = lax.fori_loop(0, owners, climb, (branch, own_count))
    return branch, branch_slot, half, count, own_count


def key_limits(block, limit_ref, own_count, half, live, lanes):
    lane = lax.broadcasted_iota(jnp.int32, (1, lanes), 1)
    position = half * SPAN + lax.rem(lane, jnp.int32(SPAN))
    own_limit = jnp.minimum(position, live - 1) - block * SPAN
    return jnp.where(block < own_count, own_limit, limit_ref[block])


def transposed_pair(rows):
    high, low = split(rows.T)
    return jnp.concatenate([high, high, low, low], axis=0)


def load_rows(ref, half, head):
    return ref[pl.ds(pl.multiple_of(half * SPAN, SPAN), SPAN), head * HEAD_DIM : (head + 1) * HEAD_DIM]


def live_column(half, live):
    position = half * SPAN + lax.broadcasted_iota(jnp.int32, (SPAN, 1), 0)
    return (position < live).astype(f32)


def block_rows(ref, offset):
    return ref[pl.ds(pl.multiple_of(offset, SPAN), SPAN), :]


def slot_rows(block):
    return pl.ds(pl.multiple_of(block * SPAN, SPAN), SPAN)


def stage_rows(target_ref, source_refs, layout):
    for index, start, offset, count in layout:
        for piece in range(0, count, SPAN):
            target_ref[offset + piece : offset + piece + SPAN, :] = pair_cat(
                source_refs[index][start + piece : start + piece + SPAN, :], 1
            )


def write_rows(source_ref, target_refs, layout):
    for index, start, offset, count in layout:
        if index > 0:
            target_refs[index - 1][start : start + count, :] = source_ref[offset : offset + count, :]
    own = layout[0]
    target_refs[-1][...] = source_ref[own[2] : own[2] + own[3], :]
    for index, start, offset, count in layout[1:]:
        if index == 0:
            target_refs[-1][start : start + count, :] += source_ref[offset : offset + count, :]


def scores(keys_ref, offset, queries, limits):
    keys = block_rows(keys_ref, offset)
    result = dot(jnp.concatenate([keys, keys], axis=1), queries)
    row = lax.broadcasted_iota(jnp.int32, result.shape, 0)
    return jnp.where(row <= limits, result, -1e30)


def fold(value, how):
    return how(value.reshape(SPAN // 8, 8, value.shape[1]), axis=0)


def soft_body(tok_ref, fork_ref, live_ref, *refs, conf):
    nb, group, owners, layout, sources, outs = conf["nb"], conf["group"], conf["owners"], conf["layout"], conf["sources"], conf["outs"]
    halves = conf["rows"] // SPAN
    lanes = group * SPAN
    q_refs, g_refs = refs[:nb], refs[nb : 2 * nb]
    key_refs = refs[2 * nb : 2 * nb + sources]
    stats_ref = refs[2 * nb + sources]
    out_refs = refs[2 * nb + sources + 1 : 2 * nb + sources + 1 + outs]
    keys_ref, sum_ref, score_ref, qt_ref, grad_ref, offset_ref, limit_ref = refs[2 * nb + sources + 1 + outs :]
    step = pl.program_id(0)
    tok = tok_ref[0]

    @pl.when(step == 0)
    def _():
        stage_rows(keys_ref, key_refs, layout)
        sum_ref[...] = jnp.zeros_like(sum_ref)

    branch, slot, half, count, own_count = list_blocks(
        tok_ref, fork_ref, offset_ref, limit_ref, step, tok, owners, halves, conf["rows"] // TILE, conf["paired"]
    )
    live = live_ref[branch]
    for source in range(nb):

        @pl.when(slot == source)
        def _():
            for head in range(group):
                qt_ref[:, head * SPAN : (head + 1) * SPAN] = transposed_pair(load_rows(q_refs[source], half, head) * logit_scale)
                grad_ref[head * SPAN : (head + 1) * SPAN, :] = pair_cat(
                    load_rows(g_refs[source], half, head) * live_column(half, live), 1
                )

    def first(block, largest):
        value = scores(keys_ref, offset_ref[block], qt_ref[...], key_limits(block, limit_ref, own_count, half, live, lanes))
        score_ref[slot_rows(block), :] = value
        return jnp.maximum(largest, fold(value, jnp.max))

    largest = lax.fori_loop(0, count, first, jnp.full((8, lanes), -1e30, f32))
    largest = jnp.max(largest, axis=0, keepdims=True)

    def second(block, total):
        value = jnp.exp(score_ref[slot_rows(block), :] - largest)
        score_ref[slot_rows(block), :] = value
        return total + fold(value, jnp.sum)

    total = lax.fori_loop(0, count, second, jnp.zeros((8, lanes), f32))
    inverse = 1.0 / jnp.sum(total, axis=0, keepdims=True)
    stats_ref[0, 0:1, :] = largest
    stats_ref[0, 1:2, :] = inverse

    def third(block, _):
        high, low = split(score_ref[slot_rows(block), :] * inverse)
        grads = grad_ref[...]
        both = dot(high, grads) + dot(low, grads)
        offset = offset_ref[block]
        sum_ref[slot_rows(offset // SPAN), :] += both[:, :HEAD_DIM] + both[:, HEAD_DIM:]
        return 0

    lax.fori_loop(0, count, third, 0)

    @pl.when(step == nb * halves - 1)
    def _():
        write_rows(sum_ref, out_refs, layout)


def grad_body(tok_ref, fork_ref, live_ref, *refs, conf):
    nb, group, owners, layout, sources, outs = conf["nb"], conf["group"], conf["owners"], conf["layout"], conf["sources"], conf["outs"]
    halves = conf["rows"] // SPAN
    lanes = group * SPAN
    q_refs, g_refs = refs[:nb], refs[nb : 2 * nb]
    at = 2 * nb
    key_refs, value_refs = refs[at : at + sources], refs[at + sources : at + 2 * sources]
    at += 2 * sources
    stats_ref = refs[at]
    dq_ref = refs[at + 1]
    out_refs = refs[at + 2 : at + 2 + outs]
    (keys_ref, values_ref, sum_ref, prob_ref, dprob_ref, qt_ref, gt_ref, q_ref, dqt_ref, offset_ref, limit_ref) = refs[at + 2 + outs :]
    step = pl.program_id(0)
    tok = tok_ref[0]

    @pl.when(step == 0)
    def _():
        stage_rows(keys_ref, key_refs, layout)
        stage_rows(values_ref, value_refs, layout)
        sum_ref[...] = jnp.zeros_like(sum_ref)

    branch, slot, half, count, own_count = list_blocks(
        tok_ref, fork_ref, offset_ref, limit_ref, step, tok, owners, halves, conf["rows"] // TILE, conf["paired"]
    )
    live = live_ref[branch]
    for source in range(nb):

        @pl.when(slot == source)
        def _():
            for head in range(group):
                rows = load_rows(q_refs[source], half, head) * logit_scale
                qt_ref[:, head * SPAN : (head + 1) * SPAN] = transposed_pair(rows)
                q_ref[head * SPAN : (head + 1) * SPAN, :] = pair_cat(rows, 1)
                gt_ref[:, head * SPAN : (head + 1) * SPAN] = transposed_pair(
                    load_rows(g_refs[source], half, head) * live_column(half, live)
                )

    largest = stats_ref[0, 0:1, :]
    inverse = stats_ref[0, 1:2, :]

    def first(block, delta):
        offset = offset_ref[block]
        value = scores(keys_ref, offset, qt_ref[...], key_limits(block, limit_ref, own_count, half, live, lanes))
        prob = jnp.exp(value - largest) * inverse
        values = block_rows(values_ref, offset)
        dprob = dot(jnp.concatenate([values, values], axis=1), gt_ref[...])
        prob_ref[slot_rows(block), :] = prob
        dprob_ref[slot_rows(block), :] = dprob
        return delta + fold(prob * dprob, jnp.sum)

    delta = lax.fori_loop(0, count, first, jnp.zeros((8, lanes), f32))
    delta = jnp.sum(delta, axis=0, keepdims=True)
    dqt_ref[...] = jnp.zeros_like(dqt_ref)

    def second(block, _):
        offset = offset_ref[block]
        high, low = split(prob_ref[slot_rows(block), :] * (dprob_ref[slot_rows(block), :] - delta))
        rows = q_ref[...]
        both = dot(high, rows) + dot(low, rows)
        sum_ref[slot_rows(offset // SPAN), :] += both[:, :HEAD_DIM] + both[:, HEAD_DIM:]
        keys = block_rows(keys_ref, offset)
        dqt_ref[...] += dot_first(keys, high) + dot_first(keys, low)
        return 0

    lax.fori_loop(0, count, second, 0)
    folded = (dqt_ref[:HEAD_DIM, :] + dqt_ref[HEAD_DIM:, :]) * logit_scale
    for head in range(group):
        dq_ref[:, head * HEAD_DIM : (head + 1) * HEAD_DIM] = folded[:, head * SPAN : (head + 1) * SPAN].T

    @pl.when(step == nb * halves - 1)
    def _():
        write_rows(sum_ref, out_refs, layout)


def attention_calls(scalars, qs, gs, layout, paired, owners, part_rows):
    rows, width = qs[0].shape
    nb, group, halves = len(qs), width // HEAD_DIM, rows // SPAN
    lanes = group * SPAN
    steps = nb * halves
    conf = dict(nb=nb, group=group, rows=rows, owners=owners, layout=layout, paired=paired, sources=1 + len(part_rows), outs=len(part_rows) + 1)
    table_rows = owners * SPAN + nb * rows
    slots = (owners + halves) * SPAN
    sums = [jax.ShapeDtypeStruct((count, HEAD_DIM), f32) for count in part_rows] + [jax.ShapeDtypeStruct((nb * rows, HEAD_DIM), f32)]
    stats = jax.ShapeDtypeStruct((steps, 8, lanes), f32)
    stats_spec = pl.BlockSpec((1, 8, lanes), lambda step: (step, 0, 0))
    table = pltpu.VMEM((table_rows, 2 * HEAD_DIM), bf16)
    table_sum = pltpu.VMEM((table_rows, HEAD_DIM), f32)
    square = pltpu.VMEM((slots, lanes), f32)
    columns = pltpu.VMEM((4 * HEAD_DIM, lanes), bf16)
    lists = [pltpu.SMEM((owners + halves + 1,), jnp.int32)] * 2
    params = pltpu.CompilerParams(vmem_limit_bytes=VMEM_LIMIT)
    work = 2 * steps * 6 * SPAN * lanes * 2 * HEAD_DIM

    def soft(keys):
        return pl.pallas_call(
            functools.partial(soft_body, conf=conf),
            grid=(steps,),
            in_specs=[smem_spec] * 3 + [whole_spec(a) for a in (*qs, *gs, *keys)],
            out_specs=[stats_spec] + [whole_spec(a) for a in sums],
            out_shape=[stats] + sums,
            scratch_shapes=[table, table_sum, square, columns, pltpu.VMEM((lanes, 2 * HEAD_DIM), bf16)] + lists,
            compiler_params=params,
            cost_estimate=pl.CostEstimate(flops=2 * work, bytes_accessed=4 * rows * width, transcendentals=0),
        )(*scalars, *qs, *gs, *keys)

    def grad(keys, values, stats_in):
        dq = jax.ShapeDtypeStruct((nb * rows, width), f32)
        return pl.pallas_call(
            functools.partial(grad_body, conf=conf),
            grid=(steps,),
            in_specs=[smem_spec] * 3 + [whole_spec(a) for a in (*qs, *gs, *keys, *values)] + [stats_spec],
            out_specs=[pl.BlockSpec((SPAN, width), lambda step: (step, 0))] + [whole_spec(a) for a in sums],
            out_shape=[dq] + sums,
            scratch_shapes=[
                table,
                table,
                table_sum,
                square,
                square,
                columns,
                columns,
                pltpu.VMEM((lanes, 2 * HEAD_DIM), bf16),
                pltpu.VMEM((2 * HEAD_DIM, lanes), f32),
            ]
            + lists,
            compiler_params=params,
            cost_estimate=pl.CostEstimate(flops=4 * work, bytes_accessed=4 * rows * width, transcendentals=0),
        )(*scalars, *qs, *gs, *keys, *values, stats_in)

    return soft, grad


def flip(array, mask):
    count = lax.axis_size("tok")
    return lax.ppermute(array, "tok", [(index, index ^ mask) for index in range(count)])


def gather_square(array, cut):
    across = flip(array, 2)
    down = flip(array, 4)
    return across, down, flip(across[:cut], 4), flip(down[cut:], 2)


def scatter_square(across, down, corner_head, corner_tail, cut):
    from_across = flip(corner_head, 2)
    from_down = flip(corner_tail, 4)
    down = down.at[:cut].add(from_across)
    across = across.at[cut:].add(from_down)
    return flip(across, 2), flip(down, 4)


def shards_paired(hidden, queries, out_grad, w_key, w_value, fork_tile, live_len):
    owners = lax.axis_size("tok")
    depth = lax.axis_size("head")
    tok = lax.axis_index("tok").astype(jnp.int32)
    core = tok % 2
    rows = hidden.shape[0]
    width = queries.shape[1] // 2
    scalars = (tok.reshape(1), fork_tile, live_len)
    place = (tok // 2) ^ jnp.arange(depth, dtype=jnp.int32)
    half_depth = w_key.shape[0] // 2

    def gather_weight(w):
        across, down, head, tail = gather_square(w, half_depth)
        return [w, across, down, jnp.concatenate([head, tail], axis=0)]

    def mine(array):
        return lax.dynamic_slice_in_dim(array, core * width, width, 1)

    def partners(array):
        return flip(lax.dynamic_slice_in_dim(array, (1 - core) * width, width, 1), 1)

    xs = [hidden, flip(hidden, 1)]
    qs = [mine(queries), partners(queries)]
    gs = [mine(out_grad), partners(out_grad)]
    keys = lax.psum_scatter(project(place, xs, gather_weight(w_key)), "head", scatter_dimension=0, tiled=True)[0]
    values = lax.psum_scatter(project(place, xs, gather_weight(w_value)), "head", scatter_dimension=0, tiled=True)[0]

    def lead(array):
        return jnp.concatenate([array[:SPAN], array[rows : rows + SPAN]], axis=0)

    base = owners * SPAN
    layout = (
        (0, 0, base, 2 * rows),
        (0, 0, 0, SPAN),
        (0, rows, SPAN, SPAN),
        (1, 0, 2 * SPAN, 2 * SPAN),
        (2, 0, 4 * SPAN, 2 * SPAN),
        (3, 0, 6 * SPAN, SPAN),
        (4, 0, 7 * SPAN, SPAN),
    )
    soft, grad = attention_calls(scalars, qs, gs, layout, True, owners, (2 * SPAN, 2 * SPAN, SPAN, SPAN))

    def returned(own, across, down, head, tail):
        first, second = scatter_square(across, down, head, tail, SPAN)
        both = first + second
        return own.at[:SPAN].add(both[:SPAN]).at[rows : rows + SPAN].add(both[SPAN:])

    def weight(grads):
        every = lax.all_gather(grads, "head", axis=0, tiled=False)
        own, across, down, corner = weight_grad(place, xs, every)
        first, second = scatter_square(across, down, corner[:half_depth], corner[half_depth:], half_depth)
        return own + first + second

    def home(array):
        kept, received = array[:rows], flip(array[rows:], 1)
        return jnp.where(core == 0, jnp.concatenate([kept, received], axis=1), jnp.concatenate([received, kept], axis=1))

    key_parts = [keys, *gather_square(lead(keys), SPAN)]
    stats, *value_sums = soft(key_parts)
    value_grads = returned(value_sums[-1], *value_sums[:-1])
    grad_w_value = weight(value_grads)
    value_parts = [values, *gather_square(lead(values), SPAN)]
    grad_query, *key_sums = grad(key_parts, value_parts, stats)
    key_grads = returned(key_sums[-1], *key_sums[:-1])
    grad_w_key = weight(key_grads)
    return home(grad_query), home(key_grads), home(value_grads), grad_w_key, grad_w_value


def shards_single(hidden, queries, out_grad, w_key, w_value, fork_tile, live_len):
    owners = lax.axis_size("tok")
    depth = lax.axis_size("head")
    tok = lax.axis_index("tok").astype(jnp.int32)
    scalars = (tok.reshape(1), fork_tile, live_len)
    place = jnp.arange(depth, dtype=jnp.int32)

    def projected(w):
        every = lax.all_gather(w, "tok", axis=1, tiled=True)
        pieces = [every[:, index * HEAD_DIM : (index + 1) * HEAD_DIM] for index in range(depth)]
        return lax.psum_scatter(project(place, [hidden], pieces), "head", scatter_dimension=0, tiled=True)[0]

    keys, values = projected(w_key), projected(w_value)
    layout = ((0, 0, owners * SPAN, hidden.shape[0]), (1, 0, 0, owners * SPAN))
    soft, grad = attention_calls(scalars, [queries], [out_grad], layout, False, owners, (owners * SPAN,))

    def parts(array):
        return [array, lax.all_gather(array[:SPAN], "tok", axis=0, tiled=True)]

    def returned(remote, own):
        return own.at[:SPAN].add(lax.psum_scatter(remote, "tok", scatter_dimension=0, tiled=True))

    def weight(grads):
        every = lax.all_gather(grads, "head", axis=0, tiled=False)
        columns = jnp.concatenate(weight_grad(place, [hidden], every), axis=1)
        return lax.psum_scatter(columns, "tok", scatter_dimension=1, tiled=True)

    key_parts = parts(keys)
    stats, *value_sums = soft(key_parts)
    value_grads = returned(*value_sums)
    grad_query, *key_sums = grad(key_parts, parts(values), stats)
    key_grads = returned(*key_sums)
    return grad_query, key_grads, value_grads, weight(key_grads), weight(value_grads)


def solution(mesh):
    owners, depth = mesh.shape["tok"], mesh.shape["head"]
    paired = owners == 8 and depth == 4

    placed = (P("tok", "head"), P("tok", "head"), P("tok", "head"), P("head", "tok"), P("head", "tok"), P(), P())
    return jax.shard_map(
        shards_paired if paired else shards_single,
        mesh=mesh,
        in_specs=placed,
        out_specs=(P("tok", "head"), P("tok", "head"), P("tok", "head"), P("head", "tok"), P("head", "tok")),
        check_vma=False,
    )
```

time: 632 us -> 393 us (0.62)
  matrix products: 187 us -> 0 us
  waiting for transfers between devices: 328 us -> 198 us
  starting transfers between devices: 0.25 us -> 80.1 us
  Pallas kernels: 0 us -> 64.5 us
  loops' own time: 23.3 us -> 0 us
  other arithmetic: 37.1 us -> 14.8 us
  local copies, waits for them, and re-layouts: 32.9 us -> 18.1 us
    dot_general x26 -> x0, matrix products: 187 us -> none  [the longest x4 28.7 us: attend(): jnp.dot(weights.T, grad_head, precision=highest)]
    reduce_scatter x3 -> x2, waiting for transfers between devices: 176 us -> 46.7 us  [the longest x1 41.6 us: shards_paired(): lax.psum_scatter(project(place, xs, gather_weight(w_value)), 'head', scat...]
    all_gather x3 -> x2, waiting for transfers between devices: 151 us -> 59.1 us  [weight(): every = lax.all_gather(grads, 'head', axis=0, tiled=False)]
    ppermute x0 -> x38, waiting for transfers between devices: none -> 91.6 us  [flip(): lax.ppermute(array, 'tok', [(index, index ^ mask) for index in range(coun...]
    ppermute x0 -> x38, starting transfers between devices: none -> 79.8 us  [flip(): lax.ppermute(array, 'tok', [(index, index ^ mask) for index in range(coun...]
    pallas_call x0 -> x6, Pallas kernels: none -> 64.5 us  [the longest x2 20 us: weight_grad(): pl.pallas_call(functools.partial(weight_grad_body, row_inputs=len(xs), pa...]
    another operation x1 -> x0, loops' own time: 23.3 us -> none  [path_table(): return lax.fori_loop(1, owners, visit_branch, initial)]
    another operation x21 -> x0, other arithmetic: 17.9 us -> none
  transfers between devices with their start and end apart: 6 -> 42, of which waited for: 5 -> 26; matrix products, arithmetic and copies ran while one was open for 11% -> 6% of each run, Pallas kernels for 0% -> 10%
where the time goes in v1:
time: 393 us; the launch traced here: 389 us
  waiting for transfers between devices  198 us (50%)
  starting transfers between devices  80.1 us (20%)
  Pallas kernels  64.5 us (16%)
  local copies, waits for them, and re-layouts  18.1 us (5%)
  other arithmetic  14.8 us (4%)
  between operations  14.2 us (4%)
    ppermute x38, waiting for transfers between devices, flip(): lax.ppermute(array, 'tok', [(index, index ^ mask) for index in range(coun...  91.6 us
    ppermute x38, starting transfers between devices, flip(): lax.ppermute(array, 'tok', [(index, index ^ mask) for index in range(coun...  79.8 us
    all_gather x2, waiting for transfers between devices, weight(): every = lax.all_gather(grads, 'head', axis=0, tiled=False)  59.1 us
    reduce_scatter x1, waiting for transfers between devices, shards_paired(): lax.psum_scatter(project(place, xs, gather_weight(w_value)), 'head', scat...  41.6 us
    pallas_call x2, Pallas kernels, weight_grad(): pl.pallas_call(functools.partial(weight_grad_body, row_inputs=len(xs), pa...  20 us
    pallas_call x2, Pallas kernels, project(): pl.pallas_call(functools.partial(project_body, row_inputs=len(xs), parts=...  19.8 us
    pallas_call x1, Pallas kernels, grad(): pl.pallas_call(functools.partial(grad_body, conf=conf), grid=(steps,), in...  14.1 us
    pallas_call x1, Pallas kernels, soft(): pl.pallas_call(functools.partial(soft_body, conf=conf), grid=(steps,), in...  10.6 us
  transfers between devices with their start and end apart: 42, of which 26 were waited for; matrix products, arithmetic and copies ran while one was open for 6% of the time, Pallas kernels for 10%

profile of v1, /device:TPU:0, one launch (start us, length us, event | category | flops | bytes accessed | tf_op | source)
XLA Modules:
  0.0 389.2 jit_solution(14889720767641608697)
XLA Ops:
  11.8 14.7 %collective-permute-done.4.refs_4_ = f32[1344,128]{1,0:T(8,128)S(1)} collective-permute-done((f32[1344,128]{1,0:T(8,128)}, f32[1344,128]{1,0:T(8,128)S(1)}, u32[]{:S(2)}, u32[]{:S(2)}) %collective-permute-start.4) | collective-permute-done | bytes 688160 | tf_op jit(solution)/shard_map/ppermute | solution.py:419
  31.5 3.3 copy.17.refs_0_
  36.5 3.2 collective-permute-done.5
  43.8 9.9 %shard_map.110 = f32[4,1024,128]{2,1,0:T(8,128)} custom-call(s32[4]{0:T(128)} %iota_xor_fusion.place_ref, f32[512,1344]{1,0:T(8,128)} %copy.17.refs_0_, f32[512,1344]{1,0:T(8,128)} %copy.18.refs_1_, f32[1344,128]{1,0:T(8,128)} %refs_2_.2, f32[1344,128]{1,0:T(8,128)} %copy-done.10, f32[1344,128]{1,0:T(8,128)} %copy-done.9, f32[1344,128]{1,0:T(8,128)} %pad_maximum_fusion.refs_5_), custom_call_target="tpu_custom_call" | custom-call | flops 4227858432 | bytes 5505024 | tf_op jit(solution)/shard_map/pallas_call | solution.py:78
  56.4 13.2 %collective-permute-done.12.refs_4_ = f32[1344,128]{1,0:T(8,128)S(1)} collective-permute-done((f32[1344,128]{1,0:T(8,128)S(1)}, f32[1344,128]{1,0:T(8,128)S(1)}, u32[]{:S(2)}, u32[]{:S(2)}) %collective-permute-start.12) | collective-permute-done | bytes 688160 | tf_op jit(solution)/shard_map/ppermute | solution.py:419
  72.7 5.6 %collective-permute-done.14 = f32[672,128]{1,0:T(8,128)S(1)} collective-permute-done((f32[672,128]{1,0:T(8,128)S(1)}, f32[672,128]{1,0:T(8,128)S(1)}, u32[]{:S(2)}, u32[]{:S(2)}) %collective-permute-start.14) | collective-permute-done | bytes 344096 | tf_op jit(solution)/shard_map/ppermute | solution.py:419
  79.9 9.9 %shard_map.111 = f32[4,1024,128]{2,1,0:T(8,128)} custom-call(s32[4]{0:T(128)} %iota_xor_fusion.place_ref, f32[512,1344]{1,0:T(8,128)} %copy.17.refs_0_, f32[512,1344]{1,0:T(8,128)} %copy.18.refs_1_, f32[1344,128]{1,0:T(8,128)} %refs_2_.3, f32[1344,128]{1,0:T(8,128)} %copy-done.16, f32[1344,128]{1,0:T(8,128)} %copy-done.15, f32[1344,128]{1,0:T(8,128)} %pad_maximum_fusion.1.refs_5_), custom_call_target="tpu_custom_call" | custom-call | flops 4227858432 | bytes 5505024 | tf_op jit(solution)/shard_map/pallas_call | solution.py:78
  93.4 5.1 %reduce-scatter.3.cloned.1.call-done = f32[1,1024,128]{2,1,0:T(8,128)} async-done(((f32[4,1024,128]{2,1,0:T(8,128)}), f32[1,1024,128]{2,1,0:T(8,128)}) %reduce-scatter.3.cloned.1.call-update) | async-done | bytes 524304 | tf_op jit(solution)/shard_map/reduce_scatter | solution.py:460
  102.5 41.6 %reduce-scatter.5.cloned.1.call-done = f32[1,1024,128]{2,1,0:T(8,128)} async-done(((f32[4,1024,128]{2,1,0:T(8,128)}), f32[1,1024,128]{2,1,0:T(8,128)}) %reduce-scatter.5.cloned.1.call-update) | async-done | bytes 524304 | tf_op jit(solution)/shard_map/reduce_scatter | solution.py:461
  148.8 4.3 %collective-permute-done.15.refs_10_ = f32[512,128]{1,0:T(8,128)S(1)} collective-permute-done((f32[512,128]{1,0:T(8,128)S(1)}, f32[512,128]{1,0:T(8,128)S(1)}, u32[]{:S(2)}, u32[]{:S(2)}) %collective-permute-start.15) | collective-permute-done | bytes 262176 | tf_op jit(solution)/shard_map/ppermute | solution.py:419
  159.8 10.6 %shard_map.112 = (f32[4,8,512]{2,1,0:T(8,128)}, f32[512,128]{1,0:T(8,128)}, f32[512,128]{1,0:T(8,128)}, f32[256,128]{1,0:T(8,128)}, f32[256,128]{1,0:T(8,128)}, /*index=5*/f32[1024,128]{1,0:T(8,128)}) custom-call(s32[1]{0:T(128)} %bitcast.tok_ref, s32[7]{0:T(128)} %fork_ref.3, s32[8]{0:T(128)} %live_ref.3, f32[512,256]{1,0:T(8,128)} %get-tuple-element.194.refs_0_, ...), custom_call_target="tpu_custom_call" | custom-call | flops 3221225472 | bytes 524288 | tf_op jit(solution)/shard_map/pallas_call | solution.py:379
  171.1 14.1 %shard_map.113 = (f32[1024,256]{1,0:T(8,128)}, f32[512,128]{1,0:T(8,128)}, f32[512,128]{1,0:T(8,128)}, f32[256,128]{1,0:T(8,128)}, f32[256,128]{1,0:T(8,128)}, /*index=5*/f32[1024,128]{1,0:T(8,128)}) custom-call(s32[1]{0:T(128)} %bitcast.tok_ref, s32[7]{0:T(128)} %fork_ref.3, s32[8]{0:T(128)} %live_ref.3, f32[512,256]{1,0:T(8,128)} %get-tuple-element.194.refs_0_, ...), custom_call_target="tpu_custom_call" | custom-call | flops 6442450944 | bytes 524288 | tf_op jit(solution)/shard_map/pallas_call | solution.py:392
  185.2 21.3 %collective-permute-start.20 = (f32[256,128]{1,0:T(8,128)}, f32[256,128]{1,0:T(8,128)S(1)}, u32[]{:S(2)}, u32[]{:S(2)}) collective-permute-start(f32[256,128]{1,0:T(8,128)} %get-tuple-element.173), channel_id=1, source_target_pairs={{0,16},{4,20},{8,24},{12,28},{16,0},{20,4},{24,8},{28,12},{1,17},{... | collective-permute-start | bytes 393224 | tf_op jit(solution)/shard_map/ppermute | solution.py:419
  206.5 14.6 %collective-permute-start.22 = (f32[256,128]{1,0:T(8,128)}, f32[256,128]{1,0:T(8,128)S(1)}, u32[]{:S(2)}, u32[]{:S(2)}) collective-permute-start(f32[256,128]{1,0:T(8,128)} %get-tuple-element.175), channel_id=1, source_target_pairs={{0,8},{4,12},{8,0},{12,4},{16,24},{20,28},{24,16},{28,20},{1,9},{5... | collective-permute-start | bytes 393224 | tf_op jit(solution)/shard_map/ppermute | solution.py:419
  230.4 3.6 collective-permute-done.23
  239.5 4.3 %collective-permute-done.25 = f32[256,128]{1,0:T(8,128)S(1)} collective-permute-done((f32[256,128]{1,0:T(8,128)S(1)}, f32[256,128]{1,0:T(8,128)S(1)}, u32[]{:S(2)}, u32[]{:S(2)}) %collective-permute-start.25) | collective-permute-done | bytes 131104 | tf_op jit(solution)/shard_map/ppermute | solution.py:419
  246.0 4.2 %collective-permute-done.26 = f32[512,128]{1,0:T(8,128)S(1)} collective-permute-done((f32[512,128]{1,0:T(8,128)S(1)}, f32[512,128]{1,0:T(8,128)S(1)}, u32[]{:S(2)}, u32[]{:S(2)}) %collective-permute-start.26) | collective-permute-done | bytes 262176 | tf_op jit(solution)/shard_map/ppermute | solution.py:419
  256.1 26.5 %all-gather.5.cloned.1.call-done = f32[4096,128]{1,0:T(8,128)} async-done(((f32[1024,128]{1,0:T(8,128)}), f32[4096,128]{1,0:T(8,128)}) %all-gather.5.cloned.1.call-update) | async-done | bytes 2097168 | tf_op jit(solution)/shard_map/all_gather | solution.py:484
  282.6 9.9 %shard_map.114 = (f32[1344,128]{1,0:T(8,128)}, f32[1344,128]{1,0:T(8,128)}, f32[1344,128]{1,0:T(8,128)}, f32[1344,128]{1,0:T(8,128)}) custom-call(s32[4]{0:T(128)} %iota_xor_fusion.place_ref, f32[512,1344]{1,0:T(8,128)} %copy.17.refs_0_, f32[512,1344]{1,0:T(8,128)} %copy.18.refs_1_, f32[4,1024,128]{2,1,0:T(8,128)} %bitcast.16), custom_call_target="tpu_custom_call" | custom-call | flops 4227858432 | bytes 5505024 | tf_op jit(solution)/shard_map/pallas_call | solution.py:122
  296.9 32.6 %all-gather.7.cloned.1.call-done = f32[4096,128]{1,0:T(8,128)} async-done(((f32[1024,128]{1,0:T(8,128)}), f32[4096,128]{1,0:T(8,128)}) %all-gather.7.cloned.1.call-update) | async-done | bytes 2097168 | tf_op jit(solution)/shard_map/all_gather | solution.py:484
  329.5 10.1 %shard_map.115 = (f32[1344,128]{1,0:T(8,128)}, f32[1344,128]{1,0:T(8,128)}, f32[1344,128]{1,0:T(8,128)}, f32[1344,128]{1,0:T(8,128)}) custom-call(s32[4]{0:T(128)} %iota_xor_fusion.place_ref, f32[512,1344]{1,0:T(8,128)} %copy.17.refs_0_, f32[512,1344]{1,0:T(8,128)} %copy.18.refs_1_, f32[4,1024,128]{2,1,0:T(8,128)} %bitcast.17), custom_call_target="tpu_custom_call" | custom-call | flops 4227858432 | bytes 5505024 | tf_op jit(solution)/shard_map/pallas_call | solution.py:122
  344.6 6.1 %collective-permute-done.36 = f32[672,128]{1,0:T(8,128)S(1)} collective-permute-done((f32[672,128]{1,0:T(8,128)S(1)}, f32[672,128]{1,0:T(8,128)S(1)}, u32[]{:S(2)}, u32[]{:S(2)}) %collective-permute-start.36) | collective-permute-done | bytes 344096 | tf_op jit(solution)/shard_map/ppermute | solution.py:419
  357.2 10.9 %collective-permute-done.33 = f32[1344,128]{1,0:T(8,128)S(1)} collective-permute-done((f32[1344,128]{1,0:T(8,128)S(1)}, f32[1344,128]{1,0:T(8,128)S(1)}, u32[]{:S(2)}, u32[]{:S(2)}) %collective-permute-start.33) | collective-permute-done | bytes 688160 | tf_op jit(solution)/shard_map/ppermute | solution.py:419
  370.0 11.4 %collective-permute-done.37 = f32[1344,128]{1,0:T(8,128)S(1)} collective-permute-done((f32[1344,128]{1,0:T(8,128)S(1)}, f32[1344,128]{1,0:T(8,128)S(1)}, u32[]{:S(2)}, u32[]{:S(2)}) %collective-permute-start.37) | collective-permute-done | bytes 688160 | tf_op jit(solution)/shard_map/ppermute | solution.py:419
  (175 shorter events, 84.2 us)
Async XLA Ops:
  7.2 91.4 %reduce-scatter.3.cloned.1.call-start = ((), (), s32[]{:S(2)}) async-start(), calls=%async_computation.2 | async-start | bytes 2621440 | tf_op jit(solution)/shard_map/reduce_scatter | solution.py:460
  7.2 34.3 %collective-permute-start.2 = (f32[512,1344]{0,1:T(8,128)}, f32[512,1344]{0,1:T(8,128)S(1)}, u32[]{:S(2)}, u32[]{:S(2)}) collective-permute-start(f32[512,1344]{0,1:T(8,128)} %param.31), channel_id=1, source_target_pairs={{0,4},{4,0},{8,12},{12,8},{16,20},{20,16},{24,28},{28,24},{1,5},{5... | collective-permute-start | bytes 8257544 | tf_op jit(solution)/shard_map/ppermute | solution.py:419
  7.7 18.8 %collective-permute-start.4 = (f32[1344,128]{1,0:T(8,128)}, f32[1344,128]{1,0:T(8,128)S(1)}, u32[]{:S(2)}, u32[]{:S(2)}) collective-permute-start(f32[1344,128]{1,0:T(8,128)} %refs_2_.2), channel_id=1, source_target_pairs={{0,16},{4,20},{8,24},{12,28},{16,0},{20,4},{24,8},{28,12},{1,17},{... | collective-permute-start | bytes 2064392 | tf_op jit(solution)/shard_map/ppermute | solution.py:419
  10.3 18.1 %collective-permute-start.3 = (f32[1344,128]{1,0:T(8,128)}, f32[1344,128]{1,0:T(8,128)S(1)}, u32[]{:S(2)}, u32[]{:S(2)}) collective-permute-start(f32[1344,128]{1,0:T(8,128)} %refs_2_.2), channel_id=1, source_target_pairs={{0,8},{4,12},{8,0},{12,4},{16,24},{20,28},{24,16},{28,20},{1,9},{5... | collective-permute-start | bytes 2064392 | tf_op jit(solution)/shard_map/ppermute | solution.py:419
  53.7 90.4 %reduce-scatter.5.cloned.1.call-start = ((), (), s32[]{:S(2)}) async-start(), calls=%async_computation.3 | async-start | bytes 2621440 | tf_op jit(solution)/shard_map/reduce_scatter | solution.py:461
  53.8 15.9 %collective-permute-start.12 = (f32[1344,128]{1,0:T(8,128)S(1)}, f32[1344,128]{1,0:T(8,128)S(1)}, u32[]{:S(2)}, u32[]{:S(2)}) collective-permute-start(f32[1344,128]{1,0:T(8,128)S(1)} %copy-done.23), channel_id=1, source_target_pairs={{0,16},{4,20},{8,24},{12,28},{16,0},{20,4},{24,8},{28,12},{1,17},{... | collective-permute-start | bytes 2064392 | tf_op jit(solution)/shard_map/ppermute | solution.py:419
  55.3 16.4 %collective-permute-start.11 = (f32[1344,128]{1,0:T(8,128)S(1)}, f32[1344,128]{1,0:T(8,128)S(1)}, u32[]{:S(2)}, u32[]{:S(2)}) collective-permute-start(f32[1344,128]{1,0:T(8,128)S(1)} %copy-done.23), channel_id=1, source_target_pairs={{0,8},{4,12},{8,0},{12,4},{16,24},{20,28},{24,16},{28,20},{1,9},{5... | collective-permute-start | bytes 2064392 | tf_op jit(solution)/shard_map/ppermute | solution.py:419
  89.9 192.7 %all-gather.5.cloned.1.call-start = ((), (), s32[]{:S(2)}) async-start(), calls=%async_computation.4 | async-start | bytes 2621440 | tf_op jit(solution)/shard_map/all_gather | solution.py:484
  92.0 65.2 %collective-permute-start = (f32[512,256]{1,0:T(8,128)S(1)}, f32[512,256]{1,0:T(8,128)S(1)}, u32[]{:S(2)}, u32[]{:S(2)}) collective-permute-start(f32[512,256]{1,0:T(8,128)S(1)} %get-tuple-element.193), channel_id=1, source_target_pairs={{0,4},{4,0},{8,12},{12,8},{16,20},{20,16},{24,28},{28,24},{1,5},{5... | collective-permute-start | bytes 1572872 | tf_op jit(solution)/shard_map/ppermute | solution.py:419
  92.9 64.9 %collective-permute-start.1 = (f32[512,256]{1,0:T(8,128)S(1)}, f32[512,256]{1,0:T(8,128)}, u32[]{:S(2)}, u32[]{:S(2)}) collective-permute-start(f32[512,256]{1,0:T(8,128)S(1)} %get-tuple-element.191), channel_id=1, source_target_pairs={{0,4},{4,0},{8,12},{12,8},{16,20},{20,16},{24,28},{28,24},{1,5},{5... | collective-permute-start | bytes 1572872 | tf_op jit(solution)/shard_map/ppermute | solution.py:419
  99.5 47.1 %collective-permute-start.7 = (f32[512,128]{1,0:T(8,128)S(1)}, f32[512,128]{1,0:T(8,128)S(1)}, u32[]{:S(2)}, u32[]{:S(2)}) collective-permute-start(f32[512,128]{1,0:T(8,128)S(1)} %pad_maximum_fusion.2), channel_id=1, source_target_pairs={{0,8},{4,12},{8,0},{12,4},{16,24},{20,28},{24,16},{28,20},{1,9},{5... | collective-permute-start | bytes 786440 | tf_op jit(solution)/shard_map/ppermute | solution.py:419
  101.1 47.1 %collective-permute-start.8 = (f32[512,128]{1,0:T(8,128)S(1)}, f32[512,128]{1,0:T(8,128)S(1)}, u32[]{:S(2)}, u32[]{:S(2)}) collective-permute-start(f32[512,128]{1,0:T(8,128)S(1)} %pad_maximum_fusion.2), channel_id=1, source_target_pairs={{0,16},{4,20},{8,24},{12,28},{16,0},{20,4},{24,8},{28,12},{1,17},{... | collective-permute-start | bytes 786440 | tf_op jit(solution)/shard_map/ppermute | solution.py:419
  155.7 14.7 %collective-permute-start.17 = (f32[256,128]{1,0:T(8,128)S(1)}, f32[256,128]{1,0:T(8,128)S(1)}, u32[]{:S(2)}, u32[]{:S(2)}) collective-permute-start(f32[256,128]{1,0:T(8,128)S(1)} %slice.370), channel_id=1, source_target_pairs={{0,16},{4,20},{8,24},{12,28},{16,0},{20,4},{24,8},{28,12},{1,17},{... | collective-permute-start | bytes 393224 | tf_op jit(solution)/shard_map/ppermute | solution.py:419
  185.2 35.9 %collective-permute-start.20 = (f32[256,128]{1,0:T(8,128)}, f32[256,128]{1,0:T(8,128)S(1)}, u32[]{:S(2)}, u32[]{:S(2)}) collective-permute-start(f32[256,128]{1,0:T(8,128)} %get-tuple-element.173), channel_id=1, source_target_pairs={{0,16},{4,20},{8,24},{12,28},{16,0},{20,4},{24,8},{28,12},{1,17},{... | collective-permute-start | bytes 393224 | tf_op jit(solution)/shard_map/ppermute | solution.py:419
  206.5 19.3 %collective-permute-start.22 = (f32[256,128]{1,0:T(8,128)}, f32[256,128]{1,0:T(8,128)S(1)}, u32[]{:S(2)}, u32[]{:S(2)}) collective-permute-start(f32[256,128]{1,0:T(8,128)} %get-tuple-element.175), channel_id=1, source_target_pairs={{0,8},{4,12},{8,0},{12,4},{16,24},{20,28},{24,16},{28,20},{1,9},{5... | collective-permute-start | bytes 393224 | tf_op jit(solution)/shard_map/ppermute | solution.py:419
  237.2 92.3 %all-gather.7.cloned.1.call-start = ((), (), s32[]{:S(2)}) async-start(), calls=%async_computation.5 | async-start | bytes 2621440 | tf_op jit(solution)/shard_map/all_gather | solution.py:484
  253.7 101.2 %collective-permute-start.24 = (f32[512,128]{1,0:T(8,128)}, f32[512,128]{1,0:T(8,128)S(1)}, u32[]{:S(2)}, u32[]{:S(2)}) collective-permute-start(f32[512,128]{1,0:T(8,128)} %get-tuple-element.202), channel_id=1, source_target_pairs={{0,4},{4,0},{8,12},{12,8},{16,20},{20,16},{24,28},{28,24},{1,5},{5... | collective-permute-start | bytes 786440 | tf_op jit(solution)/shard_map/ppermute | solution.py:419
  254.9 101.5 %collective-permute-start.29 = (f32[512,128]{1,0:T(8,128)}, f32[512,128]{1,0:T(8,128)S(1)}, u32[]{:S(2)}, u32[]{:S(2)}) collective-permute-start(f32[512,128]{1,0:T(8,128)} %get-tuple-element.200), channel_id=1, source_target_pairs={{0,4},{4,0},{8,12},{12,8},{16,20},{20,16},{24,28},{28,24},{1,5},{5... | collective-permute-start | bytes 786440 | tf_op jit(solution)/shard_map/ppermute | solution.py:419
  293.7 48.7 %collective-permute-start.32 = (f32[672,128]{1,0:T(8,128)S(1)}, f32[672,128]{1,0:T(8,128)S(1)}, u32[]{:S(2)}, u32[]{:S(2)}) collective-permute-start(f32[672,128]{1,0:T(8,128)S(1)} %get-tuple-element.198), channel_id=1, source_target_pairs={{0,8},{4,12},{8,0},{12,4},{16,24},{20,28},{24,16},{28,20},{1,9},{5... | collective-permute-start | bytes 1032200 | tf_op jit(solution)/shard_map/ppermute | solution.py:419
  295.4 48.5 %collective-permute-start.30 = (f32[672,128]{1,0:T(8,128)S(1)}, f32[672,128]{1,0:T(8,128)S(1)}, u32[]{:S(2)}, u32[]{:S(2)}) collective-permute-start(f32[672,128]{1,0:T(8,128)S(1)} %get-tuple-element.197), channel_id=1, source_target_pairs={{0,16},{4,20},{8,24},{12,28},{16,0},{20,4},{24,8},{28,12},{1,17},{... | collective-permute-start | bytes 1032200 | tf_op jit(solution)/shard_map/ppermute | solution.py:419
  343.9 24.2 %collective-permute-start.33 = (f32[1344,128]{1,0:T(8,128)S(1)}, f32[1344,128]{1,0:T(8,128)S(1)}, u32[]{:S(2)}, u32[]{:S(2)}) collective-permute-start(f32[1344,128]{1,0:T(8,128)S(1)} %add_dynamic-update-slice_fusion.2), channel_id=1, source_target_pairs={{0,16},{4,20},{8,24},{12,28},{16,0},{20,4},{24,8},{28,12},{1,17},{... | collective-permute-start | bytes 2064392 | tf_op jit(solution)/shard_map/ppermute | solution.py:419
  350.7 18.4 %collective-permute-start.31 = (f32[1344,128]{1,0:T(8,128)S(1)}, f32[1344,128]{1,0:T(8,128)S(1)}, u32[]{:S(2)}, u32[]{:S(2)}) collective-permute-start(f32[1344,128]{1,0:T(8,128)S(1)} %add_dynamic-update-slice_fusion.3), channel_id=1, source_target_pairs={{0,8},{4,12},{8,0},{12,4},{16,24},{20,28},{24,16},{28,20},{1,9},{5... | collective-permute-start | bytes 2064392 | tf_op jit(solution)/shard_map/ppermute | solution.py:419
  353.3 28.0 %collective-permute-start.37 = (f32[1344,128]{1,0:T(8,128)S(1)}, f32[1344,128]{1,0:T(8,128)S(1)}, u32[]{:S(2)}, u32[]{:S(2)}) collective-permute-start(f32[1344,128]{1,0:T(8,128)S(1)} %add_dynamic-update-slice_fusion), channel_id=1, source_target_pairs={{0,16},{4,20},{8,24},{12,28},{16,0},{20,4},{24,8},{28,12},{1,17},{... | collective-permute-start | bytes 2064392 | tf_op jit(solution)/shard_map/ppermute | solution.py:419
  354.9 26.8 %collective-permute-start.35 = (f32[1344,128]{1,0:T(8,128)S(1)}, f32[1344,128]{1,0:T(8,128)S(1)}, u32[]{:S(2)}, u32[]{:S(2)}) collective-permute-start(f32[1344,128]{1,0:T(8,128)S(1)} %add_dynamic-update-slice_fusion.1), channel_id=1, source_target_pairs={{0,8},{4,12},{8,0},{12,4},{16,24},{20,28},{24,16},{28,20},{1,9},{5... | collective-permute-start | bytes 2064392 | tf_op jit(solution)/shard_map/ppermute | solution.py:419
  (49 other events, 688.1 us)
Sparse Core Ops, SparseCore 0:
  53.8 44.6 reduce-scatter.2
  100.9 43.1 reduce-scatter.4
  237.4 45.1 all-gather.4
  284.6 44.8 all-gather.6

commit v2 on v1

--- a/solution.py
+++ b/solution.py
@@ -42,48 +42,51 @@
 smem_spec = pl.BlockSpec(memory_space=pltpu.SMEM)
 
 
-def project_body(place_ref, *refs, row_inputs, parts, steps_each):
+def project_body(place_ref, *refs, row_inputs, weights, steps_each):
     x_refs = refs[:row_inputs]
-    w_refs = refs[row_inputs : row_inputs + parts]
-    out_ref, high_ref, low_ref = refs[row_inputs + parts :]
+    count = 1 + max(part for part, _ in weights)
+    w_refs = refs[row_inputs : row_inputs + len(weights)]
+    out_ref, pair_ref = refs[row_inputs + len(weights) :]
     step = pl.program_id(0)
+    columns = count * HEAD_DIM
 
     @pl.when(step == 0)
     def _():
-        for part in range(parts):
-            high, low = split(w_refs[part][...])
-            high_ref[:, part * HEAD_DIM : (part + 1) * HEAD_DIM] = high
-            low_ref[:, part * HEAD_DIM : (part + 1) * HEAD_DIM] = low
+        for (part, start), w_ref in zip(weights, w_refs):
+            high, low = split(w_ref[...].T)
+            stop = start + w_ref.shape[0]
+            pair_ref[part * HEAD_DIM : (part + 1) * HEAD_DIM, start:stop] = high
+            pair_ref[columns + part * HEAD_DIM : columns + (part + 1) * HEAD_DIM, start:stop] = low
 
     for source in range(row_inputs):
 
         @pl.when(step // steps_each == source)
         def _():
             x_high, x_low = split(x_refs[source][...])
-            total = dot(x_high, high_ref[...]) + dot(x_high, low_ref[...]) + dot(x_low, high_ref[...])
-            for part in range(parts):
-                out_ref[place_ref[part]] = total[:, part * HEAD_DIM : (part + 1) * HEAD_DIM]
-
-
-def project(place, xs, ws):
-    rows, depth = xs[0].shape
-    parts = len(ws)
+            both = dot(pair_ref[...], x_high)
+            total = both[:columns] + both[columns:] + dot(pair_ref[:columns], x_low)
+            for part in range(count):
+                out_ref[place_ref[part]] = total[part * HEAD_DIM : (part + 1) * HEAD_DIM]
+
+
+def project(place, xs, ws, weights):
+    depth, rows = xs[0].shape
+    parts = place.shape[0]
     block = 256
     steps_each = rows // block
-    steps = steps_each * len(xs)
 
     def x_map(source):
-        return lambda step: (jnp.clip(step - source * steps_each, 0, steps_each - 1), 0)
+        return lambda step: (0, jnp.clip(step - source * steps_each, 0, steps_each - 1))
 
     return pl.pallas_call(
-        functools.partial(project_body, row_inputs=len(xs), parts=parts, steps_each=steps_each),
-        grid=(steps,),
+        functools.partial(project_body, row_inputs=len(xs), weights=weights, steps_each=steps_each),
+        grid=(steps_each * len(xs),),
         in_specs=[smem_spec]
-        + [pl.BlockSpec((block, depth), x_map(source)) for source in range(len(xs))]
+        + [pl.BlockSpec((depth, block), x_map(source)) for source in range(len(xs))]
         + [whole_spec(w) for w in ws],
-        out_specs=pl.BlockSpec((parts, block, HEAD_DIM), lambda step: (0, step, 0)),
-        out_shape=jax.ShapeDtypeStruct((parts, rows * len(xs), HEAD_DIM), f32),
-        scratch_shapes=[pltpu.VMEM((depth, parts * HEAD_DIM), bf16)] * 2,
+        out_specs=pl.BlockSpec((parts, HEAD_DIM, block), lambda step: (0, 0, step)),
+        out_shape=jax.ShapeDtypeStruct((parts, HEAD_DIM, rows * len(xs)), f32),
+        scratch_shapes=[pltpu.VMEM((2 * parts * HEAD_DIM, depth), bf16)],
         compiler_params=pltpu.CompilerParams(vmem_limit_bytes=VMEM_LIMIT),
         cost_estimate=pl.CostEstimate(
             flops=6 * rows * len(xs) * depth * parts * HEAD_DIM, bytes_accessed=4 * rows * len(xs) * depth, transcendentals=0
@@ -91,41 +94,51 @@
     )(place, *xs, *ws)
 
 
-def weight_grad_body(place_ref, *refs, row_inputs, parts):
+def weight_grad_body(place_ref, *refs, row_inputs, parts, cut):
     x_refs = refs[:row_inputs]
     g_ref = refs[row_inputs]
-    out_refs = refs[row_inputs + 1 : row_inputs + 1 + parts]
-    high_ref, low_ref = refs[row_inputs + 1 + parts :]
-    rows = x_refs[0].shape[0]
-
-    @pl.when(pl.program_id(0) == 0)
+    out_refs = refs[row_inputs + 1 : -1]
+    pair_ref = refs[-1]
+    rows = x_refs[0].shape[1]
+    columns = parts * HEAD_DIM
+    step = pl.program_id(0)
+
+    @pl.when(step == 0)
     def _():
         for part in range(parts):
             high, low = split(g_ref[place_ref[part]])
-            high_ref[:, part * HEAD_DIM : (part + 1) * HEAD_DIM] = high
-            low_ref[:, part * HEAD_DIM : (part + 1) * HEAD_DIM] = low
-
-    total = jnp.zeros((x_refs[0].shape[1], parts * HEAD_DIM), f32)
+            pair_ref[:, part * HEAD_DIM : (part + 1) * HEAD_DIM] = high
+            pair_ref[:, columns + part * HEAD_DIM : columns + (part + 1) * HEAD_DIM] = low
+
+    total = jnp.zeros((x_refs[0].shape[0], columns), f32)
     for source in range(row_inputs):
         x_high, x_low = split(x_refs[source][...])
-        g_high = high_ref[source * rows : (source + 1) * rows]
-        g_low = low_ref[source * rows : (source + 1) * rows]
-        total += dot_first(x_high, g_high) + dot_first(x_high, g_low) + dot_first(x_low, g_high)
-    for part in range(parts):
+        pair = pair_ref[source * rows : (source + 1) * rows]
+        both = dot(x_high, pair)
+        total += both[:, :columns] + both[:, columns:] + dot(x_low, pair[:, :columns])
+    for part in range(parts - 1 if cut else parts):
         out_refs[part][...] = total[:, part * HEAD_DIM : (part + 1) * HEAD_DIM]
-
-
-def weight_grad(place, xs, grads):
-    rows, depth = xs[0].shape
+    if cut:
+        for piece in range(2):
+
+            @pl.when(step == piece)
+            def _():
+                out_refs[parts - 1 + piece][...] = total[:, (parts - 1) * HEAD_DIM :]
+
+
+def weight_grad(place, xs, grads, cut):
+    depth, rows = xs[0].shape
     parts = grads.shape[0]
-    block = 256
+    block = depth // 2
+    piece = jax.ShapeDtypeStruct((block, HEAD_DIM), f32)
+    full = parts - 1 if cut else parts
     return pl.pallas_call(
-        functools.partial(weight_grad_body, row_inputs=len(xs), parts=parts),
-        grid=(pl.cdiv(depth, block),),
-        in_specs=[smem_spec] + [pl.BlockSpec((rows, block), lambda step: (0, step))] * len(xs) + [whole_spec(grads)],
-        out_specs=[pl.BlockSpec((block, HEAD_DIM), lambda step: (step, 0))] * parts,
-        out_shape=[jax.ShapeDtypeStruct((depth, HEAD_DIM), f32)] * parts,
-        scratch_shapes=[pltpu.VMEM((rows * len(xs), parts * HEAD_DIM), bf16)] * 2,
+        functools.partial(weight_grad_body, row_inputs=len(xs), parts=parts, cut=cut),
+        grid=(2,),
+        in_specs=[smem_spec] + [pl.BlockSpec((block, rows), lambda step: (step, 0))] * len(xs) + [whole_spec(grads)],
+        out_specs=[pl.BlockSpec((block, HEAD_DIM), lambda step: (step, 0))] * full + [whole_spec(piece)] * (2 if cut else 0),
+        out_shape=[jax.ShapeDtypeStruct((depth, HEAD_DIM), f32)] * full + [piece] * (2 if cut else 0),
+        scratch_shapes=[pltpu.VMEM((rows * len(xs), 2 * parts * HEAD_DIM), bf16)],
         compiler_params=pltpu.CompilerParams(vmem_limit_bytes=VMEM_LIMIT),
         cost_estimate=pl.CostEstimate(
             flops=6 * rows * len(xs) * depth * parts * HEAD_DIM, bytes_accessed=4 * rows * len(xs) * depth, transcendentals=0
@@ -192,7 +205,7 @@
     for index, start, offset, count in layout:
         for piece in range(0, count, SPAN):
             target_ref[offset + piece : offset + piece + SPAN, :] = pair_cat(
-                source_refs[index][start + piece : start + piece + SPAN, :], 1
+                source_refs[index][:, start + piece : start + piece + SPAN].T, 1
             )
 
 
@@ -224,7 +237,7 @@
     lanes = group * SPAN
     q_refs, g_refs = refs[:nb], refs[nb : 2 * nb]
     key_refs = refs[2 * nb : 2 * nb + sources]
-    stats_ref = refs[2 * nb + sources]
+    prob_ref = refs[2 * nb + sources]
     out_refs = refs[2 * nb + sources + 1 : 2 * nb + sources + 1 + outs]
     keys_ref, sum_ref, score_ref, qt_ref, grad_ref, offset_ref, limit_ref = refs[2 * nb + sources + 1 + outs :]
     step = pl.program_id(0)
@@ -264,11 +277,11 @@
 
     total = lax.fori_loop(0, count, second, jnp.zeros((8, lanes), f32))
     inverse = 1.0 / jnp.sum(total, axis=0, keepdims=True)
-    stats_ref[0, 0:1, :] = largest
-    stats_ref[0, 1:2, :] = inverse
 
     def third(block, _):
-        high, low = split(score_ref[slot_rows(block), :] * inverse)
+        prob = score_ref[slot_rows(block), :] * inverse
+        prob_ref[0, slot_rows(block), :] = prob
+        high, low = split(prob)
         grads = grad_ref[...]
         both = dot(high, grads) + dot(low, grads)
         offset = offset_ref[block]
@@ -290,10 +303,10 @@
     at = 2 * nb
     key_refs, value_refs = refs[at : at + sources], refs[at + sources : at + 2 * sources]
     at += 2 * sources
-    stats_ref = refs[at]
+    prob_ref = refs[at]
     dq_ref = refs[at + 1]
     out_refs = refs[at + 2 : at + 2 + outs]
-    (keys_ref, values_ref, sum_ref, prob_ref, dprob_ref, qt_ref, gt_ref, q_ref, dqt_ref, offset_ref, limit_ref) = refs[at + 2 + outs :]
+    (keys_ref, values_ref, sum_ref, dprob_ref, gt_ref, q_ref, dqt_ref, offset_ref, limit_ref) = refs[at + 2 + outs :]
     step = pl.program_id(0)
     tok = tok_ref[0]
 
@@ -313,24 +326,16 @@
         def _():
             for head in range(group):
                 rows = load_rows(q_refs[source], half, head) * logit_scale
-                qt_ref[:, head * SPAN : (head + 1) * SPAN] = transposed_pair(rows)
                 q_ref[head * SPAN : (head + 1) * SPAN, :] = pair_cat(rows, 1)
                 gt_ref[:, head * SPAN : (head + 1) * SPAN] = transposed_pair(
                     load_rows(g_refs[source], half, head) * live_column(half, live)
                 )
 
-    largest = stats_ref[0, 0:1, :]
-    inverse = stats_ref[0, 1:2, :]
-
     def first(block, delta):
-        offset = offset_ref[block]
-        value = scores(keys_ref, offset, qt_ref[...], key_limits(block, limit_ref, own_count, half, live, lanes))
-        prob = jnp.exp(value - largest) * inverse
-        values = block_rows(values_ref, offset)
+        values = block_rows(values_ref, offset_ref[block])
         dprob = dot(jnp.concatenate([values, values], axis=1), gt_ref[...])
-        prob_ref[slot_rows(block), :] = prob
         dprob_ref[slot_rows(block), :] = dprob
-        return delta + fold(prob * dprob, jnp.sum)
+        return delta + fold(prob_ref[0, slot_rows(block), :] * dprob, jnp.sum)
 
     delta = lax.fori_loop(0, count, first, jnp.zeros((8, lanes), f32))
     delta = jnp.sum(delta, axis=0, keepdims=True)
@@ -338,7 +343,7 @@
 
     def second(block, _):
         offset = offset_ref[block]
-        high, low = split(prob_ref[slot_rows(block), :] * (dprob_ref[slot_rows(block), :] - delta))
+        high, low = split(prob_ref[0, slot_rows(block), :] * (dprob_ref[slot_rows(block), :] - delta))
         rows = q_ref[...]
         both = dot(high, rows) + dot(low, rows)
         sum_ref[slot_rows(offset // SPAN), :] += both[:, :HEAD_DIM] + both[:, HEAD_DIM:]
@@ -363,10 +368,10 @@
     steps = nb * halves
     conf = dict(nb=nb, group=group, rows=rows, owners=owners, layout=layout, paired=paired, sources=1 + len(part_rows), outs=len(part_rows) + 1)
     table_rows = owners * SPAN + nb * rows
-    slots = (owners + halves) * SPAN
+    slots = (owners - 1 + halves) * SPAN
     sums = [jax.ShapeDtypeStruct((count, HEAD_DIM), f32) for count in part_rows] + [jax.ShapeDtypeStruct((nb * rows, HEAD_DIM), f32)]
-    stats = jax.ShapeDtypeStruct((steps, 8, lanes), f32)
-    stats_spec = pl.BlockSpec((1, 8, lanes), lambda step: (step, 0, 0))
+    probs = jax.ShapeDtypeStruct((steps, slots, lanes), f32)
+    probs_spec = pl.BlockSpec((1, slots, lanes), lambda step: (step, 0, 0))
     table = pltpu.VMEM((table_rows, 2 * HEAD_DIM), bf16)
     table_sum = pltpu.VMEM((table_rows, HEAD_DIM), f32)
     square = pltpu.VMEM((slots, lanes), f32)
@@ -380,19 +385,19 @@
             functools.partial(soft_body, conf=conf),
             grid=(steps,),
             in_specs=[smem_spec] * 3 + [whole_spec(a) for a in (*qs, *gs, *keys)],
-            out_specs=[stats_spec] + [whole_spec(a) for a in sums],
-            out_shape=[stats] + sums,
+            out_specs=[probs_spec] + [whole_spec(a) for a in sums],
+            out_shape=[probs] + sums,
             scratch_shapes=[table, table_sum, square, columns, pltpu.VMEM((lanes, 2 * HEAD_DIM), bf16)] + lists,
             compiler_params=params,
             cost_estimate=pl.CostEstimate(flops=2 * work, bytes_accessed=4 * rows * width, transcendentals=0),
         )(*scalars, *qs, *gs, *keys)
 
-    def grad(keys, values, stats_in):
+    def grad(keys, values, probs_in):
         dq = jax.ShapeDtypeStruct((nb * rows, width), f32)
         return pl.pallas_call(
             functools.partial(grad_body, conf=conf),
             grid=(steps,),
-            in_specs=[smem_spec] * 3 + [whole_spec(a) for a in (*qs, *gs, *keys, *values)] + [stats_spec],
+            in_specs=[smem_spec] * 3 + [whole_spec(a) for a in (*qs, *gs, *keys, *values)] + [probs_spec],
             out_specs=[pl.BlockSpec((SPAN, width), lambda step: (step, 0))] + [whole_spec(a) for a in sums],
             out_shape=[dq] + sums,
             scratch_shapes=[
@@ -400,8 +405,6 @@
                 table,
                 table_sum,
                 square,
-                square,
-                columns,
                 columns,
                 pltpu.VMEM((lanes, 2 * HEAD_DIM), bf16),
                 pltpu.VMEM((2 * HEAD_DIM, lanes), f32),
@@ -409,7 +412,7 @@
             + lists,
             compiler_params=params,
             cost_estimate=pl.CostEstimate(flops=4 * work, bytes_accessed=4 * rows * width, transcendentals=0),
-        )(*scalars, *qs, *gs, *keys, *values, stats_in)
+        )(*scalars, *qs, *gs, *keys, *values, probs_in)
 
     return soft, grad
 
@@ -419,15 +422,20 @@
     return lax.ppermute(array, "tok", [(index, index ^ mask) for index in range(count)])
 
 
-def gather_square(array, cut):
-    across = flip(array, 2)
-    down = flip(array, 4)
-    return across, down, flip(across[:cut], 4), flip(down[cut:], 2)
-
-
-def scatter_square(across, down, corner_head, corner_tail, cut):
-    from_across = flip(corner_head, 2)
-    from_down = flip(corner_tail, 4)
+def together(*arrays):
+    return lax.optimization_barrier(arrays)
+
+
+def gather_square(array, cut, axis):
+    across, down = flip(array, 2), flip(array, 4)
+    head = lax.slice_in_dim(across, 0, cut, axis=axis)
+    tail = lax.slice_in_dim(down, cut, down.shape[axis], axis=axis)
+    return across, down, flip(head, 4), flip(tail, 2)
+
+
+def scatter_square(across, down, head, tail):
+    cut = head.shape[0]
+    from_across, from_down = flip(head, 2), flip(tail, 4)
     down = down.at[:cut].add(from_across)
     across = across.at[cut:].add(from_down)
     return flip(across, 2), flip(down, 4)
@@ -437,16 +445,13 @@
     owners = lax.axis_size("tok")
     depth = lax.axis_size("head")
     tok = lax.axis_index("tok").astype(jnp.int32)
-    core = tok % 2
+    core = tok & 1
     rows = hidden.shape[0]
     width = queries.shape[1] // 2
     scalars = (tok.reshape(1), fork_tile, live_len)
-    place = (tok // 2) ^ jnp.arange(depth, dtype=jnp.int32)
-    half_depth = w_key.shape[0] // 2
-
-    def gather_weight(w):
-        across, down, head, tail = gather_square(w, half_depth)
-        return [w, across, down, jnp.concatenate([head, tail], axis=0)]
+    place = (tok >> 1) ^ jnp.arange(depth, dtype=jnp.int32)
+    cut = w_key.shape[0] // (2 * HEAD_DIM) * HEAD_DIM
+    weights = ((0, 0), (1, 0), (2, 0), (3, 0), (3, cut))
 
     def mine(array):
         return lax.dynamic_slice_in_dim(array, core * width, width, 1)
@@ -454,14 +459,35 @@
     def partners(array):
         return flip(lax.dynamic_slice_in_dim(array, (1 - core) * width, width, 1), 1)
 
+    def sum_heads(partial):
+        return lax.psum_scatter(partial, "head", scatter_dimension=0, tiled=True)[0]
+
+    def all_heads(grads):
+        return lax.all_gather(grads, "head", axis=0, tiled=False)
+
+    def lead(array):
+        return jnp.concatenate([array[:, :SPAN], array[:, rows : rows + SPAN]], axis=1)
+
+    def returned(own, across, down, head, tail):
+        first, second = scatter_square(across, down, head, tail)
+        both = first + second
+        return own.at[:SPAN].add(both[:SPAN]).at[rows : rows + SPAN].add(both[SPAN:])
+
+    def weight(every):
+        own, *others = weight_grad(place, xs, every, True)
+        first, second = scatter_square(*others)
+        return own + first + second
+
+    def home(array):
+        kept, received = array[:rows], flip(array[rows:], 1)
+        return jnp.where(core == 0, jnp.concatenate([kept, received], axis=1), jnp.concatenate([received, kept], axis=1))
+
+    hidden = hidden.T
     xs = [hidden, flip(hidden, 1)]
     qs = [mine(queries), partners(queries)]
     gs = [mine(out_grad), partners(out_grad)]
-    keys = lax.psum_scatter(project(place, xs, gather_weight(w_key)), "head", scatter_dimension=0, tiled=True)[0]
-    values = lax.psum_scatter(project(place, xs, gather_weight(w_value)), "head", scatter_dimension=0, tiled=True)[0]
-
-    def lead(array):
-        return jnp.concatenate([array[:SPAN], array[rows : rows + SPAN]], axis=0)
+    keys = sum_heads(project(place, xs, [w_key, *gather_square(w_key, cut, 0)], weights))
+    values = sum_heads(project(place, xs, [w_value, *gather_square(w_value, cut, 0)], weights))
 
     base = owners * SPAN
     layout = (
@@ -475,30 +501,22 @@
     )
     soft, grad = attention_calls(scalars, qs, gs, layout, True, owners, (2 * SPAN, 2 * SPAN, SPAN, SPAN))
 
-    def returned(own, across, down, head, tail):
-        first, second = scatter_square(across, down, head, tail, SPAN)
-        both = first + second
-        return own.at[:SPAN].add(both[:SPAN]).at[rows : rows + SPAN].add(both[SPAN:])
-
-    def weight(grads):
-        every = lax.all_gather(grads, "head", axis=0, tiled=False)
-        own, across, down, corner = weight_grad(place, xs, every)
-        first, second = scatter_square(across, down, corner[:half_depth], corner[half_depth:], half_depth)
-        return own + first + second
-
-    def home(array):
-        kept, received = array[:rows], flip(array[rows:], 1)
-        return jnp.where(core == 0, jnp.concatenate([kept, received], axis=1), jnp.concatenate([received, kept], axis=1))
-
-    key_parts = [keys, *gather_square(lead(keys), SPAN)]
-    stats, *value_sums = soft(key_parts)
+    key_parts = [keys, *gather_square(lead(keys), SPAN, 1)]
+    probs, *value_sums = soft(key_parts)
+    values, probs = together(values, probs)
+    value_parts = [values, *gather_square(lead(values), SPAN, 1)]
     value_grads = returned(value_sums[-1], *value_sums[:-1])
-    grad_w_value = weight(value_grads)
-    value_parts = [values, *gather_square(lead(values), SPAN)]
-    grad_query, *key_sums = grad(key_parts, value_parts, stats)
+    every_value = all_heads(value_grads)
+    probs, value_grads = together(probs, value_grads)
+    grad_query, *key_sums = grad(key_parts, value_parts, probs)
     key_grads = returned(key_sums[-1], *key_sums[:-1])
-    grad_w_key = weight(key_grads)
-    return home(grad_query), home(key_grads), home(value_grads), grad_w_key, grad_w_value
+    every_key = all_heads(key_grads)
+    every_value, key_grads = together(every_value, key_grads)
+    grad_w_value = weight(every_value)
+    grad_query, grad_key, grad_value = home(grad_query), home(key_grads), home(value_grads)
+    every_key, grad_w_value, grad_query, grad_key, grad_value = together(every_key, grad_w_value, grad_query, grad_key, grad_value)
+    grad_w_key = weight(every_key)
+    return grad_query, grad_key, grad_value, grad_w_key, grad_w_value
 
 
 def shards_single(hidden, queries, out_grad, w_key, w_value, fork_tile, live_len):
@@ -507,31 +525,33 @@
     tok = lax.axis_index("tok").astype(jnp.int32)
     scalars = (tok.reshape(1), fork_tile, live_len)
     place = jnp.arange(depth, dtype=jnp.int32)
+    hidden = hidden.T
 
     def projected(w):
         every = lax.all_gather(w, "tok", axis=1, tiled=True)
         pieces = [every[:, index * HEAD_DIM : (index + 1) * HEAD_DIM] for index in range(depth)]
-        return lax.psum_scatter(project(place, [hidden], pieces), "head", scatter_dimension=0, tiled=True)[0]
+        partial = project(place, [hidden], pieces, tuple((index, 0) for index in range(depth)))
+        return lax.psum_scatter(partial, "head", scatter_dimension=0, tiled=True)[0]
 
     keys, values = projected(w_key), projected(w_value)
-    layout = ((0, 0, owners * SPAN, hidden.shape[0]), (1, 0, 0, owners * SPAN))
+    layout = ((0, 0, owners * SPAN, hidden.shape[1]), (1, 0, 0, owners * SPAN))
     soft, grad = attention_calls(scalars, [queries], [out_grad], layout, False, owners, (owners * SPAN,))
 
     def parts(array):
-        return [array, lax.all_gather(array[:SPAN], "tok", axis=0, tiled=True)]
+        return [array, lax.all_gather(array[:, :SPAN], "tok", axis=1, tiled=True)]
 
     def returned(remote, own):
         return own.at[:SPAN].add(lax.psum_scatter(remote, "tok", scatter_dimension=0, tiled=True))
 
     def weight(grads):
         every = lax.all_gather(grads, "head", axis=0, tiled=False)
-        columns = jnp.concatenate(weight_grad(place, [hidden], every), axis=1)
+        columns = jnp.concatenate(weight_grad(place, [hidden], every, False), axis=1)
         return lax.psum_scatter(columns, "tok", scatter_dimension=1, tiled=True)
 
     key_parts = parts(keys)
-    stats, *value_sums = soft(key_parts)
+    probs, *value_sums = soft(key_parts)
     value_grads = returned(*value_sums)
-    grad_query, *key_sums = grad(key_parts, parts(values), stats)
+    grad_query, *key_sums = grad(key_parts, parts(values), probs)
     key_grads = returned(*key_sums)
     return grad_query, key_grads, value_grads, weight(key_grads), weight(value_grads)
 

time: 393 us -> 309 us (0.79)
  waiting for transfers between devices: 198 us -> 119 us
  other arithmetic: 14.8 us -> 26 us
  starting transfers between devices: 80.1 us -> 70 us
  local copies, waits for them, and re-layouts: 18.1 us -> 10.6 us
    all_gather x2, waiting for transfers between devices: 59.1 us -> 9.67 us  [all_heads(): return lax.all_gather(grads, 'head', axis=0, tiled=False)]
    reduce_scatter x2, waiting for transfers between devices: 46.7 us -> 3.46 us  [sum_heads(): return lax.psum_scatter(partial, 'head', scatter_dimension=0, tiled=True)[0]]
    ppermute x38, waiting for transfers between devices: 91.6 us -> 106 us  [flip(): lax.ppermute(array, 'tok', [(index, index ^ mask) for index in range(coun...]
    ppermute x38, starting transfers between devices: 79.8 us -> 69.7 us  [flip(): lax.ppermute(array, 'tok', [(index, index ^ mask) for index in range(coun...]
    scatter-add x4, other arithmetic: 1.76 us -> 6.67 us  [scatter_square(): across = across.at[cut:].add(from_down)]
    scatter-add x4, other arithmetic: 1.74 us -> 6.65 us  [scatter_square(): down = down.at[:cut].add(from_across)]
  transfers between devices with their start and end apart: 42 -> 42, of which waited for: 26 -> 25; matrix products, arithmetic and copies ran while one was open for 6% -> 10% of each run, Pallas kernels for 10% -> 15%
where the time goes in v2:
time: 309 us; the launch traced here: 305 us
  waiting for transfers between devices  119 us (39%)
  starting transfers between devices  70 us (23%)
  Pallas kernels  65.4 us (21%)
  other arithmetic  26 us (8%)
  between operations  14.1 us (5%)
  local copies, waits for them, and re-layouts  10.6 us (3%)
    ppermute x38, waiting for transfers between devices, flip(): lax.ppermute(array, 'tok', [(index, index ^ mask) for index in range(coun...  106 us
    ppermute x38, starting transfers between devices, flip(): lax.ppermute(array, 'tok', [(index, index ^ mask) for index in range(coun...  69.7 us
    pallas_call x2, Pallas kernels, project(): pl.pallas_call(functools.partial(project_body, row_inputs=len(xs), weight...  20 us
    pallas_call x2, Pallas kernels, weight_grad(): pl.pallas_call(functools.partial(weight_grad_body, row_inputs=len(xs), pa...  18 us
    pallas_call x1, Pallas kernels, grad(): pl.pallas_call(functools.partial(grad_body, conf=conf), grid=(steps,), in...  14.7 us
    pallas_call x1, Pallas kernels, soft(): pl.pallas_call(functools.partial(soft_body, conf=conf), grid=(steps,), in...  12.7 us
    all_gather x2, waiting for transfers between devices, all_heads(): return lax.all_gather(grads, 'head', axis=0, tiled=False)  9.67 us
    scatter-add x4, other arithmetic, scatter_square(): across = across.at[cut:].add(from_down)  6.67 us
  transfers between devices with their start and end apart: 42, of which 25 were waited for; matrix products, arithmetic and copies ran while one was open for 10% of the time, Pallas kernels for 15%

profile of v2, /device:TPU:0, one launch (start us, length us, event | category | flops | bytes accessed | tf_op | source)
XLA Modules:
  0.0 305.2 jit_solution(5920923070184399663)
XLA Ops:
  11.8 14.7 %collective-permute-done.4.refs_4_ = f32[1344,128]{1,0:T(8,128)S(1)} collective-permute-done((f32[1344,128]{1,0:T(8,128)}, f32[1344,128]{1,0:T(8,128)S(1)}, u32[]{:S(2)}, u32[]{:S(2)}) %collective-permute-start.4) | collective-permute-done | bytes 688160 | tf_op jit(solution)/shard_map/ppermute | solution.py:422
  30.5 7.0 %collective-permute-done.5.refs_5_ = f32[640,128]{1,0:T(8,128)S(1)} collective-permute-done((f32[640,128]{1,0:T(8,128)S(1)}, f32[640,128]{1,0:T(8,128)S(1)}, u32[]{:S(2)}, u32[]{:S(2)}) %collective-permute-start.5) | collective-permute-done | bytes 327712 | tf_op jit(solution)/shard_map/ppermute | solution.py:422
  38.3 10.0 %shard_map.110 = f32[4,128,1024]{2,1,0:T(8,128)} custom-call(s32[4]{0:T(128)} %iota_xor_fusion.place_ref, f32[1344,512]{1,0:T(8,128)} %bitcast.12, f32[1344,512]{1,0:T(8,128)} %collective-permute-done.2.refs_1_, f32[1344,128]{1,0:T(8,128)} %refs_2_.2, f32[1344,128]{1,0:T(8,128)} %copy-done.9, f32[1344,128]{1,0:T(8,128)} %copy-done.7, f32[640,128]{1,0:T(8,128)} %copy-done.20, ...), custom_call_target="tpu_custom_call" | custom-call | flops 4227858432 | bytes 5505024 | tf_op jit(solution)/shard_map/pallas_call | solution.py:81
  51.7 13.5 %collective-permute-done.12.refs_4_ = f32[1344,128]{1,0:T(8,128)S(1)} collective-permute-done((f32[1344,128]{1,0:T(8,128)S(1)}, f32[1344,128]{1,0:T(8,128)S(1)}, u32[]{:S(2)}, u32[]{:S(2)}) %collective-permute-start.12) | collective-permute-done | bytes 688160 | tf_op jit(solution)/shard_map/ppermute | solution.py:422
  68.0 6.5 %collective-permute-done.13.refs_5_ = f32[640,128]{1,0:T(8,128)S(1)} collective-permute-done((f32[640,128]{1,0:T(8,128)S(1)}, f32[640,128]{1,0:T(8,128)S(1)}, u32[]{:S(2)}, u32[]{:S(2)}) %collective-permute-start.13) | collective-permute-done | bytes 327712 | tf_op jit(solution)/shard_map/ppermute | solution.py:422
  75.9 10.0 %shard_map.111 = f32[4,128,1024]{2,1,0:T(8,128)} custom-call(s32[4]{0:T(128)} %iota_xor_fusion.place_ref, f32[1344,512]{1,0:T(8,128)} %bitcast.13, f32[1344,512]{1,0:T(8,128)} %collective-permute-done.2.refs_1_, f32[1344,128]{1,0:T(8,128)} %refs_2_.3, f32[1344,128]{1,0:T(8,128)} %copy-done.10, f32[1344,128]{1,0:T(8,128)} %copy-done.8, ...), custom_call_target="tpu_custom_call" | custom-call | flops 4227858432 | bytes 5505024 | tf_op jit(solution)/shard_map/pallas_call | solution.py:81
  89.5 3.4 %reduce-scatter.3.cloned.1.call-done = f32[1,128,1024]{2,1,0:T(8,128)} async-done(((f32[4,128,1024]{2,1,0:T(8,128)}), f32[1,128,1024]{2,1,0:T(8,128)}) %reduce-scatter.3.cloned.1.call-update) | async-done | bytes 524304 | tf_op jit(solution)/shard_map/reduce_scatter | solution.py:463
  96.9 4.9 %collective-permute-done.8.refs_6_ = f32[128,512]{1,0:T(8,128)S(1)} collective-permute-done((f32[128,512]{1,0:T(8,128)S(1)}, f32[128,512]{1,0:T(8,128)S(1)}, u32[]{:S(2)}, u32[]{:S(2)}) %collective-permute-start.8) | collective-permute-done | bytes 262176 | tf_op jit(solution)/shard_map/ppermute | solution.py:422
  109.1 12.7 %shard_map.112 = (f32[4,2304,512]{2,1,0:T(8,128)}, f32[512,128]{1,0:T(8,128)}, f32[512,128]{1,0:T(8,128)}, f32[256,128]{1,0:T(8,128)}, f32[256,128]{1,0:T(8,128)}, /*index=5*/f32[1024,128]{1,0:T(8,128)}) custom-call(s32[1]{0:T(128)} %bitcast.tok_ref, s32[7]{0:T(128)} %fork_ref.3, s32[8]{0:T(128)} %live_ref.3, f32[512,256]{1,0:T(8,128)} %get-tuple-element.220.refs_0_, ...), custom_call_target="tpu_custom_call" | custom-call | flops 3221225472 | bytes 524288 | tf_op jit(solution)/shard_map/pallas_call | solution.py:384
  121.8 3.6 %collective-permute-start.21 = (f32[256,128]{1,0:T(8,128)}, f32[256,128]{1,0:T(8,128)S(1)}, u32[]{:S(2)}, u32[]{:S(2)}) collective-permute-start(f32[256,128]{1,0:T(8,128)} %get-tuple-element.189), channel_id=1, source_target_pairs={{0,8},{4,12},{8,0},{12,4},{16,24},{20,28},{24,16},{28,20},{1,9},{5... | collective-permute-start | bytes 393224 | tf_op jit(solution)/shard_map/ppermute | solution.py:422
  125.4 9.2 %collective-permute-start.19 = (f32[256,128]{1,0:T(8,128)}, f32[256,128]{1,0:T(8,128)S(1)}, u32[]{:S(2)}, u32[]{:S(2)}) collective-permute-start(f32[256,128]{1,0:T(8,128)} %get-tuple-element.187), channel_id=1, source_target_pairs={{0,16},{4,20},{8,24},{12,28},{16,0},{20,4},{24,8},{28,12},{1,17},{... | collective-permute-start | bytes 393224 | tf_op jit(solution)/shard_map/ppermute | solution.py:422
  143.8 3.6 %collective-permute-done.20 = f32[512,128]{1,0:T(8,128)S(1)} collective-permute-done((f32[512,128]{1,0:T(8,128)}, f32[512,128]{1,0:T(8,128)S(1)}, u32[]{:S(2)}, u32[]{:S(2)}) %collective-permute-start.20) | collective-permute-done | bytes 262176 | tf_op jit(solution)/shard_map/ppermute | solution.py:422
  154.1 4.9 %collective-permute-done.16.refs_11_ = f32[128,512]{1,0:T(8,128)S(1)} collective-permute-done((f32[128,512]{1,0:T(8,128)S(1)}, f32[128,512]{1,0:T(8,128)S(1)}, u32[]{:S(2)}, u32[]{:S(2)}) %collective-permute-start.16) | collective-permute-done | bytes 262176 | tf_op jit(solution)/shard_map/ppermute | solution.py:422
  167.6 14.7 %shard_map.113 = (f32[1024,256]{1,0:T(8,128)}, f32[512,128]{1,0:T(8,128)}, f32[512,128]{1,0:T(8,128)}, f32[256,128]{1,0:T(8,128)}, f32[256,128]{1,0:T(8,128)}, /*index=5*/f32[1024,128]{1,0:T(8,128)}) custom-call(s32[1]{0:T(128)} %bitcast.tok_ref, s32[7]{0:T(128)} %fork_ref.3, s32[8]{0:T(128)} %live_ref.3, f32[512,256]{1,0:T(8,128)} %get-tuple-element.220.refs_0_, ...), custom_call_target="tpu_custom_call" | custom-call | flops 6442450944 | bytes 524288 | tf_op jit(solution)/shard_map/pallas_call | solution.py:397
  182.3 3.4 %collective-permute-start.25 = (f32[256,128]{1,0:T(8,128)}, f32[256,128]{1,0:T(8,128)S(1)}, u32[]{:S(2)}, u32[]{:S(2)}) collective-permute-start(f32[256,128]{1,0:T(8,128)} %get-tuple-element.195), channel_id=1, source_target_pairs={{0,8},{4,12},{8,0},{12,4},{16,24},{20,28},{24,16},{28,20},{1,9},{5... | collective-permute-start | bytes 393224 | tf_op jit(solution)/shard_map/ppermute | solution.py:422
  185.7 9.2 %collective-permute-start.23 = (f32[256,128]{1,0:T(8,128)}, f32[256,128]{1,0:T(8,128)S(1)}, u32[]{:S(2)}, u32[]{:S(2)}) collective-permute-start(f32[256,128]{1,0:T(8,128)} %get-tuple-element.193), channel_id=1, source_target_pairs={{0,16},{4,20},{8,24},{12,28},{16,0},{20,4},{24,8},{28,12},{1,17},{... | collective-permute-start | bytes 393224 | tf_op jit(solution)/shard_map/ppermute | solution.py:422
  204.2 3.9 %collective-permute-done.24 = f32[512,128]{1,0:T(8,128)S(1)} collective-permute-done((f32[512,128]{1,0:T(8,128)}, f32[512,128]{1,0:T(8,128)S(1)}, u32[]{:S(2)}, u32[]{:S(2)}) %collective-permute-start.24) | collective-permute-done | bytes 262176 | tf_op jit(solution)/shard_map/ppermute | solution.py:422
  211.4 9.1 %shard_map.114 = (f32[1344,128]{1,0:T(8,128)}, f32[1344,128]{1,0:T(8,128)}, f32[1344,128]{1,0:T(8,128)}, f32[672,128]{1,0:T(8,128)}, f32[672,128]{1,0:T(8,128)}) custom-call(s32[4]{0:T(128)} %iota_xor_fusion.place_ref, f32[1344,512]{1,0:T(8,128)} %bitcast.14, f32[1344,512]{1,0:T(8,128)} %collective-permute-done.2.refs_1_, f32[4,1024,128]{2,1,0:T(8,128)} %bitcast.16), custom_call_target="tpu_custom_call" | custom-call | flops 4227858432 | bytes 5505024 | tf_op jit(solution)/shard_map/pallas_call | solution.py:135
  223.5 4.6 %collective-permute-done.29 = f32[672,128]{1,0:T(8,128)S(1)} collective-permute-done((f32[672,128]{1,0:T(8,128)}, f32[672,128]{1,0:T(8,128)S(1)}, u32[]{:S(2)}, u32[]{:S(2)}) %collective-permute-start.29) | collective-permute-done | bytes 344096 | tf_op jit(solution)/shard_map/ppermute | solution.py:422
  239.3 5.5 %collective-permute-done.30 = f32[1344,128]{1,0:T(8,128)S(1)} collective-permute-done((f32[1344,128]{1,0:T(8,128)}, f32[1344,128]{1,0:T(8,128)S(1)}, u32[]{:S(2)}, u32[]{:S(2)}) %collective-permute-start.30) | collective-permute-done | bytes 688160 | tf_op jit(solution)/shard_map/ppermute | solution.py:422
  247.8 9.6 %all-gather.5.cloned.1.call-done = f32[4096,128]{1,0:T(8,128)} async-done(((f32[1024,128]{1,0:T(8,128)}), f32[4096,128]{1,0:T(8,128)}) %all-gather.5.cloned.1.call-update) | async-done | bytes 2097168 | tf_op jit(solution)/shard_map/all_gather | solution.py:466
  257.4 9.0 %shard_map.115 = (f32[1344,128]{1,0:T(8,128)}, f32[1344,128]{1,0:T(8,128)}, f32[1344,128]{1,0:T(8,128)}, f32[672,128]{1,0:T(8,128)}, f32[672,128]{1,0:T(8,128)}) custom-call(s32[4]{0:T(128)} %iota_xor_fusion.place_ref, f32[1344,512]{1,0:T(8,128)} %bitcast.15, f32[1344,512]{1,0:T(8,128)} %collective-permute-done.2.refs_1_, f32[4,1024,128]{2,1,0:T(8,128)} %bitcast.17), custom_call_target="tpu_custom_call" | custom-call | flops 4227858432 | bytes 5505024 | tf_op jit(solution)/shard_map/pallas_call | solution.py:135
  269.4 7.1 %collective-permute-done.36 = f32[672,128]{1,0:T(8,128)S(1)} collective-permute-done((f32[672,128]{1,0:T(8,128)}, f32[672,128]{1,0:T(8,128)S(1)}, u32[]{:S(2)}, u32[]{:S(2)}) %collective-permute-start.36) | collective-permute-done | bytes 344096 | tf_op jit(solution)/shard_map/ppermute | solution.py:422
  282.9 11.8 %collective-permute-done.37 = f32[1344,128]{1,0:T(8,128)S(1)} collective-permute-done((f32[1344,128]{1,0:T(8,128)}, f32[1344,128]{1,0:T(8,128)S(1)}, u32[]{:S(2)}, u32[]{:S(2)}) %collective-permute-start.37) | collective-permute-done | bytes 688160 | tf_op jit(solution)/shard_map/ppermute | solution.py:422
  (159 shorter events, 99.1 us)
Async XLA Ops:
  7.2 85.7 %reduce-scatter.3.cloned.1.call-start = ((), (), s32[]{:S(2)}) async-start(), calls=%async_computation.2 | async-start | bytes 2621440 | tf_op jit(solution)/shard_map/reduce_scatter | solution.py:463
  7.2 30.3 %collective-permute-start.2 = (f32[1344,512]{1,0:T(8,128)}, f32[1344,512]{1,0:T(8,128)}, u32[]{:S(2)}, u32[]{:S(2)}) collective-permute-start(f32[1344,512]{1,0:T(8,128)} %bitcast.11), channel_id=1, source_target_pairs={{0,4},{4,0},{8,12},{12,8},{16,20},{20,16},{24,28},{28,24},{1,5},{5... | collective-permute-start | bytes 8257544 | tf_op jit(solution)/shard_map/ppermute | solution.py:422
  7.7 18.8 %collective-permute-start.4 = (f32[1344,128]{1,0:T(8,128)}, f32[1344,128]{1,0:T(8,128)S(1)}, u32[]{:S(2)}, u32[]{:S(2)}) collective-permute-start(f32[1344,128]{1,0:T(8,128)} %refs_2_.2), channel_id=1, source_target_pairs={{0,16},{4,20},{8,24},{12,28},{16,0},{20,4},{24,8},{28,12},{1,17},{... | collective-permute-start | bytes 2064392 | tf_op jit(solution)/shard_map/ppermute | solution.py:422
  10.3 18.1 %collective-permute-start.3 = (f32[1344,128]{1,0:T(8,128)}, f32[1344,128]{1,0:T(8,128)S(1)}, u32[]{:S(2)}, u32[]{:S(2)}) collective-permute-start(f32[1344,128]{1,0:T(8,128)} %refs_2_.2), channel_id=1, source_target_pairs={{0,8},{4,12},{8,0},{12,4},{16,24},{20,28},{24,16},{28,20},{1,9},{5... | collective-permute-start | bytes 2064392 | tf_op jit(solution)/shard_map/ppermute | solution.py:422
  26.6 10.9 %collective-permute-start.6 = (f32[704,128]{1,0:T(8,128)S(1)}, f32[704,128]{1,0:T(8,128)S(1)}, u32[]{:S(2)}, u32[]{:S(2)}) collective-permute-start(f32[704,128]{1,0:T(8,128)S(1)} %slice.329), channel_id=1, source_target_pairs={{0,8},{4,12},{8,0},{12,4},{16,24},{20,28},{24,16},{28,20},{1,9},{5... | collective-permute-start | bytes 1081352 | tf_op jit(solution)/shard_map/ppermute | solution.py:422
  48.3 102.6 %reduce-scatter.5.cloned.1.call-start = ((), (), s32[]{:S(2)}) async-start(), calls=%async_computation.3 | async-start | bytes 2621440 | tf_op jit(solution)/shard_map/reduce_scatter | solution.py:463
  49.4 15.8 %collective-permute-start.12 = (f32[1344,128]{1,0:T(8,128)S(1)}, f32[1344,128]{1,0:T(8,128)S(1)}, u32[]{:S(2)}, u32[]{:S(2)}) collective-permute-start(f32[1344,128]{1,0:T(8,128)S(1)} %copy-done.15), channel_id=1, source_target_pairs={{0,16},{4,20},{8,24},{12,28},{16,0},{20,4},{24,8},{28,12},{1,17},{... | collective-permute-start | bytes 2064392 | tf_op jit(solution)/shard_map/ppermute | solution.py:422
  50.9 16.4 %collective-permute-start.11 = (f32[1344,128]{1,0:T(8,128)S(1)}, f32[1344,128]{1,0:T(8,128)S(1)}, u32[]{:S(2)}, u32[]{:S(2)}) collective-permute-start(f32[1344,128]{1,0:T(8,128)S(1)} %copy-done.15), channel_id=1, source_target_pairs={{0,8},{4,12},{8,0},{12,4},{16,24},{20,28},{24,16},{28,20},{1,9},{5... | collective-permute-start | bytes 2064392 | tf_op jit(solution)/shard_map/ppermute | solution.py:422
  65.2 9.2 %collective-permute-start.14 = (f32[704,128]{1,0:T(8,128)S(1)}, f32[704,128]{1,0:T(8,128)S(1)}, u32[]{:S(2)}, u32[]{:S(2)}) collective-permute-start(f32[704,128]{1,0:T(8,128)S(1)} %slice.335), channel_id=1, source_target_pairs={{0,8},{4,12},{8,0},{12,4},{16,24},{20,28},{24,16},{28,20},{1,9},{5... | collective-permute-start | bytes 1081352 | tf_op jit(solution)/shard_map/ppermute | solution.py:422
  86.0 125.4 %all-gather.7.cloned.1.call-start = ((), (), s32[]{:S(2)}) async-start(), calls=%async_computation.5 | async-start | bytes 2621440 | tf_op jit(solution)/shard_map/all_gather | solution.py:466
  88.1 16.9 %collective-permute-start = (f32[512,256]{1,0:T(8,128)S(1)}, f32[512,256]{1,0:T(8,128)S(1)}, u32[]{:S(2)}, u32[]{:S(2)}) collective-permute-start(f32[512,256]{1,0:T(8,128)S(1)} %get-tuple-element.219), channel_id=1, source_target_pairs={{0,4},{4,0},{8,12},{12,8},{16,20},{20,16},{24,28},{28,24},{1,5},{5... | collective-permute-start | bytes 1572872 | tf_op jit(solution)/shard_map/ppermute | solution.py:422
  89.0 16.0 %collective-permute-start.1 = (f32[512,256]{1,0:T(8,128)S(1)}, f32[512,256]{1,0:T(8,128)S(1)}, u32[]{:S(2)}, u32[]{:S(2)}) collective-permute-start(f32[512,256]{1,0:T(8,128)S(1)} %get-tuple-element.217), channel_id=1, source_target_pairs={{0,4},{4,0},{8,12},{12,8},{16,20},{20,16},{24,28},{28,24},{1,5},{5... | collective-permute-start | bytes 1572872 | tf_op jit(solution)/shard_map/ppermute | solution.py:422
  121.8 12.8 %collective-permute-start.21 = (f32[256,128]{1,0:T(8,128)}, f32[256,128]{1,0:T(8,128)S(1)}, u32[]{:S(2)}, u32[]{:S(2)}) collective-permute-start(f32[256,128]{1,0:T(8,128)} %get-tuple-element.189), channel_id=1, source_target_pairs={{0,8},{4,12},{8,0},{12,4},{16,24},{20,28},{24,16},{28,20},{1,9},{5... | collective-permute-start | bytes 393224 | tf_op jit(solution)/shard_map/ppermute | solution.py:422
  125.4 13.9 %collective-permute-start.19 = (f32[256,128]{1,0:T(8,128)}, f32[256,128]{1,0:T(8,128)S(1)}, u32[]{:S(2)}, u32[]{:S(2)}) collective-permute-start(f32[256,128]{1,0:T(8,128)} %get-tuple-element.187), channel_id=1, source_target_pairs={{0,16},{4,20},{8,24},{12,28},{16,0},{20,4},{24,8},{28,12},{1,17},{... | collective-permute-start | bytes 393224 | tf_op jit(solution)/shard_map/ppermute | solution.py:422
  150.6 106.7 %all-gather.5.cloned.1.call-start = ((), (), s32[]{:S(2)}) async-start(), calls=%async_computation.4 | async-start | bytes 2621440 | tf_op jit(solution)/shard_map/all_gather | solution.py:466
  182.3 12.6 %collective-permute-start.25 = (f32[256,128]{1,0:T(8,128)}, f32[256,128]{1,0:T(8,128)S(1)}, u32[]{:S(2)}, u32[]{:S(2)}) collective-permute-start(f32[256,128]{1,0:T(8,128)} %get-tuple-element.195), channel_id=1, source_target_pairs={{0,8},{4,12},{8,0},{12,4},{16,24},{20,28},{24,16},{28,20},{1,9},{5... | collective-permute-start | bytes 393224 | tf_op jit(solution)/shard_map/ppermute | solution.py:422
  185.7 14.0 %collective-permute-start.23 = (f32[256,128]{1,0:T(8,128)}, f32[256,128]{1,0:T(8,128)S(1)}, u32[]{:S(2)}, u32[]{:S(2)}) collective-permute-start(f32[256,128]{1,0:T(8,128)} %get-tuple-element.193), channel_id=1, source_target_pairs={{0,16},{4,20},{8,24},{12,28},{16,0},{20,4},{24,8},{28,12},{1,17},{... | collective-permute-start | bytes 393224 | tf_op jit(solution)/shard_map/ppermute | solution.py:422
  223.5 13.8 %collective-permute-start.31 = (f32[512,256]{1,0:T(8,128)}, f32[512,256]{1,0:T(8,128)S(1)}, u32[]{:S(2)}, u32[]{:S(2)}) collective-permute-start(f32[512,256]{1,0:T(8,128)} %get-tuple-element.216), channel_id=1, source_target_pairs={{0,4},{4,0},{8,12},{12,8},{16,20},{20,16},{24,28},{28,24},{1,5},{5... | collective-permute-start | bytes 1572872 | tf_op jit(solution)/shard_map/ppermute | solution.py:422
  229.8 15.0 %collective-permute-start.30 = (f32[1344,128]{1,0:T(8,128)}, f32[1344,128]{1,0:T(8,128)S(1)}, u32[]{:S(2)}, u32[]{:S(2)}) collective-permute-start(f32[1344,128]{1,0:T(8,128)} %add_dynamic-update-slice_fusion.2), channel_id=1, source_target_pairs={{0,16},{4,20},{8,24},{12,28},{16,0},{20,4},{24,8},{28,12},{1,17},{... | collective-permute-start | bytes 2064392 | tf_op jit(solution)/shard_map/ppermute | solution.py:422
  233.0 13.8 %collective-permute-start.28 = (f32[1344,128]{1,0:T(8,128)}, f32[1344,128]{1,0:T(8,128)S(1)}, u32[]{:S(2)}, u32[]{:S(2)}) collective-permute-start(f32[1344,128]{1,0:T(8,128)} %add_dynamic-update-slice_fusion.3), channel_id=1, source_target_pairs={{0,8},{4,12},{8,0},{12,4},{16,24},{20,28},{24,16},{28,20},{1,9},{5... | collective-permute-start | bytes 2064392 | tf_op jit(solution)/shard_map/ppermute | solution.py:422
  266.4 10.1 %collective-permute-start.36 = (f32[672,128]{1,0:T(8,128)}, f32[672,128]{1,0:T(8,128)S(1)}, u32[]{:S(2)}, u32[]{:S(2)}) collective-permute-start(f32[672,128]{1,0:T(8,128)} %get-tuple-element.213), channel_id=1, source_target_pairs={{0,8},{4,12},{8,0},{12,4},{16,24},{20,28},{24,16},{28,20},{1,9},{5... | collective-permute-start | bytes 1032200 | tf_op jit(solution)/shard_map/ppermute | solution.py:422
  267.9 11.8 %collective-permute-start.34 = (f32[672,128]{1,0:T(8,128)}, f32[672,128]{1,0:T(8,128)S(1)}, u32[]{:S(2)}, u32[]{:S(2)}) collective-permute-start(f32[672,128]{1,0:T(8,128)} %get-tuple-element.211), channel_id=1, source_target_pairs={{0,16},{4,20},{8,24},{12,28},{16,0},{20,4},{24,8},{28,12},{1,17},{... | collective-permute-start | bytes 1032200 | tf_op jit(solution)/shard_map/ppermute | solution.py:422
  278.2 16.5 %collective-permute-start.37 = (f32[1344,128]{1,0:T(8,128)}, f32[1344,128]{1,0:T(8,128)S(1)}, u32[]{:S(2)}, u32[]{:S(2)}) collective-permute-start(f32[1344,128]{1,0:T(8,128)} %add_dynamic-update-slice_fusion), channel_id=1, source_target_pairs={{0,16},{4,20},{8,24},{12,28},{16,0},{20,4},{24,8},{28,12},{1,17},{... | collective-permute-start | bytes 2064392 | tf_op jit(solution)/shard_map/ppermute | solution.py:422
  281.5 16.2 %collective-permute-start.35 = (f32[1344,128]{1,0:T(8,128)}, f32[1344,128]{1,0:T(8,128)S(1)}, u32[]{:S(2)}, u32[]{:S(2)}) collective-permute-start(f32[1344,128]{1,0:T(8,128)} %add_dynamic-update-slice_fusion.1), channel_id=1, source_target_pairs={{0,8},{4,12},{8,0},{12,4},{16,24},{20,28},{24,16},{28,20},{1,9},{5... | collective-permute-start | bytes 2064392 | tf_op jit(solution)/shard_map/ppermute | solution.py:422
  (44 other events, 279.3 us)
Sparse Core Ops, SparseCore 0:
  48.5 44.4 reduce-scatter.2
  95.3 43.1 reduce-scatter.4
  150.8 45.0 all-gather.6
  211.5 45.8 all-gather.4

commit v3 on v2

v3 whole, which is shorter than its diff:
```python
import functools

import jax
import jax.numpy as jnp
from jax import lax
from jax.experimental import pallas as pl
from jax.experimental.pallas import tpu as pltpu
from jax.sharding import PartitionSpec as P

HEAD_DIM = 128
TILE = 128
CAP = 2
SPAN = CAP * TILE

logit_scale = 168.0 ** (-0.5)
f32 = jnp.float32
bf16 = jnp.bfloat16
MIB = 1024 * 1024


def split(rows):
    high = rows.astype(bf16)
    return high, (rows - high.astype(f32)).astype(bf16)


def pair_cat(rows, axis):
    return jnp.concatenate(split(rows), axis=axis)


def dot(left, right):
    return jnp.dot(left, right, preferred_element_type=f32)


def dot_first(left, right):
    return lax.dot_general(left, right, (((0,), (0,)), ((), ())), preferred_element_type=f32)


def whole_spec(array):
    return pl.BlockSpec(array.shape, lambda *_: (0,) * len(array.shape))


smem_spec = pl.BlockSpec(memory_space=pltpu.SMEM)


def project_body(place_ref, *refs, row_inputs, pieces, parts, steps_each):
    x_refs = refs[:row_inputs]
    w_refs = refs[row_inputs : row_inputs + len(pieces)]
    out_ref, pair_ref, x_ref = refs[-3:]
    step, part_step = pl.program_id(0), pl.program_id(1)
    columns = x_refs[0].shape[1]

    @pl.when((step == 0) & (part_step == 0))
    def _():
        for (part, start), w_ref in zip(pieces, w_refs):
            high, low = split(w_ref[...].T)
            stop = start + w_ref.shape[0]
            pair_ref[part, :HEAD_DIM, start:stop] = high
            pair_ref[part, HEAD_DIM:, start:stop] = low

    for source in range(row_inputs):

        @pl.when((step // steps_each == source) & (part_step == 0))
        def _():
            high, low = split(x_refs[source][...])
            x_ref[:, :columns] = high
            x_ref[:, columns:] = low

    total = dot(pair_ref[part_step], x_ref[...])
    total = total[:, :columns] + total[:, columns:]
    out_ref[0] = total[:HEAD_DIM] + total[HEAD_DIM:]


def project(place, slots, xs, pieces, ws, before=None):
    depth, rows = xs[0].shape
    block = 256
    steps_each = rows // block
    first = slots[0]

    def x_map(source):
        return lambda step, part, place_ref: (0, jnp.clip(step - source * steps_each, 0, steps_each - 1))

    extra = [] if before is None else [before]
    return pl.pallas_call(
        functools.partial(project_body, row_inputs=len(xs), pieces=pieces, parts=len(slots), steps_each=steps_each),
        grid_spec=pltpu.PrefetchScalarGridSpec(
            num_scalar_prefetch=1,
            grid=(steps_each * len(xs), len(slots)),
            in_specs=[pl.BlockSpec((depth, block), x_map(source)) for source in range(len(xs))]
            + [whole_spec(w) for w in ws]
            + [pl.BlockSpec(memory_space=pl.ANY)] * len(extra),
            out_specs=pl.BlockSpec((1, HEAD_DIM, block), lambda step, part, place_ref: (place_ref[first + part], 0, step)),
            scratch_shapes=[pltpu.VMEM((len(slots), 2 * HEAD_DIM, depth), bf16), pltpu.VMEM((depth, 2 * block), bf16)],
        ),
        out_shape=jax.ShapeDtypeStruct((place.shape[0], HEAD_DIM, rows * len(xs)), f32),
        input_output_aliases={1 + len(xs) + len(ws): 0} if extra else {},
        compiler_params=pltpu.CompilerParams(vmem_limit_bytes=24 * MIB),
        cost_estimate=pl.CostEstimate(
            flops=6 * rows * len(xs) * depth * len(slots) * HEAD_DIM, bytes_accessed=4 * rows * len(xs) * depth, transcendentals=0
        ),
    )(place, *xs, *ws, *extra)


def weight_grad_body(place_ref, *refs, row_inputs, parts):
    x_refs = refs[:row_inputs]
    g_refs = refs[row_inputs : row_inputs + parts]
    out_refs, pair_ref = refs[row_inputs + parts : -1], refs[-1]
    rows = x_refs[0].shape[1]
    step, half = pl.program_id(0), pl.num_programs(0) // 2

    @pl.when(step == 0)
    def _():
        for part in range(parts):
            pair_ref[:, 2 * part * HEAD_DIM : 2 * (part + 1) * HEAD_DIM] = pair_cat(g_refs[part][0], 1)

    total = 0.0
    for source in range(row_inputs):
        high, low = split(x_refs[source][...])
        pair = pair_ref[source * rows : (source + 1) * rows]
        total += dot(high, pair) + dot(low, pair)
    for part in range(parts):
        value = total[:, 2 * part * HEAD_DIM : (2 * part + 1) * HEAD_DIM] + total[:, (2 * part + 1) * HEAD_DIM : 2 * (part + 1) * HEAD_DIM]
        for piece in range(2):

            @pl.when(step // half == piece)
            def _():
                out_refs[2 * part + piece][...] = value


def weight_grad(place, slots, xs, grads):
    depth, rows = xs[0].shape
    parts = len(slots)
    steps = 4
    half = steps // 2
    block = depth // steps

    def g_map(slot):
        return lambda step, place_ref: (place_ref[slot], 0, 0)

    head = pl.BlockSpec((block, HEAD_DIM), lambda step, place_ref: (jnp.minimum(step, half - 1), 0))
    tail = pl.BlockSpec((block, HEAD_DIM), lambda step, place_ref: (jnp.maximum(step - half, 0), 0))
    return pl.pallas_call(
        functools.partial(weight_grad_body, row_inputs=len(xs), parts=parts),
        grid_spec=pltpu.PrefetchScalarGridSpec(
            num_scalar_prefetch=1,
            grid=(steps,),
            in_specs=[pl.BlockSpec((block, rows), lambda step, place_ref: (step, 0))] * len(xs)
            + [pl.BlockSpec((1, *grads.shape[1:]), g_map(slot)) for slot in slots],
            out_specs=[head, tail] * parts,
            scratch_shapes=[pltpu.VMEM((rows * len(xs), 2 * parts * HEAD_DIM), bf16)],
        ),
        out_shape=[jax.ShapeDtypeStruct((block * half, HEAD_DIM), f32)] * (2 * parts),
        compiler_params=pltpu.CompilerParams(vmem_limit_bytes=24 * MIB),
        cost_estimate=pl.CostEstimate(
            flops=6 * rows * len(xs) * depth * parts * HEAD_DIM, bytes_accessed=4 * rows * len(xs) * depth, transcendentals=0
        ),
    )(place, *xs, *[grads] * parts)


def combine_body(own_ref, *refs, starts):
    out_ref = refs[-1]
    out_ref[...] = own_ref[...]
    for index, start in enumerate(starts):
        first, second = refs[2 * index], refs[2 * index + 1]
        out_ref[start : start + first.shape[0], :] += first[...] + second[...]


def combine(own, starts, arrivals):
    return pl.pallas_call(
        functools.partial(combine_body, starts=starts),
        out_shape=jax.ShapeDtypeStruct(own.shape, f32),
        compiler_params=pltpu.CompilerParams(vmem_limit_bytes=24 * MIB),
        cost_estimate=pl.CostEstimate(flops=own.size, bytes_accessed=12 * own.size, transcendentals=0),
    )(own, *arrivals)


def list_ancestors(fork_ref, offset_ref, limit_ref, many_ref, tok, slots, tiles, paired):
    for slot in range(slots):

        def climb(carry, slot=slot):
            current, count = carry
            fork_at = fork_ref[current - 1]
            parent = lax.div(fork_at, jnp.int32(tiles))
            offset_ref[slot, count] = ((tok ^ parent) if paired else parent) * SPAN
            limit_ref[slot, count] = (lax.rem(fork_at, jnp.int32(tiles)) + 1) * TILE - 1
            return parent, count + 1

        _, count = lax.while_loop(lambda carry: carry[0] > 0, climb, (tok ^ slot, jnp.int32(0)))
        many_ref[slot] = count
        offset_ref[slot, count] = 0
        limit_ref[slot, count] = -1


def find_step(many_ref, step, tok, halves):
    slot, half = lax.div(step, jnp.int32(halves)), lax.rem(step, jnp.int32(halves))
    return tok ^ slot, slot, half, half + 1 + many_ref[slot]


def block_offset(offset_ref, base, slot, half, halves, block):
    later = jnp.maximum(block - half - 1, 0)
    return jnp.where(block <= half, base + (slot * halves + block) * SPAN, offset_ref[slot, later])


def even(count):
    return 2 * lax.div(count + 1, jnp.int32(2))


def paired_loop(count, body, start, before=None):
    def both(pair, carry):
        if before is not None:
            before(2 * pair)
            before(2 * pair + 1)
        return body(2 * pair + 1, body(2 * pair, carry))

    return lax.fori_loop(0, lax.div(count + 1, jnp.int32(2)), both, start)


def key_limits(limit_ref, slot, half, live, block, lanes):
    lane = lax.broadcasted_iota(jnp.int32, (1, lanes), 1)
    position = half * SPAN + lax.rem(lane, jnp.int32(SPAN))
    own_limit = jnp.minimum(position, live - 1) - block * SPAN
    return jnp.where(block <= half, own_limit, limit_ref[slot, jnp.maximum(block - half - 1, 0)])


def transposed_pair(rows):
    high, low = split(rows.T)
    return jnp.concatenate([high, high, low, low], axis=0)


def load_rows(ref, half, head):
    return ref[pl.ds(pl.multiple_of(half * SPAN, SPAN), SPAN), head * HEAD_DIM : (head + 1) * HEAD_DIM]


def live_column(half, live):
    position = half * SPAN + lax.broadcasted_iota(jnp.int32, (SPAN, 1), 0)
    return (position < live).astype(f32)


def block_rows(ref, offset):
    return ref[pl.ds(pl.multiple_of(offset, SPAN), SPAN), :]


def slot_rows(block):
    return pl.ds(pl.multiple_of(block * SPAN, SPAN), SPAN)


def stage_rows(target_ref, source_refs, layout):
    for index, start, offset, count in layout:
        for piece in range(0, count, SPAN):
            target_ref[offset + piece : offset + piece + SPAN, :] = pair_cat(
                source_refs[index][:, start + piece : start + piece + SPAN].T, 1
            )


def write_rows(source_ref, target_refs, layout, sums):
    for target_ref, (start, offset, count) in zip(target_refs, sums):
        target_ref[start : start + count, :] = source_ref[offset : offset + count, :]
    own = layout[0]
    target_refs[-1][...] = source_ref[own[2] : own[2] + own[3], :]
    for index, start, offset, count in layout[1:]:
        if index == 0:
            target_refs[-1][start : start + count, :] += source_ref[offset : offset + count, :]


def scores(keys_ref, offset, queries, limits):
    keys = block_rows(keys_ref, offset)
    result = dot(jnp.concatenate([keys, keys], axis=1), queries)
    row = lax.broadcasted_iota(jnp.int32, result.shape, 0)
    return jnp.where(row <= limits, result, -1e30)


def fold(value, how):
    return how(value.reshape(SPAN // 8, 8, value.shape[1]), axis=0)


def soft_body(tok_ref, fork_ref, live_ref, *refs, conf):
    nb, group, owners, layout, sources, outs = conf["nb"], conf["group"], conf["owners"], conf["layout"], conf["sources"], conf["outs"]
    halves = conf["rows"] // SPAN
    lanes = group * SPAN
    q_refs, g_refs = refs[:nb], refs[nb : 2 * nb]
    key_refs = refs[2 * nb : 2 * nb + sources]
    prob_ref = refs[2 * nb + sources]
    out_refs = refs[2 * nb + sources + 1 : 2 * nb + sources + 1 + outs]
    keys_ref, sum_ref, scores_ref, qt_ref, grad_ref, offset_ref, limit_ref, many_ref, sems = refs[2 * nb + sources + 1 + outs :]
    step = pl.program_id(0)
    tok = tok_ref[0]
    turn = lax.rem(step, 2)
    score_ref = scores_ref.at[turn]

    def copy_out(of_step, block):
        side = lax.rem(of_step, 2)
        rows = slot_rows(block)
        return pltpu.make_async_copy(scores_ref.at[side, rows], prob_ref.at[of_step, rows], sems.at[side, block])

    def wait_out(of_step):
        def wait(block, _):
            copy_out(of_step, block).wait()
            return 0

        lax.fori_loop(0, even(find_step(many_ref, of_step, tok, halves)[3]), wait, 0)

    @pl.when(step == 0)
    def _():
        list_ancestors(fork_ref, offset_ref, limit_ref, many_ref, tok, nb, conf["rows"] // TILE, conf["paired"])
        stage_rows(keys_ref, key_refs, layout)
        sum_ref[...] = jnp.zeros_like(sum_ref)

    branch, slot, half, count = find_step(many_ref, step, tok, halves)
    place_of = functools.partial(block_offset, offset_ref, owners * SPAN, slot, half, halves)
    live = live_ref[branch]
    for source in range(nb):

        @pl.when(slot == source)
        def _():
            for head in range(group):
                qt_ref[:, head * SPAN : (head + 1) * SPAN] = transposed_pair(load_rows(q_refs[source], half, head) * logit_scale)
                grad_ref[head * SPAN : (head + 1) * SPAN, :] = pair_cat(
                    load_rows(g_refs[source], half, head) * live_column(half, live), 1
                )

    def first(block, largest):
        value = scores(keys_ref, place_of(block), qt_ref[...], key_limits(limit_ref, slot, half, live, block, lanes))
        score_ref[slot_rows(block), :] = value
        return jnp.maximum(largest, fold(value, jnp.max))

    largest = paired_loop(count, first, jnp.full((8, lanes), -1e30, f32))
    largest = jnp.max(largest, axis=0, keepdims=True)

    def second(block, total):
        value = jnp.exp(score_ref[slot_rows(block), :] - largest)
        score_ref[slot_rows(block), :] = value
        return total + fold(value, jnp.sum)

    total = paired_loop(count, second, jnp.zeros((8, lanes), f32))
    inverse = 1.0 / jnp.sum(total, axis=0, keepdims=True)

    def third(block, _):
        prob = score_ref[slot_rows(block), :] * inverse
        score_ref[slot_rows(block), :] = prob
        copy_out(step, block).start()
        high, low = split(prob)
        grads = grad_ref[...]
        both = dot(high, grads) + dot(low, grads)
        offset = place_of(block)
        sum_ref[slot_rows(offset // SPAN), :] += both[:, :HEAD_DIM] + both[:, HEAD_DIM:]
        return 0

    paired_loop(count, third, 0)

    @pl.when(step > 0)
    def _():
        wait_out(step - 1)

    @pl.when(step == nb * halves - 1)
    def _():
        wait_out(step)
        write_rows(sum_ref, out_refs, layout, conf["sums"])


def grad_body(tok_ref, fork_ref, live_ref, *refs, conf):
    nb, group, owners, layout, sources, outs = conf["nb"], conf["group"], conf["owners"], conf["layout"], conf["sources"], conf["outs"]
    halves = conf["rows"] // SPAN
    lanes = group * SPAN
    q_refs, g_refs = refs[:nb], refs[nb : 2 * nb]
    at = 2 * nb
    key_refs, value_refs = refs[at : at + sources], refs[at + sources : at + 2 * sources]
    at += 2 * sources
    prob_ref = refs[at]
    dq_ref = refs[at + 1]
    out_refs = refs[at + 2 : at + 2 + outs]
    (keys_ref, values_ref, sum_ref, probs_ref, dprob_ref, gt_ref, q_ref, dqt_ref, offset_ref, limit_ref, many_ref, sems) = refs[at + 2 + outs :]
    step = pl.program_id(0)
    tok = tok_ref[0]
    held_ref = probs_ref.at[lax.rem(step, 2)]

    def copy_in(of_step, block):
        side = lax.rem(of_step, 2)
        rows = slot_rows(block)
        return pltpu.make_async_copy(prob_ref.at[of_step, rows], probs_ref.at[side, rows], sems.at[side, block])

    def start_in(of_step):
        def start(block, _):
            copy_in(of_step, block).start()
            return 0

        lax.fori_loop(0, even(find_step(many_ref, of_step, tok, halves)[3]), start, 0)

    @pl.when(step == 0)
    def _():
        list_ancestors(fork_ref, offset_ref, limit_ref, many_ref, tok, nb, conf["rows"] // TILE, conf["paired"])
        start_in(step)
        stage_rows(keys_ref, key_refs, layout)
        stage_rows(values_ref, value_refs, layout)
        sum_ref[...] = jnp.zeros_like(sum_ref)

    @pl.when(step < nb * halves - 1)
    def _():
        start_in(step + 1)

    branch, slot, half, count = find_step(many_ref, step, tok, halves)
    place_of = functools.partial(block_offset, offset_ref, owners * SPAN, slot, half, halves)
    live = live_ref[branch]
    for source in range(nb):

        @pl.when(slot == source)
        def _():
            for head in range(group):
                rows = load_rows(q_refs[source], half, head) * logit_scale
                q_ref[head * SPAN : (head + 1) * SPAN, :] = pair_cat(rows, 1)
                gt_ref[:, head * SPAN : (head + 1) * SPAN] = transposed_pair(
                    load_rows(g_refs[source], half, head) * live_column(half, live)
                )

    def first(block, delta):
        values = block_rows(values_ref, place_of(block))
        dprob = dot(jnp.concatenate([values, values], axis=1), gt_ref[...])
        dprob_ref[slot_rows(block), :] = dprob
        return delta + fold(held_ref[slot_rows(block), :] * dprob, jnp.sum)

    delta = paired_loop(count, first, jnp.zeros((8, lanes), f32), lambda block: copy_in(step, block).wait())
    delta = jnp.sum(delta, axis=0, keepdims=True)
    dqt_ref[...] = jnp.zeros_like(dqt_ref)

    def second(block, _):
        offset = place_of(block)
        high, low = split(held_ref[slot_rows(block), :] * (dprob_ref[slot_rows(block), :] - delta))
        rows = q_ref[...]
        both = dot(high, rows) + dot(low, rows)
        sum_ref[slot_rows(offset // SPAN), :] += both[:, :HEAD_DIM] + both[:, HEAD_DIM:]
        keys = block_rows(keys_ref, offset)
        dqt_ref[...] += dot_first(keys, high) + dot_first(keys, low)
        return 0

    paired_loop(count, second, 0)
    folded = (dqt_ref[:HEAD_DIM, :] + dqt_ref[HEAD_DIM:, :]) * logit_scale
    for head in range(group):
        dq_ref[:, head * HEAD_DIM : (head + 1) * HEAD_DIM] = folded[:, head * SPAN : (head + 1) * SPAN].T

    @pl.when(step == nb * halves - 1)
    def _():
        write_rows(sum_ref, out_refs, layout, conf["sums"])


def attention_calls(scalars, qs, gs, layout, sum_rows, paired, owners, parts):
    rows, width = qs[0].shape
    nb, group, halves = len(qs), width // HEAD_DIM, rows // SPAN
    lanes = group * SPAN
    steps = nb * halves
    conf = dict(nb=nb, group=group, rows=rows, owners=owners, layout=layout, paired=paired, sources=1 + parts, sums=sum_rows, outs=len(sum_rows) + 1)
    table_rows = owners * SPAN + nb * rows
    slots = (owners + halves) * SPAN
    sums = [jax.ShapeDtypeStruct((count, HEAD_DIM), f32) for _, _, count in sum_rows] + [jax.ShapeDtypeStruct((nb * rows, HEAD_DIM), f32)]
    probs = jax.ShapeDtypeStruct((steps, slots, lanes), f32)
    probs_spec = pl.BlockSpec(memory_space=pl.ANY)
    two_squares = pltpu.VMEM((2, slots, lanes), f32)
    sems = pltpu.SemaphoreType.DMA((2, slots // SPAN))
    table = pltpu.VMEM((table_rows, 2 * HEAD_DIM), bf16)
    table_sum = pltpu.VMEM((table_rows, HEAD_DIM), f32)
    square = pltpu.VMEM((slots, lanes), f32)
    columns = pltpu.VMEM((4 * HEAD_DIM, lanes), bf16)
    lists = [pltpu.SMEM((nb, owners + 1), jnp.int32)] * 2 + [pltpu.SMEM((nb,), jnp.int32)]
    params = pltpu.CompilerParams(vmem_limit_bytes=56 * MIB)
    work = 2 * steps * 6 * SPAN * lanes * 2 * HEAD_DIM

    def soft(keys):
        return pl.pallas_call(
            functools.partial(soft_body, conf=conf),
            grid=(steps,),
            in_specs=[smem_spec] * 3 + [whole_spec(a) for a in (*qs, *gs, *keys)],
            out_specs=[probs_spec] + [whole_spec(a) for a in sums],
            out_shape=[probs] + sums,
            scratch_shapes=[table, table_sum, two_squares, columns, pltpu.VMEM((lanes, 2 * HEAD_DIM), bf16)]
            + lists
            + [sems],
            compiler_params=params,
            cost_estimate=pl.CostEstimate(flops=2 * work, bytes_accessed=4 * rows * width, transcendentals=0),
        )(*scalars, *qs, *gs, *keys)

    def grad(keys, values, probs_in):
        dq = jax.ShapeDtypeStruct((nb * rows, width), f32)
        return pl.pallas_call(
            functools.partial(grad_body, conf=conf),
            grid=(steps,),
            in_specs=[smem_spec] * 3 + [whole_spec(a) for a in (*qs, *gs, *keys, *values)] + [probs_spec],
            out_specs=[pl.BlockSpec((SPAN, width), lambda step: (step, 0))] + [whole_spec(a) for a in sums],
            out_shape=[dq] + sums,
            scratch_shapes=[
                table,
                table,
                table_sum,
                two_squares,
                square,
                columns,
                pltpu.VMEM((lanes, 2 * HEAD_DIM), bf16),
                pltpu.VMEM((2 * HEAD_DIM, lanes), f32),
            ]
            + lists
            + [sems],
            compiler_params=params,
            cost_estimate=pl.CostEstimate(flops=4 * work, bytes_accessed=4 * rows * width, transcendentals=0),
        )(*scalars, *qs, *gs, *keys, *values, probs_in)

    return soft, grad


def flip(array, mask):
    count = lax.axis_size("tok")
    return lax.ppermute(array, "tok", [(index, index ^ mask) for index in range(count)])


def together(*arrays):
    return lax.optimization_barrier(arrays)


def gather_square(array, cut, axis):
    across, down = flip(array, 2), flip(array, 4)
    head = lax.slice_in_dim(across, 0, cut, axis=axis)
    tail = lax.slice_in_dim(down, cut, down.shape[axis], axis=axis)
    return across, down, flip(head, 4), flip(tail, 2)


def scatter_square(across, down, corner):
    from_across, from_down = flip(corner[0], 2), flip(corner[1], 4)
    across_head, down_tail = flip(across[0], 2), flip(down[1], 4)
    across_tail, down_head = flip(across[1] + from_down, 2), flip(down[0] + from_across, 4)
    return across_head, down_head, across_tail, down_tail


def shards_paired(hidden, queries, out_grad, w_key, w_value, fork_tile, live_len):
    owners = lax.axis_size("tok")
    depth = lax.axis_size("head")
    tok = lax.axis_index("tok").astype(jnp.int32)
    core = tok & 1
    rows = hidden.shape[0]
    width = queries.shape[1] // 2
    scalars = (tok.reshape(1), fork_tile, live_len)
    place = (tok >> 1) ^ jnp.arange(depth, dtype=jnp.int32)
    cut = w_key.shape[0] // (2 * HEAD_DIM) * HEAD_DIM

    def mine(array):
        return lax.dynamic_slice_in_dim(array, core * width, width, 1)

    def partners(array):
        return flip(lax.dynamic_slice_in_dim(array, (1 - core) * width, width, 1), 1)

    def project_all(w):
        partial = project(place, (0,), xs, ((0, 0),), [w])
        across, down = flip(w, 2), flip(w, 4)
        across, down, partial = together(across, down, partial)
        head, tail = flip(across[:cut], 4), flip(down[cut:], 2)
        partial = project(place, (1, 2), xs, ((0, 0), (1, 0)), [across, down], partial)
        return project(place, (3,), xs, ((0, 0), (0, cut)), [head, tail], partial)

    def sum_heads(partial):
        return lax.psum_scatter(partial, "head", scatter_dimension=0, tiled=True)[0]

    def all_heads(grads):
        return lax.all_gather(grads, "head", axis=0, tiled=False)

    def lead(array):
        return jnp.concatenate([array[:, :SPAN], array[:, rows : rows + SPAN]], axis=1)

    def returned(across_head, across_tail, down_head, down_tail, corner_head, corner_tail, own):
        arrivals = scatter_square((across_head, across_tail), (down_head, down_tail), (corner_head, corner_tail))
        return combine(own, (0, rows), arrivals)

    def weight(every):
        corner = weight_grad(place, (3,), xs, every)
        across_head, across_tail, down_head, down_tail = weight_grad(place, (1, 2), xs, every)
        kept = weight_grad(place, (0,), xs, every)
        arrivals = scatter_square((across_head, across_tail), (down_head, down_tail), corner)
        return kept, arrivals

    def finish(kept, arrivals):
        across_head, down_head, across_tail, down_tail = arrivals
        return jnp.concatenate([kept[0] + across_head + down_head, kept[1] + across_tail + down_tail], axis=0)

    def home(array):
        kept, received = array[:rows], flip(array[rows:], 1)
        return jnp.where(core == 0, jnp.concatenate([kept, received], axis=1), jnp.concatenate([received, kept], axis=1))

    hidden = hidden.T
    xs = [hidden, flip(hidden, 1)]
    qs = [mine(queries), partners(queries)]
    gs = [mine(out_grad), partners(out_grad)]
    keys = sum_heads(project_all(w_key))
    values = sum_heads(project_all(w_value))

    base = owners * SPAN
    layout = (
        (0, 0, base, 2 * rows),
        (0, 0, 0, SPAN),
        (0, rows, SPAN, SPAN),
        (1, 0, 2 * SPAN, 2 * SPAN),
        (2, 0, 4 * SPAN, 2 * SPAN),
        (3, 0, 6 * SPAN, SPAN),
        (4, 0, 7 * SPAN, SPAN),
    )
    sums = tuple((0, (2 + index) * SPAN, SPAN) for index in range(6))
    soft, grad = attention_calls(scalars, qs, gs, layout, sums, True, owners, 4)

    key_parts = [keys, *gather_square(lead(keys), SPAN, 1)]
    probs, *value_sums = soft(key_parts)
    values, *value_sums = together(values, *value_sums)
    across_head, across_tail, down_head, down_tail, corner_head, corner_tail, own = value_sums
    leading = lead(values)
    value_across, value_down = flip(leading, 2), flip(leading, 4)
    from_across, from_down = flip(corner_head, 2), flip(corner_tail, 4)
    across_head, down_tail = flip(across_head, 2), flip(down_tail, 4)
    value_across, value_down, from_across, from_down = together(value_across, value_down, from_across, from_down)
    value_parts = [values, value_across, value_down, flip(value_across[:, :SPAN], 4), flip(value_down[:, SPAN:], 2)]
    across_tail, down_head = flip(across_tail + from_down, 2), flip(down_head + from_across, 4)
    *value_parts, across_tail, down_head = together(*value_parts, across_tail, down_head)
    value_grads = combine(own, (0, rows), (across_head, down_head, across_tail, down_tail))
    every_value = all_heads(value_grads)
    probs, value_grads = together(probs, value_grads)
    grad_query, *key_sums = grad(key_parts, value_parts, probs)
    key_grads = returned(*key_sums)
    every_key = all_heads(key_grads)
    every_value, key_grads = together(every_value, key_grads)
    grad_w_value = finish(*weight(every_value))
    grad_query, grad_key, grad_value = home(grad_query), home(key_grads), home(value_grads)
    every_key, grad_w_value, grad_query, grad_key, grad_value = together(every_key, grad_w_value, grad_query, grad_key, grad_value)
    grad_w_key = finish(*weight(every_key))
    return grad_query, grad_key, grad_value, grad_w_key, grad_w_value


def shards_single(hidden, queries, out_grad, w_key, w_value, fork_tile, live_len):
    owners = lax.axis_size("tok")
    tok = lax.axis_index("tok").astype(jnp.int32)
    scalars = (tok.reshape(1), fork_tile, live_len)

    def projected(w):
        every = lax.all_gather(w, "tok", axis=1, tiled=True)
        partial = lax.dot_general(every, hidden, (((0,), (1,)), ((), ())), precision=lax.Precision.HIGHEST)
        return lax.psum_scatter(partial, "head", scatter_dimension=0, tiled=True)

    keys, values = projected(w_key), projected(w_value)
    layout = ((0, 0, owners * SPAN, hidden.shape[0]), (1, 0, 0, owners * SPAN))
    sums = ((0, 0, owners * SPAN),)
    soft, grad = attention_calls(scalars, [queries], [out_grad], layout, sums, False, owners, 1)

    def parts(array):
        return [array, lax.all_gather(array[:, :SPAN], "tok", axis=1, tiled=True)]

    def returned(remote, own):
        return own.at[:SPAN].add(lax.psum_scatter(remote, "tok", scatter_dimension=0, tiled=True))

    def weight(grads):
        every = lax.all_gather(grads, "head", axis=1, tiled=True)
        columns = lax.dot_general(hidden, every, (((0,), (0,)), ((), ())), precision=lax.Precision.HIGHEST)
        return lax.psum_scatter(columns, "tok", scatter_dimension=1, tiled=True)

    key_parts = parts(keys)
    probs, *value_sums = soft(key_parts)
    value_grads = returned(*value_sums)
    grad_query, *key_sums = grad(key_parts, parts(values), probs)
    key_grads = returned(*key_sums)
    return grad_query, key_grads, value_grads, weight(key_grads), weight(value_grads)


def shards(hidden, queries, out_grad, w_key, w_value, fork_tile, live_len):
    pairs = lax.axis_size("tok") // 2
    whole_heads = w_key.shape[1] == HEAD_DIM
    paired = whole_heads and pairs == lax.axis_size("head") and pairs == 4
    run = shards_paired if paired else shards_single
    return run(hidden, queries, out_grad, w_key, w_value, fork_tile, live_len)


def solution(mesh):
    placed = (P("tok", "head"), P("tok", "head"), P("tok", "head"), P("head", "tok"), P("head", "tok"), P(), P())
    return jax.shard_map(
        shards,
        mesh=mesh,
        in_specs=placed,
        out_specs=(P("tok", "head"), P("tok", "head"), P("tok", "head"), P("head", "tok"), P("head", "tok")),
        check_vma=False,
    )
```

time: 309 us -> 295 us (0.955)
  waiting for transfers between devices: 119 us -> 95.5 us
  local copies, waits for them, and re-layouts: 10.6 us -> 29.3 us
  other arithmetic: 26 us -> 9.96 us
  Pallas kernels: 65.4 us -> 78.9 us
  starting transfers between devices: 70 us -> 66.2 us
    ppermute x38 -> x46, waiting for transfers between devices: 106 us -> 60.1 us  [flip(): lax.ppermute(array, 'tok', [(index, index ^ mask) for index in range(coun...]
    reduce_scatter x2, waiting for transfers between devices: 3.46 us -> 25.6 us  [sum_heads(): return lax.psum_scatter(partial, 'head', scatter_dimension=0, tiled=True)[0]]
    scatter-add x12 -> x0, other arithmetic: 19.6 us -> none  [the longest x4 6.67 us: scatter_square(): across = across.at[cut:].add(from_down)]
    pallas_call x2 -> x8, Pallas kernels: 20 us -> 34.4 us  [the longest x6 32.7 us: project(): pl.pallas_call(functools.partial(project_body, row_inputs=len(xs), pieces...]
    unnamed x52 -> x54, local copies, waits for them, and re-layouts: 5.75 us -> 18.6 us
    ppermute x38 -> x46, starting transfers between devices: 69.7 us -> 65.8 us  [flip(): lax.ppermute(array, 'tok', [(index, index ^ mask) for index in range(coun...]
    slice x3, local copies, waits for them, and re-layouts: 0.93 us -> 4.19 us  [home(): kept, received = (array[:rows], flip(array[rows:], 1))]
    pallas_call x2 -> x6, Pallas kernels: 18 us -> 20.6 us  [weight_grad(): pl.pallas_call(functools.partial(weight_grad_body, row_inputs=len(xs), pa...]
  transfers between devices with their start and end apart: 42 -> 50, of which waited for: 25 -> 25; matrix products, arithmetic and copies ran while one was open for 10% -> 6% of each run, Pallas kernels for 15% -> 24%
where the time goes in v3:
time: 295 us; the launch traced here: 294 us
  waiting for transfers between devices  95.5 us (32%)
  Pallas kernels  78.9 us (27%)
  starting transfers between devices  66.2 us (22%)
  local copies, waits for them, and re-layouts  29.3 us (10%)
  between operations  14.2 us (5%)
  other arithmetic  9.96 us (3%)
    ppermute x46, starting transfers between devices, flip(): lax.ppermute(array, 'tok', [(index, index ^ mask) for index in range(coun...  65.8 us
    ppermute x46, waiting for transfers between devices, flip(): lax.ppermute(array, 'tok', [(index, index ^ mask) for index in range(coun...  60.1 us
    pallas_call x6, Pallas kernels, project(): pl.pallas_call(functools.partial(project_body, row_inputs=len(xs), pieces...  32.7 us
    reduce_scatter x2, waiting for transfers between devices, sum_heads(): return lax.psum_scatter(partial, 'head', scatter_dimension=0, tiled=True)[0]  25.6 us
    pallas_call x6, Pallas kernels, weight_grad(): pl.pallas_call(functools.partial(weight_grad_body, row_inputs=len(xs), pa...  20.6 us
    unnamed x54, local copies, waits for them, and re-layouts  18.6 us
    pallas_call x1, Pallas kernels, grad(): pl.pallas_call(functools.partial(grad_body, conf=conf), grid=(steps,), in...  12.7 us
    pallas_call x1, Pallas kernels, soft(): pl.pallas_call(functools.partial(soft_body, conf=conf), grid=(steps,), in...  11.2 us
  transfers between devices with their start and end apart: 50, of which 25 were waited for; matrix products, arithmetic and copies ran while one was open for 6% of the time, Pallas kernels for 24%

profile of v3, /device:TPU:0, one launch (start us, length us, event | category | flops | bytes accessed | tf_op | source)
XLA Modules:
  0.0 293.9 jit_solution(13199358148807146163)
XLA Ops:
  15.5 4.4 %shard_map.110.refs_4_ = f32[4,128,1024]{2,1,0:T(8,128)S(1)} custom-call(s32[4]{0:T(128)S(1)} %iota_xor_fusion.place_ref, f32[1344,512]{1,0:T(8,128)S(1)} %bitcast.7, f32[1344,512]{1,0:T(8,128)S(1)} %collective-permute-done.2.refs_1_, f32[1344,128]{1,0:T(8,128)S(1)} %copy-done.11), custom_call_target="tpu_custom_call" | custom-call | flops 1056964608 | bytes 5505024 | tf_op jit(solution)/shard_map/pallas_call | solution.py:83
  19.9 6.7 %collective-permute-done.3.refs_2_ = f32[1344,128]{1,0:T(8,128)} collective-permute-done((f32[1344,128]{1,0:T(8,128)}, f32[1344,128]{1,0:T(8,128)}, u32[]{:S(2)}, u32[]{:S(2)}) %collective-permute-start.3) | collective-permute-done | bytes 688160 | tf_op jit(solution)/shard_map/ppermute | solution.py:507
  31.2 8.2 %shard_map.111.refs_4_ = f32[4,128,1024]{2,1,0:T(8,128)S(1)} custom-call(s32[4]{0:T(128)S(1)} %iota_xor_fusion.place_ref, f32[1344,512]{1,0:T(8,128)S(1)} %bitcast.8, f32[1344,512]{1,0:T(8,128)S(1)} %collective-permute-done.2.refs_1_, f32[1344,128]{1,0:T(8,128)} %collective-permute-done.3.refs_2_, ...), custom_call_target="tpu_custom_call", output_to_operand_aliasing={{}: (5, {})} | custom-call | flops 2113929216 | bytes 5505024 | tf_op jit(solution)/shard_map/pallas_call | solution.py:83
  41.2 4.4 %shard_map.112 = f32[4,128,1024]{2,1,0:T(8,128)S(1)} custom-call(s32[4]{0:T(128)S(1)} %iota_xor_fusion.place_ref, f32[1344,512]{1,0:T(8,128)S(1)} %bitcast.9, f32[1344,512]{1,0:T(8,128)S(1)} %copy-done.3, f32[640,128]{1,0:T(8,128)S(1)} %collective-permute-done.5.refs_2_, ...), custom_call_target="tpu_custom_call", output_to_operand_aliasing={{}: (5, {})} | custom-call | flops 1056964608 | bytes 5505024 | tf_op jit(solution)/shard_map/pallas_call | solution.py:83
  51.8 4.4 %shard_map.113.refs_4_ = f32[4,128,1024]{2,1,0:T(8,128)S(1)} custom-call(s32[4]{0:T(128)S(1)} %iota_xor_fusion.place_ref, f32[1344,512]{1,0:T(8,128)S(1)} %bitcast.10, f32[1344,512]{1,0:T(8,128)S(1)} %copy-done.4, f32[1344,128]{1,0:T(8,128)S(1)} %copy-done.12), custom_call_target="tpu_custom_call" | custom-call | flops 1056964608 | bytes 5505024 | tf_op jit(solution)/shard_map/pallas_call | solution.py:83
  56.1 8.1 %collective-permute-done.11.refs_2_ = f32[1344,128]{1,0:T(8,128)S(1)} collective-permute-done((f32[1344,128]{1,0:T(8,128)S(1)}, f32[1344,128]{1,0:T(8,128)S(1)}, u32[]{:S(2)}, u32[]{:S(2)}) %collective-permute-start.11) | collective-permute-done | bytes 688160 | tf_op jit(solution)/shard_map/ppermute | solution.py:507
  66.7 7.1 %shard_map.114.refs_4_ = f32[4,128,1024]{2,1,0:T(8,128)S(1)} custom-call(s32[4]{0:T(128)S(1)} %iota_xor_fusion.place_ref, f32[1344,512]{1,0:T(8,128)S(1)} %bitcast.11, f32[1344,512]{1,0:T(8,128)S(1)} %copy-done.4, f32[1344,128]{1,0:T(8,128)S(1)} %collective-permute-done.11.refs_2_, ...), custom_call_target="tpu_custom_call", output_to_operand_aliasing={{}: (5, {})} | custom-call | flops 2113929216 | bytes 5505024 | tf_op jit(solution)/shard_map/pallas_call | solution.py:83
  73.8 4.4 %shard_map.115 = f32[4,128,1024]{2,1,0:T(8,128)S(1)} custom-call(s32[4]{0:T(128)S(1)} %iota_xor_fusion.place_ref, f32[1344,512]{1,0:T(8,128)S(1)} %bitcast.12, f32[1344,512]{1,0:T(8,128)S(1)} %copy-done.4, f32[640,128]{1,0:T(8,128)S(1)} %collective-permute-done.13.refs_2_, ...), custom_call_target="tpu_custom_call", output_to_operand_aliasing={{}: (5, {})} | custom-call | flops 1056964608 | bytes 5505024 | tf_op jit(solution)/shard_map/pallas_call | solution.py:83
  83.8 7.5 %reduce-scatter.3.cloned.1.call-done = f32[1,128,1024]{2,1,0:T(8,128)} async-done(((f32[4,128,1024]{2,1,0:T(8,128)}), f32[1,128,1024]{2,1,0:T(8,128)}) %reduce-scatter.3.cloned.1.call-update) | async-done | bytes 524304 | tf_op jit(solution)/shard_map/reduce_scatter | solution.py:554
  95.3 4.9 %collective-permute-done.8.refs_6_ = f32[128,512]{1,0:T(8,128)S(1)} collective-permute-done((f32[128,512]{1,0:T(8,128)S(1)}, f32[128,512]{1,0:T(8,128)S(1)}, u32[]{:S(2)}, u32[]{:S(2)}) %collective-permute-start.8) | collective-permute-done | bytes 262176 | tf_op jit(solution)/shard_map/ppermute | solution.py:507
  107.4 11.2 %shard_map.116 = (f32[4,2560,512]{2,1,0:T(8,128)}, f32[256,128]{1,0:T(8,128)}, f32[256,128]{1,0:T(8,128)}, f32[256,128]{1,0:T(8,128)}, f32[256,128]{1,0:T(8,128)...) custom-call(s32[1]{0:T(128)} %bitcast.tok_ref, s32[7]{0:T(128)} %fork_ref.3, s32[8]{0:T(128)} %live_ref.3, ...), custom_call_target="tpu_custom_call" | custom-call | flops 3221225472 | bytes 524288 | tf_op jit(solution)/shard_map/pallas_call | solution.py:465
  118.6 18.2 %reduce-scatter.5.cloned.1.call-done = f32[1,128,1024]{2,1,0:T(8,128)} async-done(((f32[4,128,1024]{2,1,0:T(8,128)}), f32[1,128,1024]{2,1,0:T(8,128)}) %reduce-scatter.5.cloned.1.call-update) | async-done | bytes 524304 | tf_op jit(solution)/shard_map/reduce_scatter | solution.py:554
  142.0 7.8 %collective-permute-done.17 = f32[256,128]{1,0:T(8,128)S(1)} collective-permute-done((f32[256,128]{1,0:T(8,128)}, f32[256,128]{1,0:T(8,128)S(1)}, u32[]{:S(2)}, u32[]{:S(2)}) %collective-permute-start.17) | collective-permute-done | bytes 131104 | tf_op jit(solution)/shard_map/ppermute | solution.py:507
  163.5 12.7 %shard_map.118 = (f32[1024,256]{1,0:T(8,128)}, f32[256,128]{1,0:T(8,128)}, f32[256,128]{1,0:T(8,128)}, f32[256,128]{1,0:T(8,128)}, f32[256,128]{1,0:T(8,128)}, /...) custom-call(s32[1]{0:T(128)} %bitcast.tok_ref, s32[7]{0:T(128)} %fork_ref.3, s32[8]{0:T(128)} %live_ref.3, ...), custom_call_target="tpu_custom_call" | custom-call | flops 6442450944 | bytes 524288 | tf_op jit(solution)/shard_map/pallas_call | solution.py:480
  176.2 5.5 %collective-permute-start.26 = (f32[256,128]{1,0:T(8,128)}, f32[256,128]{1,0:T(8,128)S(1)}, u32[]{:S(2)}, u32[]{:S(2)}) collective-permute-start(f32[256,128]{1,0:T(8,128)} %get-tuple-element.108), channel_id=1, source_target_pairs={{0,8},{4,12},{8,0},{12,4},{16,24},{20,28},{24,16},{28,20},{1,9},{5... | collective-permute-start | bytes 393224 | tf_op jit(solution)/shard_map/ppermute | solution.py:507
  181.8 10.4 %collective-permute-start.28 = (f32[256,128]{1,0:T(8,128)}, f32[256,128]{1,0:T(8,128)S(1)}, u32[]{:S(2)}, u32[]{:S(2)}) collective-permute-start(f32[256,128]{1,0:T(8,128)} %get-tuple-element.110), channel_id=1, source_target_pairs={{0,16},{4,20},{8,24},{12,28},{16,0},{20,4},{24,8},{28,12},{1,17},{... | collective-permute-start | bytes 393224 | tf_op jit(solution)/shard_map/ppermute | solution.py:507
  193.2 3.1 %collective-permute-start.27 = (f32[256,128]{1,0:T(8,128)S(1)}, f32[256,128]{1,0:T(8,128)S(1)}, u32[]{:S(2)}, u32[]{:S(2)}) collective-permute-start(f32[256,128]{1,0:T(8,128)S(1)} %add.64), channel_id=1, source_target_pairs={{0,16},{4,20},{8,24},{12,28},{16,0},{20,4},{24,8},{28,12},{1,17},{... | collective-permute-start | bytes 393224 | tf_op jit(solution)/shard_map/ppermute | solution.py:507
  212.2 2.9 shard_map.122
  218.7 4.5 %shard_map.121 = (f32[672,128]{1,0:T(8,128)S(1)}, f32[672,128]{1,0:T(8,128)S(1)}, f32[672,128]{1,0:T(8,128)S(1)}, f32[672,128]{1,0:T(8,128)S(1)}) custom-call(s32[4]{0:T(128)S(1)} %iota_xor_fusion.place_ref, f32[1344,512]{1,0:T(8,128)S(1)} %bitcast.14, f32[1344,512]{1,0:T(8,128)S(1)} %copy-done.5, f32[4,1024,128]{2,1,0:T(8,128)S(1)} %bitcast.24, ...), custom_call_target="tpu_custom_call" | custom-call | flops 2113929216 | bytes 5505024 | tf_op jit(solution)/shard_map/pallas_call | solution.py:141
  236.6 6.9 %collective-permute-done.36 = f32[672,128]{1,0:T(8,128)S(1)} collective-permute-done((f32[672,128]{1,0:T(8,128)S(1)}, f32[672,128]{1,0:T(8,128)S(1)}, u32[]{:S(2)}, u32[]{:S(2)}) %collective-permute-start.36) | collective-permute-done | bytes 344096 | tf_op jit(solution)/shard_map/ppermute | solution.py:507
  244.4 9.7 %all-gather.5.cloned.1.call-done = f32[4096,128]{1,0:T(8,128)} async-done(((f32[1024,128]{1,0:T(8,128)}), f32[4096,128]{1,0:T(8,128)}) %all-gather.5.cloned.1.call-update) | async-done | bytes 2097168 | tf_op jit(solution)/shard_map/all_gather | solution.py:557
  263.3 4.5 %shard_map.124 = (f32[672,128]{1,0:T(8,128)S(1)}, f32[672,128]{1,0:T(8,128)S(1)}, f32[672,128]{1,0:T(8,128)S(1)}, f32[672,128]{1,0:T(8,128)S(1)}) custom-call(s32[4]{0:T(128)S(1)} %iota_xor_fusion.place_ref, f32[1344,512]{1,0:T(8,128)S(1)} %bitcast.17, f32[1344,512]{1,0:T(8,128)S(1)} %copy-done.6, f32[4,1024,128]{2,1,0:T(8,128)S(1)} %bitcast.20, ...), custom_call_target="tpu_custom_call" | custom-call | flops 2113929216 | bytes 5505024 | tf_op jit(solution)/shard_map/pallas_call | solution.py:141
  278.9 3.2 %collective-permute-done.42 = f32[672,128]{1,0:T(8,128)S(1)} collective-permute-done((f32[672,128]{1,0:T(8,128)S(1)}, f32[672,128]{1,0:T(8,128)S(1)}, u32[]{:S(2)}, u32[]{:S(2)}) %collective-permute-start.42) | collective-permute-done | bytes 344096 | tf_op jit(solution)/shard_map/ppermute | solution.py:507
  282.2 4.3 %collective-permute-done.45 = f32[672,128]{1,0:T(8,128)S(1)} collective-permute-done((f32[672,128]{1,0:T(8,128)S(1)}, f32[672,128]{1,0:T(8,128)S(1)}, u32[]{:S(2)}, u32[]{:S(2)}) %collective-permute-start.45) | collective-permute-done | bytes 344096 | tf_op jit(solution)/shard_map/ppermute | solution.py:507
  (185 shorter events, 115.0 us)
Async XLA Ops:
  7.2 84.1 %reduce-scatter.3.cloned.1.call-start = ((), (), s32[]{:S(2)}) async-start(), calls=%async_computation.2 | async-start | bytes 2621440 | tf_op jit(solution)/shard_map/reduce_scatter | solution.py:554
  7.7 18.9 %collective-permute-start.3 = (f32[1344,128]{1,0:T(8,128)}, f32[1344,128]{1,0:T(8,128)}, u32[]{:S(2)}, u32[]{:S(2)}) collective-permute-start(f32[1344,128]{1,0:T(8,128)} %refs_2_.2), channel_id=1, source_target_pairs={{0,8},{4,12},{8,0},{12,4},{16,24},{20,28},{24,16},{28,20},{1,9},{5... | collective-permute-start | bytes 2064392 | tf_op jit(solution)/shard_map/ppermute | solution.py:507
  10.3 17.7 %collective-permute-start.4 = (f32[1344,128]{1,0:T(8,128)}, f32[1344,128]{1,0:T(8,128)S(1)}, u32[]{:S(2)}, u32[]{:S(2)}) collective-permute-start(f32[1344,128]{1,0:T(8,128)} %refs_2_.2), channel_id=1, source_target_pairs={{0,16},{4,20},{8,24},{12,28},{16,0},{20,4},{24,8},{28,12},{1,17},{... | collective-permute-start | bytes 2064392 | tf_op jit(solution)/shard_map/ppermute | solution.py:507
  28.0 11.4 %collective-permute-start.6 = (f32[704,128]{1,0:T(8,128)S(1)}, f32[704,128]{1,0:T(8,128)S(1)}, u32[]{:S(2)}, u32[]{:S(2)}) collective-permute-start(f32[704,128]{1,0:T(8,128)S(1)} %slice.55), channel_id=1, source_target_pairs={{0,8},{4,12},{8,0},{12,4},{16,24},{20,28},{24,16},{28,20},{1,9},{5... | collective-permute-start | bytes 1081352 | tf_op jit(solution)/shard_map/ppermute | solution.py:507
  46.9 89.9 %reduce-scatter.5.cloned.1.call-start = ((), (), s32[]{:S(2)}) async-start(), calls=%async_computation.3 | async-start | bytes 2621440 | tf_op jit(solution)/shard_map/reduce_scatter | solution.py:554
  48.0 16.3 %collective-permute-start.11 = (f32[1344,128]{1,0:T(8,128)S(1)}, f32[1344,128]{1,0:T(8,128)S(1)}, u32[]{:S(2)}, u32[]{:S(2)}) collective-permute-start(f32[1344,128]{1,0:T(8,128)S(1)} %copy-done.12), channel_id=1, source_target_pairs={{0,8},{4,12},{8,0},{12,4},{16,24},{20,28},{24,16},{28,20},{1,9},{5... | collective-permute-start | bytes 2064392 | tf_op jit(solution)/shard_map/ppermute | solution.py:507
  49.5 15.8 %collective-permute-start.12 = (f32[1344,128]{1,0:T(8,128)S(1)}, f32[1344,128]{1,0:T(8,128)S(1)}, u32[]{:S(2)}, u32[]{:S(2)}) collective-permute-start(f32[1344,128]{1,0:T(8,128)S(1)} %copy-done.12), channel_id=1, source_target_pairs={{0,16},{4,20},{8,24},{12,28},{16,0},{20,4},{24,8},{28,12},{1,17},{... | collective-permute-start | bytes 2064392 | tf_op jit(solution)/shard_map/ppermute | solution.py:507
  79.6 129.2 %all-gather.7.cloned.1.call-start = ((), (), s32[]{:S(2)}) async-start(), calls=%async_computation.5 | async-start | bytes 2621440 | tf_op jit(solution)/shard_map/all_gather | solution.py:557
  82.2 21.1 %collective-permute-start = (f32[512,256]{1,0:T(8,128)}, f32[512,256]{1,0:T(8,128)S(1)}, u32[]{:S(2)}, u32[]{:S(2)}) collective-permute-start(f32[512,256]{1,0:T(8,128)} %get-tuple-element.141), channel_id=1, source_target_pairs={{0,4},{4,0},{8,12},{12,8},{16,20},{20,16},{24,28},{28,24},{1,5},{5... | collective-permute-start | bytes 1572872 | tf_op jit(solution)/shard_map/ppermute | solution.py:507
  83.2 20.1 %collective-permute-start.1 = (f32[512,256]{1,0:T(8,128)}, f32[512,256]{1,0:T(8,128)}, u32[]{:S(2)}, u32[]{:S(2)}) collective-permute-start(f32[512,256]{1,0:T(8,128)} %get-tuple-element.139), channel_id=1, source_target_pairs={{0,4},{4,0},{8,12},{12,8},{16,20},{20,16},{24,28},{28,24},{1,5},{5... | collective-permute-start | bytes 1572872 | tf_op jit(solution)/shard_map/ppermute | solution.py:507
  137.9 12.0 %collective-permute-start.16 = (f32[128,512]{1,0:T(8,128)S(1)}, f32[128,512]{1,0:T(8,128)S(1)}, u32[]{:S(2)}, u32[]{:S(2)}) collective-permute-start(f32[128,512]{1,0:T(8,128)S(1)} %pad_maximum_fusion.3), channel_id=1, source_target_pairs={{0,16},{4,20},{8,24},{12,28},{16,0},{20,4},{24,8},{28,12},{1,17},{... | collective-permute-start | bytes 786440 | tf_op jit(solution)/shard_map/ppermute | solution.py:507
  163.5 90.6 %all-gather.5.cloned.1.call-start = ((), (), s32[]{:S(2)}) async-start(), calls=%async_computation.4 | async-start | bytes 2621440 | tf_op jit(solution)/shard_map/all_gather | solution.py:557
  176.2 16.1 %collective-permute-start.26 = (f32[256,128]{1,0:T(8,128)}, f32[256,128]{1,0:T(8,128)S(1)}, u32[]{:S(2)}, u32[]{:S(2)}) collective-permute-start(f32[256,128]{1,0:T(8,128)} %get-tuple-element.108), channel_id=1, source_target_pairs={{0,8},{4,12},{8,0},{12,4},{16,24},{20,28},{24,16},{28,20},{1,9},{5... | collective-permute-start | bytes 393224 | tf_op jit(solution)/shard_map/ppermute | solution.py:507
  181.8 14.7 %collective-permute-start.28 = (f32[256,128]{1,0:T(8,128)}, f32[256,128]{1,0:T(8,128)S(1)}, u32[]{:S(2)}, u32[]{:S(2)}) collective-permute-start(f32[256,128]{1,0:T(8,128)} %get-tuple-element.110), channel_id=1, source_target_pairs={{0,16},{4,20},{8,24},{12,28},{16,0},{20,4},{24,8},{28,12},{1,17},{... | collective-permute-start | bytes 393224 | tf_op jit(solution)/shard_map/ppermute | solution.py:507
  207.5 20.0 %collective-permute-start.37 = (f32[512,256]{1,0:T(8,128)}, f32[512,256]{1,0:T(8,128)}, u32[]{:S(2)}, u32[]{:S(2)}) collective-permute-start(f32[512,256]{1,0:T(8,128)} %get-tuple-element.138), channel_id=1, source_target_pairs={{0,4},{4,0},{8,12},{12,8},{16,20},{20,16},{24,28},{28,24},{1,5},{5... | collective-permute-start | bytes 1572872 | tf_op jit(solution)/shard_map/ppermute | solution.py:507
  218.1 16.5 %collective-permute-start.38 = (f32[512,128]{1,0:T(8,128)S(1)}, f32[512,128]{1,0:T(8,128)S(1)}, u32[]{:S(2)}, u32[]{:S(2)}) collective-permute-start(f32[512,128]{1,0:T(8,128)S(1)} %get-tuple-element.146), channel_id=1, source_target_pairs={{0,4},{4,0},{8,12},{12,8},{16,20},{20,16},{24,28},{28,24},{1,5},{5... | collective-permute-start | bytes 786440 | tf_op jit(solution)/shard_map/ppermute | solution.py:507
  218.2 14.7 %collective-permute-start.34 = (f32[672,128]{1,0:T(8,128)S(1)}, f32[672,128]{1,0:T(8,128)S(1)}, u32[]{:S(2)}, u32[]{:S(2)}) collective-permute-start(f32[672,128]{1,0:T(8,128)S(1)} %get-tuple-element.119), channel_id=1, source_target_pairs={{0,16},{4,20},{8,24},{12,28},{16,0},{20,4},{24,8},{28,12},{1,17},{... | collective-permute-start | bytes 1032200 | tf_op jit(solution)/shard_map/ppermute | solution.py:507
  223.2 12.2 %collective-permute-start.31 = (f32[672,128]{1,0:T(8,128)S(1)}, f32[672,128]{1,0:T(8,128)S(1)}, u32[]{:S(2)}, u32[]{:S(2)}) collective-permute-start(f32[672,128]{1,0:T(8,128)S(1)} %get-tuple-element.114), channel_id=1, source_target_pairs={{0,8},{4,12},{8,0},{12,4},{16,24},{20,28},{24,16},{28,20},{1,9},{5... | collective-permute-start | bytes 1032200 | tf_op jit(solution)/shard_map/ppermute | solution.py:507
  225.4 11.2 %collective-permute-start.33 = (f32[672,128]{1,0:T(8,128)S(1)}, f32[672,128]{1,0:T(8,128)S(1)}, u32[]{:S(2)}, u32[]{:S(2)}) collective-permute-start(f32[672,128]{1,0:T(8,128)S(1)} %add.67), channel_id=1, source_target_pairs={{0,16},{4,20},{8,24},{12,28},{16,0},{20,4},{24,8},{28,12},{1,17},{... | collective-permute-start | bytes 1032200 | tf_op jit(solution)/shard_map/ppermute | solution.py:507
  229.9 13.5 %collective-permute-start.36 = (f32[672,128]{1,0:T(8,128)S(1)}, f32[672,128]{1,0:T(8,128)S(1)}, u32[]{:S(2)}, u32[]{:S(2)}) collective-permute-start(f32[672,128]{1,0:T(8,128)S(1)} %get-tuple-element.120), channel_id=1, source_target_pairs={{0,16},{4,20},{8,24},{12,28},{16,0},{20,4},{24,8},{28,12},{1,17},{... | collective-permute-start | bytes 1032200 | tf_op jit(solution)/shard_map/ppermute | solution.py:507
  261.9 11.4 %collective-permute-start.43 = (f32[672,128]{1,0:T(8,128)S(1)}, f32[672,128]{1,0:T(8,128)S(1)}, u32[]{:S(2)}, u32[]{:S(2)}) collective-permute-start(f32[672,128]{1,0:T(8,128)S(1)} %get-tuple-element.134), channel_id=1, source_target_pairs={{0,16},{4,20},{8,24},{12,28},{16,0},{20,4},{24,8},{28,12},{1,17},{... | collective-permute-start | bytes 1032200 | tf_op jit(solution)/shard_map/ppermute | solution.py:507
  270.5 11.7 %collective-permute-start.42 = (f32[672,128]{1,0:T(8,128)S(1)}, f32[672,128]{1,0:T(8,128)S(1)}, u32[]{:S(2)}, u32[]{:S(2)}) collective-permute-start(f32[672,128]{1,0:T(8,128)S(1)} %add.73), channel_id=1, source_target_pairs={{0,16},{4,20},{8,24},{12,28},{16,0},{20,4},{24,8},{28,12},{1,17},{... | collective-permute-start | bytes 1032200 | tf_op jit(solution)/shard_map/ppermute | solution.py:507
  273.1 13.3 %collective-permute-start.45 = (f32[672,128]{1,0:T(8,128)S(1)}, f32[672,128]{1,0:T(8,128)S(1)}, u32[]{:S(2)}, u32[]{:S(2)}) collective-permute-start(f32[672,128]{1,0:T(8,128)S(1)} %get-tuple-element.135), channel_id=1, source_target_pairs={{0,16},{4,20},{8,24},{12,28},{16,0},{20,4},{24,8},{28,12},{1,17},{... | collective-permute-start | bytes 1032200 | tf_op jit(solution)/shard_map/ppermute | solution.py:507
  273.3 13.2 %collective-permute-start.44 = (f32[672,128]{1,0:T(8,128)S(1)}, f32[672,128]{1,0:T(8,128)S(1)}, u32[]{:S(2)}, u32[]{:S(2)}) collective-permute-start(f32[672,128]{1,0:T(8,128)S(1)} %add.75), channel_id=1, source_target_pairs={{0,8},{4,12},{8,0},{12,4},{16,24},{20,28},{24,16},{28,20},{1,9},{5... | collective-permute-start | bytes 1032200 | tf_op jit(solution)/shard_map/ppermute | solution.py:507
  (53 other events, 371.3 us)
Sparse Core Ops, SparseCore 0:
  47.0 44.1 reduce-scatter.2
  93.6 43.1 reduce-scatter.4
  163.6 43.6 all-gather.6
  209.3 44.7 all-gather.4

commit v4 on v3

--- a/solution.py
+++ b/solution.py
@@ -42,12 +42,31 @@
 smem_spec = pl.BlockSpec(memory_space=pltpu.SMEM)
 
 
-def project_body(place_ref, *refs, row_inputs, pieces, parts, steps_each):
+def halve_body(x_ref, out_ref):
+    out_ref[...] = pair_cat(x_ref[...], 1)
+
+
+def halve(x):
+    depth, rows = x.shape
+    block = depth // 4
+    return pl.pallas_call(
+        halve_body,
+        grid=(4,),
+        in_specs=[pl.BlockSpec((block, rows), lambda step: (step, 0))],
+        out_specs=pl.BlockSpec((block, 2 * rows), lambda step: (step, 0)),
+        out_shape=jax.ShapeDtypeStruct((depth, 2 * rows), bf16),
+        compiler_params=pltpu.CompilerParams(vmem_limit_bytes=12 * MIB),
+        cost_estimate=pl.CostEstimate(flops=4 * x.size, bytes_accessed=8 * x.size, transcendentals=0),
+    )(x)
+
+
+def project_body(place_ref, *refs, row_inputs, pieces, outs):
     x_refs = refs[:row_inputs]
     w_refs = refs[row_inputs : row_inputs + len(pieces)]
-    out_ref, pair_ref, x_ref = refs[-3:]
+    out_refs, pair_ref = refs[-1 - outs : -1], refs[-1]
     step, part_step = pl.program_id(0), pl.program_id(1)
-    columns = x_refs[0].shape[1]
+    columns = x_refs[0].shape[1] // 2
+    width = columns // outs
 
     @pl.when((step == 0) & (part_step == 0))
     def _():
@@ -59,52 +78,46 @@
 
     for source in range(row_inputs):
 
-        @pl.when((step // steps_each == source) & (part_step == 0))
+        @pl.when(step == source)
         def _():
-            high, low = split(x_refs[source][...])
-            x_ref[:, :columns] = high
-            x_ref[:, columns:] = low
-
-    total = dot(pair_ref[part_step], x_ref[...])
-    total = total[:, :columns] + total[:, columns:]
-    out_ref[0] = total[:HEAD_DIM] + total[HEAD_DIM:]
-
-
-def project(place, slots, xs, pieces, ws, before=None):
+            total = dot(pair_ref[part_step], x_refs[source][...])
+            total = total[:, :columns] + total[:, columns:]
+            total = total[:HEAD_DIM] + total[HEAD_DIM:]
+            for index, out_ref in enumerate(out_refs):
+                out_ref[0] = total[:, index * width : (index + 1) * width]
+
+
+def project(place, slots, xs, pieces, ws, outs, before=()):
     depth, rows = xs[0].shape
-    block = 256
-    steps_each = rows // block
+    rows = rows // 2
     first = slots[0]
-
-    def x_map(source):
-        return lambda step, part, place_ref: (0, jnp.clip(step - source * steps_each, 0, steps_each - 1))
-
-    extra = [] if before is None else [before]
+    width = rows // outs
+    inputs = 1 + len(xs) + len(ws)
     return pl.pallas_call(
-        functools.partial(project_body, row_inputs=len(xs), pieces=pieces, parts=len(slots), steps_each=steps_each),
+        functools.partial(project_body, row_inputs=len(xs), pieces=pieces, outs=outs),
         grid_spec=pltpu.PrefetchScalarGridSpec(
             num_scalar_prefetch=1,
-            grid=(steps_each * len(xs), len(slots)),
-            in_specs=[pl.BlockSpec((depth, block), x_map(source)) for source in range(len(xs))]
+            grid=(len(xs), len(slots)),
+            in_specs=[whole_spec(x) for x in xs]
             + [whole_spec(w) for w in ws]
-            + [pl.BlockSpec(memory_space=pl.ANY)] * len(extra),
-            out_specs=pl.BlockSpec((1, HEAD_DIM, block), lambda step, part, place_ref: (place_ref[first + part], 0, step)),
-            scratch_shapes=[pltpu.VMEM((len(slots), 2 * HEAD_DIM, depth), bf16), pltpu.VMEM((depth, 2 * block), bf16)],
+            + [pl.BlockSpec(memory_space=pl.ANY)] * len(before),
+            out_specs=[pl.BlockSpec((1, HEAD_DIM, width), lambda step, part, place_ref: (place_ref[first + part], 0, step))] * outs,
+            scratch_shapes=[pltpu.VMEM((len(slots), 2 * HEAD_DIM, depth), bf16)],
         ),
-        out_shape=jax.ShapeDtypeStruct((place.shape[0], HEAD_DIM, rows * len(xs)), f32),
-        input_output_aliases={1 + len(xs) + len(ws): 0} if extra else {},
+        out_shape=[jax.ShapeDtypeStruct((place.shape[0], HEAD_DIM, width * len(xs)), f32)] * outs,
+        input_output_aliases={inputs + index: index for index in range(len(before))},
         compiler_params=pltpu.CompilerParams(vmem_limit_bytes=24 * MIB),
         cost_estimate=pl.CostEstimate(
             flops=6 * rows * len(xs) * depth * len(slots) * HEAD_DIM, bytes_accessed=4 * rows * len(xs) * depth, transcendentals=0
         ),
-    )(place, *xs, *ws, *extra)
+    )(place, *xs, *ws, *before)
 
 
 def weight_grad_body(place_ref, *refs, row_inputs, parts):
     x_refs = refs[:row_inputs]
     g_refs = refs[row_inputs : row_inputs + parts]
     out_refs, pair_ref = refs[row_inputs + parts : -1], refs[-1]
-    rows = x_refs[0].shape[1]
+    rows = x_refs[0].shape[1] // 2
     step, half = pl.program_id(0), pl.num_programs(0) // 2
 
     @pl.when(step == 0)
@@ -114,9 +127,8 @@
 
     total = 0.0
     for source in range(row_inputs):
-        high, low = split(x_refs[source][...])
         pair = pair_ref[source * rows : (source + 1) * rows]
-        total += dot(high, pair) + dot(low, pair)
+        total += dot(x_refs[source][:, :rows], pair) + dot(x_refs[source][:, rows:], pair)
     for part in range(parts):
         value = total[:, 2 * part * HEAD_DIM : (2 * part + 1) * HEAD_DIM] + total[:, (2 * part + 1) * HEAD_DIM : 2 * (part + 1) * HEAD_DIM]
         for piece in range(2):
@@ -128,6 +140,7 @@
 
 def weight_grad(place, slots, xs, grads):
     depth, rows = xs[0].shape
+    rows = rows // 2
     parts = len(slots)
     steps = 4
     half = steps // 2
@@ -143,7 +156,7 @@
         grid_spec=pltpu.PrefetchScalarGridSpec(
             num_scalar_prefetch=1,
             grid=(steps,),
-            in_specs=[pl.BlockSpec((block, rows), lambda step, place_ref: (step, 0))] * len(xs)
+            in_specs=[pl.BlockSpec((block, 2 * rows), lambda step, place_ref: (step, 0))] * len(xs)
             + [pl.BlockSpec((1, *grads.shape[1:]), g_map(slot)) for slot in slots],
             out_specs=[head, tail] * parts,
             scratch_shapes=[pltpu.VMEM((rows * len(xs), 2 * parts * HEAD_DIM), bf16)],
@@ -156,17 +169,16 @@
     )(place, *xs, *[grads] * parts)
 
 
-def combine_body(own_ref, *refs, starts):
+def combine_body(own_ref, *refs, plan):
     out_ref = refs[-1]
     out_ref[...] = own_ref[...]
-    for index, start in enumerate(starts):
-        first, second = refs[2 * index], refs[2 * index + 1]
-        out_ref[start : start + first.shape[0], :] += first[...] + second[...]
-
-
-def combine(own, starts, arrivals):
+    for index, source, target, count in plan:
+        out_ref[target : target + count, :] += refs[index][source : source + count, :]
+
+
+def combine(own, arrivals, plan):
     return pl.pallas_call(
-        functools.partial(combine_body, starts=starts),
+        functools.partial(combine_body, plan=plan),
         out_shape=jax.ShapeDtypeStruct(own.shape, f32),
         compiler_params=pltpu.CompilerParams(vmem_limit_bytes=24 * MIB),
         cost_estimate=pl.CostEstimate(flops=own.size, bytes_accessed=12 * own.size, transcendentals=0),
@@ -362,8 +374,9 @@
     lanes = group * SPAN
     q_refs, g_refs = refs[:nb], refs[nb : 2 * nb]
     at = 2 * nb
-    key_refs, value_refs = refs[at : at + sources], refs[at + sources : at + 2 * sources]
-    at += 2 * sources
+    value_sources = conf["value_sources"]
+    key_refs, value_refs = refs[at : at + sources], refs[at + sources : at + sources + value_sources]
+    at += sources + value_sources
     prob_ref = refs[at]
     dq_ref = refs[at + 1]
     out_refs = refs[at + 2 : at + 2 + outs]
@@ -389,7 +402,7 @@
         list_ancestors(fork_ref, offset_ref, limit_ref, many_ref, tok, nb, conf["rows"] // TILE, conf["paired"])
         start_in(step)
         stage_rows(keys_ref, key_refs, layout)
-        stage_rows(values_ref, value_refs, layout)
+        stage_rows(values_ref, value_refs, conf["value_layout"])
         sum_ref[...] = jnp.zeros_like(sum_ref)
 
     @pl.when(step < nb * halves - 1)
@@ -440,15 +453,23 @@
         write_rows(sum_ref, out_refs, layout, conf["sums"])
 
 
-def attention_calls(scalars, qs, gs, layout, sum_rows, paired, owners, parts):
+def attention_calls(scalars, qs, gs, layout, value_layout, key_sum_rows, value_sum_rows, paired, owners):
     rows, width = qs[0].shape
     nb, group, halves = len(qs), width // HEAD_DIM, rows // SPAN
     lanes = group * SPAN
     steps = nb * halves
-    conf = dict(nb=nb, group=group, rows=rows, owners=owners, layout=layout, paired=paired, sources=1 + parts, sums=sum_rows, outs=len(sum_rows) + 1)
+    conf = dict(nb=nb, group=group, rows=rows, owners=owners, layout=layout, value_layout=value_layout, paired=paired)
+    conf["sources"] = 1 + max(entry[0] for entry in layout)
+    conf["value_sources"] = 1 + max(entry[0] for entry in value_layout)
     table_rows = owners * SPAN + nb * rows
     slots = (owners + halves) * SPAN
-    sums = [jax.ShapeDtypeStruct((count, HEAD_DIM), f32) for _, _, count in sum_rows] + [jax.ShapeDtypeStruct((nb * rows, HEAD_DIM), f32)]
+
+    def sums_of(sum_rows):
+        shapes = [jax.ShapeDtypeStruct((count, HEAD_DIM), f32) for _, _, count in sum_rows]
+        return shapes + [jax.ShapeDtypeStruct((nb * rows, HEAD_DIM), f32)], dict(conf, sums=sum_rows, outs=len(sum_rows) + 1)
+
+    key_sums, key_conf = sums_of(key_sum_rows)
+    value_sums, value_conf = sums_of(value_sum_rows)
     probs = jax.ShapeDtypeStruct((steps, slots, lanes), f32)
     probs_spec = pl.BlockSpec(memory_space=pl.ANY)
     two_squares = pltpu.VMEM((2, slots, lanes), f32)
@@ -463,11 +484,11 @@
 
     def soft(keys):
         return pl.pallas_call(
-            functools.partial(soft_body, conf=conf),
+            functools.partial(soft_body, conf=value_conf),
             grid=(steps,),
             in_specs=[smem_spec] * 3 + [whole_spec(a) for a in (*qs, *gs, *keys)],
-            out_specs=[probs_spec] + [whole_spec(a) for a in sums],
-            out_shape=[probs] + sums,
+            out_specs=[probs_spec] + [whole_spec(a) for a in value_sums],
+            out_shape=[probs] + value_sums,
             scratch_shapes=[table, table_sum, two_squares, columns, pltpu.VMEM((lanes, 2 * HEAD_DIM), bf16)]
             + lists
             + [sems],
@@ -478,11 +499,11 @@
     def grad(keys, values, probs_in):
         dq = jax.ShapeDtypeStruct((nb * rows, width), f32)
         return pl.pallas_call(
-            functools.partial(grad_body, conf=conf),
+            functools.partial(grad_body, conf=key_conf),
             grid=(steps,),
             in_specs=[smem_spec] * 3 + [whole_spec(a) for a in (*qs, *gs, *keys, *values)] + [probs_spec],
-            out_specs=[pl.BlockSpec((SPAN, width), lambda step: (step, 0))] + [whole_spec(a) for a in sums],
-            out_shape=[dq] + sums,
+            out_specs=[pl.BlockSpec((SPAN, width), lambda step: (step, 0))] + [whole_spec(a) for a in key_sums],
+            out_shape=[dq] + key_sums,
             scratch_shapes=[
                 table,
                 table,
@@ -542,13 +563,13 @@
     def partners(array):
         return flip(lax.dynamic_slice_in_dim(array, (1 - core) * width, width, 1), 1)
 
-    def project_all(w):
-        partial = project(place, (0,), xs, ((0, 0),), [w])
+    def project_all(w, outs):
+        partial = project(place, (0,), xs, ((0, 0),), [w], outs)
         across, down = flip(w, 2), flip(w, 4)
-        across, down, partial = together(across, down, partial)
+        across, down, *partial = together(across, down, *partial)
         head, tail = flip(across[:cut], 4), flip(down[cut:], 2)
-        partial = project(place, (1, 2), xs, ((0, 0), (1, 0)), [across, down], partial)
-        return project(place, (3,), xs, ((0, 0), (0, cut)), [head, tail], partial)
+        partial = project(place, (1, 2), xs, ((0, 0), (1, 0)), [across, down], outs, partial)
+        return project(place, (3,), xs, ((0, 0), (0, cut)), [head, tail], outs, partial)
 
     def sum_heads(partial):
         return lax.psum_scatter(partial, "head", scatter_dimension=0, tiled=True)[0]
@@ -561,9 +582,14 @@
 
     def returned(across_head, across_tail, down_head, down_tail, corner_head, corner_tail, own):
         arrivals = scatter_square((across_head, across_tail), (down_head, down_tail), (corner_head, corner_tail))
-        return combine(own, (0, rows), arrivals)
-
-    def weight(every):
+        plan = tuple((index, 0, rows * (index // 2), SPAN) for index in range(4))
+        return combine(own, arrivals, plan)
+
+    def returned_at_once(across, down, corner, own):
+        plan = tuple((index, slot * SPAN, slot * rows, SPAN) for index in range(3) for slot in range(2))
+        return combine(own, [flip(across, 2), flip(down, 4), flip(corner, 6)], plan)
+
+    def weight(every, xs):
         corner = weight_grad(place, (3,), xs, every)
         across_head, across_tail, down_head, down_tail = weight_grad(place, (1, 2), xs, every)
         kept = weight_grad(place, (0,), xs, every)
@@ -579,11 +605,12 @@
         return jnp.where(core == 0, jnp.concatenate([kept, received], axis=1), jnp.concatenate([received, kept], axis=1))
 
     hidden = hidden.T
-    xs = [hidden, flip(hidden, 1)]
+    both = [hidden, flip(hidden, 1)]
+    xs = [halve(x) for x in both]
     qs = [mine(queries), partners(queries)]
     gs = [mine(out_grad), partners(out_grad)]
-    keys = sum_heads(project_all(w_key))
-    values = sum_heads(project_all(w_value))
+    keys = sum_heads(project_all(w_key, 1)[0])
+    leading, trailing = map(sum_heads, project_all(w_value, 2))
 
     base = owners * SPAN
     layout = (
@@ -595,32 +622,36 @@
         (3, 0, 6 * SPAN, SPAN),
         (4, 0, 7 * SPAN, SPAN),
     )
-    sums = tuple((0, (2 + index) * SPAN, SPAN) for index in range(6))
-    soft, grad = attention_calls(scalars, qs, gs, layout, sums, True, owners, 4)
+    value_layout = (
+        (0, 0, base, SPAN),
+        (0, SPAN, base + rows, SPAN),
+        (0, 0, 0, 2 * SPAN),
+        (1, 0, base + SPAN, SPAN),
+        (1, SPAN, base + rows + SPAN, SPAN),
+    ) + tuple((index + 1, *rest) for index, *rest in layout[3:])
+    key_sum_rows = tuple((0, (2 + index) * SPAN, SPAN) for index in range(6))
+    value_sum_rows = tuple((0, 2 * (1 + index) * SPAN, 2 * SPAN) for index in range(3))
+    soft, grad = attention_calls(scalars, qs, gs, layout, value_layout, key_sum_rows, value_sum_rows, True, owners)
 
     key_parts = [keys, *gather_square(lead(keys), SPAN, 1)]
     probs, *value_sums = soft(key_parts)
-    values, *value_sums = together(values, *value_sums)
-    across_head, across_tail, down_head, down_tail, corner_head, corner_tail, own = value_sums
-    leading = lead(values)
-    value_across, value_down = flip(leading, 2), flip(leading, 4)
-    from_across, from_down = flip(corner_head, 2), flip(corner_tail, 4)
-    across_head, down_tail = flip(across_head, 2), flip(down_tail, 4)
-    value_across, value_down, from_across, from_down = together(value_across, value_down, from_across, from_down)
-    value_parts = [values, value_across, value_down, flip(value_across[:, :SPAN], 4), flip(value_down[:, SPAN:], 2)]
-    across_tail, down_head = flip(across_tail + from_down, 2), flip(down_head + from_across, 4)
-    *value_parts, across_tail, down_head = together(*value_parts, across_tail, down_head)
-    value_grads = combine(own, (0, rows), (across_head, down_head, across_tail, down_tail))
+    value_parts = list(together(leading, *value_sums))[:1]
+    value_parts += gather_square(value_parts[0], SPAN, 1)
+    value_grads = returned_at_once(*value_sums)
+    probs, value_grads, *value_parts = together(probs, value_grads, *value_parts)
+    trailing, value_grads = together(trailing, value_grads)
     every_value = all_heads(value_grads)
-    probs, value_grads = together(probs, value_grads)
+    value_parts = [value_parts[0], trailing, *value_parts[1:]]
     grad_query, *key_sums = grad(key_parts, value_parts, probs)
     key_grads = returned(*key_sums)
     every_key = all_heads(key_grads)
     every_value, key_grads = together(every_value, key_grads)
-    grad_w_value = finish(*weight(every_value))
+    grad_w_value = finish(*weight(every_value, xs))
     grad_query, grad_key, grad_value = home(grad_query), home(key_grads), home(value_grads)
-    every_key, grad_w_value, grad_query, grad_key, grad_value = together(every_key, grad_w_value, grad_query, grad_key, grad_value)
-    grad_w_key = finish(*weight(every_key))
+    *both, grad_w_value = together(*both, grad_w_value)
+    late = [halve(x) for x in both]
+    every_key, grad_w_value, grad_query, grad_key, grad_value, *late = together(every_key, grad_w_value, grad_query, grad_key, grad_value, *late)
+    grad_w_key = finish(*weight(every_key, late))
     return grad_query, grad_key, grad_value, grad_w_key, grad_w_value
 
 
@@ -637,7 +668,7 @@
     keys, values = projected(w_key), projected(w_value)
     layout = ((0, 0, owners * SPAN, hidden.shape[0]), (1, 0, 0, owners * SPAN))
     sums = ((0, 0, owners * SPAN),)
-    soft, grad = attention_calls(scalars, [queries], [out_grad], layout, sums, False, owners, 1)
+    soft, grad = attention_calls(scalars, [queries], [out_grad], layout, layout, sums, sums, False, owners)
 
     def parts(array):
         return [array, lax.all_gather(array[:, :SPAN], "tok", axis=1, tiled=True)]

time: 295 us -> 283 us (0.959)
  waiting for transfers between devices: 95.5 us -> 73.5 us
  starting transfers between devices: 66.2 us -> 82 us
  Pallas kernels: 78.9 us -> 75 us
    ppermute x46 -> x43, starting transfers between devices: 65.8 us -> 81.6 us  [flip(): lax.ppermute(array, 'tok', [(index, index ^ mask) for index in range(coun...]
    reduce_scatter x2 -> x3, waiting for transfers between devices: 25.6 us -> 12.5 us  [sum_heads(): return lax.psum_scatter(partial, 'head', scatter_dimension=0, tiled=True)[0]]
    pallas_call x6, Pallas kernels: 32.7 us -> 23.1 us  [project(): pl.pallas_call(functools.partial(project_body, row_inputs=len(xs), pieces...]
    pallas_call x4 -> x8, Pallas kernels: 25.6 us -> 31.6 us  [the longest x1 12.7 us: grad(): pl.pallas_call(functools.partial(grad_body, conf=key_conf), grid=(steps,)...]
    all_gather x2, waiting for transfers between devices: 9.66 us -> 3.87 us  [all_heads(): return lax.all_gather(grads, 'head', axis=0, tiled=False)]
    ppermute x46 -> x43, waiting for transfers between devices: 60.1 us -> 56.4 us  [flip(): lax.ppermute(array, 'tok', [(index, index ^ mask) for index in range(coun...]
    unnamed x54 -> x50, local copies, waits for them, and re-layouts: 18.6 us -> 18.4 us
  transfers between devices with their start and end apart: 50 -> 48, of which waited for: 25 -> 22; matrix products, arithmetic and copies ran while one was open for 6% -> 6% of each run, Pallas kernels for 24% -> 25%
where the time goes in v4:
time: 283 us; the launch traced here: 282 us
  starting transfers between devices  82 us (29%)
  Pallas kernels  75 us (27%)
  waiting for transfers between devices  73.5 us (26%)
  local copies, waits for them, and re-layouts  29.4 us (10%)
  between operations  14.2 us (5%)
  other arithmetic  8.06 us (3%)
    ppermute x43, starting transfers between devices, flip(): lax.ppermute(array, 'tok', [(index, index ^ mask) for index in range(coun...  81.6 us
    ppermute x43, waiting for transfers between devices, flip(): lax.ppermute(array, 'tok', [(index, index ^ mask) for index in range(coun...  56.4 us
    pallas_call x6, Pallas kernels, project(): pl.pallas_call(functools.partial(project_body, row_inputs=len(xs), pieces...  23.1 us
    pallas_call x6, Pallas kernels, weight_grad(): pl.pallas_call(functools.partial(weight_grad_body, row_inputs=len(xs), pa...  20.3 us
    unnamed x50, local copies, waits for them, and re-layouts  18.4 us
    pallas_call x1, Pallas kernels, grad(): pl.pallas_call(functools.partial(grad_body, conf=key_conf), grid=(steps,)...  12.7 us
    reduce_scatter x3, waiting for transfers between devices, sum_heads(): return lax.psum_scatter(partial, 'head', scatter_dimension=0, tiled=True)[0]  12.5 us
    pallas_call x1, Pallas kernels, soft(): pl.pallas_call(functools.partial(soft_body, conf=value_conf), grid=(steps...  11.1 us
  transfers between devices with their start and end apart: 48, of which 22 were waited for; matrix products, arithmetic and copies ran while one was open for 6% of the time, Pallas kernels for 25%

profile of v4, /device:TPU:0, one launch (start us, length us, event | category | flops | bytes accessed | tf_op | source)
XLA Modules:
  0.0 282.2 jit_solution(11313680632250060078)
XLA Ops:
  16.7 2.9 %shard_map.112.refs_4_ = f32[4,128,1024]{2,1,0:T(8,128)S(1)} custom-call(s32[4]{0:T(128)S(1)} %iota_xor_fusion.place_ref, bf16[1344,1024]{1,0:T(8,128)(2,1)S(1)} %shard_map.110.refs_0_, bf16[1344,1024]{1,0:T(8,128)(2,1)S(1)} %shard_map.111.refs_1_, f32[1344,128]{1,0:T(8,128)S(1)} %copy-done.13), custom_call_target="tpu_custom_call" | custom-call | flops 1056964608 | bytes 5505024 | tf_op jit(solution)/shard_map/pallas_call | solution.py:96
  19.7 6.9 %collective-permute-done.3.refs_2_ = f32[1344,128]{1,0:T(8,128)} collective-permute-done((f32[1344,128]{1,0:T(8,128)}, f32[1344,128]{1,0:T(8,128)}, u32[]{:S(2)}, u32[]{:S(2)}) %collective-permute-start.3) | collective-permute-done | bytes 688160 | tf_op jit(solution)/shard_map/ppermute | solution.py:528
  31.2 6.2 %shard_map.113.refs_4_ = f32[4,128,1024]{2,1,0:T(8,128)S(1)} custom-call(s32[4]{0:T(128)S(1)} %iota_xor_fusion.place_ref, bf16[1344,1024]{1,0:T(8,128)(2,1)S(1)} %shard_map.110.refs_0_, bf16[1344,1024]{1,0:T(8,128)(2,1)S(1)} %shard_map.111.refs_1_, f32[1344,128]{1,0:T(8,128)} %collective-permute-done.3.refs_2_, ...), custom_call_target="tpu_custom_call", output_to_operand_aliasing={{}: (5, {})} | custom-call | flops 2113929216 | bytes 5505024 | tf_op jit(solution)/shard_map/pallas_call | solution.py:96
  50.5 8.3 %collective-permute-done.14.refs_2_ = f32[1344,128]{1,0:T(8,128)S(1)} collective-permute-done((f32[1344,128]{1,0:T(8,128)S(1)}, f32[1344,128]{1,0:T(8,128)S(1)}, u32[]{:S(2)}, u32[]{:S(2)}) %collective-permute-start.14) | collective-permute-done | bytes 688160 | tf_op jit(solution)/shard_map/ppermute | solution.py:528
  62.0 5.1 %shard_map.118 = (f32[4,128,512]{2,1,0:T(8,128)S(1)}, f32[4,128,512]{2,1,0:T(8,128)S(1)}) custom-call(s32[4]{0:T(128)S(1)} %iota_xor_fusion.place_ref, bf16[1344,1024]{1,0:T(8,128)(2,1)S(1)} %shard_map.110.refs_0_, bf16[1344,1024]{1,0:T(8,128)(2,1)S(1)} %copy-done.1, ...), custom_call_target="tpu_custom_call", output_to_operand_aliasing={{0}: (5, {}), {1}: (6, {})} | custom-call | flops 2113929216 | bytes 5505024 | tf_op jit(solution)/shard_map/pallas_call | solution.py:96
  67.8 3.0 %shard_map.119 = (f32[4,128,512]{2,1,0:T(8,128)S(1)}, f32[4,128,512]{2,1,0:T(8,128)S(1)}) custom-call(s32[4]{0:T(128)S(1)} %iota_xor_fusion.place_ref, bf16[1344,1024]{1,0:T(8,128)(2,1)S(1)} %shard_map.110.refs_0_, bf16[1344,1024]{1,0:T(8,128)(2,1)S(1)} %copy-done.1, ...), custom_call_target="tpu_custom_call", output_to_operand_aliasing={{0}: (5, {}), {1}: (6, {})} | custom-call | flops 1056964608 | bytes 5505024 | tf_op jit(solution)/shard_map/pallas_call | solution.py:96
  77.6 10.2 %reduce-scatter.4.cloned.1.call-done = f32[1,128,1024]{2,1,0:T(8,128)} async-done(((f32[4,128,1024]{2,1,0:T(8,128)}), f32[1,128,1024]{2,1,0:T(8,128)}) %reduce-scatter.4.cloned.1.call-update) | async-done | bytes 524304 | tf_op jit(solution)/shard_map/reduce_scatter | solution.py:575
  91.9 4.8 %collective-permute-done.8.refs_6_ = f32[128,512]{1,0:T(8,128)S(1)} collective-permute-done((f32[128,512]{1,0:T(8,128)S(1)}, f32[128,512]{1,0:T(8,128)S(1)}, u32[]{:S(2)}, u32[]{:S(2)}) %collective-permute-start.8) | collective-permute-done | bytes 262176 | tf_op jit(solution)/shard_map/ppermute | solution.py:528
  104.0 11.1 %shard_map.115 = (f32[4,2560,512]{2,1,0:T(8,128)}, f32[512,128]{1,0:T(8,128)}, f32[512,128]{1,0:T(8,128)}, f32[512,128]{1,0:T(8,128)}, f32[1024,128]{1,0:T(8,128)}) custom-call(s32[1]{0:T(128)} %bitcast.tok_ref, s32[7]{0:T(128)} %fork_ref.3, s32[8]{0:T(128)} %live_ref.3, f32[512,256]{1,0:T(8,128)} %get-tuple-element.138.refs_0_, ...), custom_call_target="tpu_custom_call" | custom-call | flops 3221225472 | bytes 524288 | tf_op jit(solution)/shard_map/pallas_call | solution.py:486
  117.4 8.2 %collective-permute-start.19 = (f32[128,512]{1,0:T(8,128)}, f32[128,512]{1,0:T(8,128)S(1)}, u32[]{:S(2)}, u32[]{:S(2)}) collective-permute-start(f32[128,512]{1,0:T(8,128)} %bitcast.21), channel_id=1, source_target_pairs={{0,16},{4,20},{8,24},{12,28},{16,0},{20,4},{24,8},{28,12},{1,17},{... | collective-permute-start | bytes 786440 | tf_op jit(solution)/shard_map/ppermute | solution.py:528
  125.6 4.8 %collective-permute-start.18 = (f32[128,512]{1,0:T(8,128)}, f32[128,512]{1,0:T(8,128)S(1)}, u32[]{:S(2)}, u32[]{:S(2)}) collective-permute-start(f32[128,512]{1,0:T(8,128)} %bitcast.22), channel_id=1, source_target_pairs={{0,8},{4,12},{8,0},{12,4},{16,24},{20,28},{24,16},{28,20},{1,9},{5... | collective-permute-start | bytes 786440 | tf_op jit(solution)/shard_map/ppermute | solution.py:528
  130.5 3.3 %collective-permute-start.13 = (f32[512,128]{1,0:T(8,128)}, f32[512,128]{1,0:T(8,128)S(1)}, u32[]{:S(2)}, u32[]{:S(2)}) collective-permute-start(f32[512,128]{1,0:T(8,128)} %get-tuple-element.76), channel_id=1, source_target_pairs={{0,24},{4,28},{8,16},{12,20},{16,8},{20,12},{24,0},{28,4},{1,25},{... | collective-permute-start | bytes 786440 | tf_op jit(solution)/shard_map/ppermute | solution.py:528
  134.6 3.9 %collective-permute-start.21 = (f32[128,256]{1,0:T(8,128)}, f32[128,256]{1,0:T(8,128)S(1)}, u32[]{:S(2)}, u32[]{:S(2)}) collective-permute-start(f32[128,256]{1,0:T(8,128)} %slice.69), channel_id=1, source_target_pairs={{0,8},{4,12},{8,0},{12,4},{16,24},{20,28},{24,16},{28,20},{1,9},{5... | collective-permute-start | bytes 393224 | tf_op jit(solution)/shard_map/ppermute | solution.py:528
  143.5 3.6 %collective-permute-done.13.refs_2_ = f32[512,128]{1,0:T(8,128)S(1)} collective-permute-done((f32[512,128]{1,0:T(8,128)}, f32[512,128]{1,0:T(8,128)S(1)}, u32[]{:S(2)}, u32[]{:S(2)}) %collective-permute-start.13) | collective-permute-done | bytes 262176 | tf_op jit(solution)/shard_map/ppermute | solution.py:528
  149.7 12.7 %shard_map.120 = (f32[1024,256]{1,0:T(8,128)}, f32[256,128]{1,0:T(8,128)}, f32[256,128]{1,0:T(8,128)}, f32[256,128]{1,0:T(8,128)}, f32[256,128]{1,0:T(8,128)}, /...) custom-call(s32[1]{0:T(128)} %bitcast.tok_ref, s32[7]{0:T(128)} %fork_ref.3, s32[8]{0:T(128)} %live_ref.3, ...), custom_call_target="tpu_custom_call" | custom-call | flops 6442450944 | bytes 524288 | tf_op jit(solution)/shard_map/pallas_call | solution.py:501
  162.3 6.7 %collective-permute-start.23 = (f32[256,128]{1,0:T(8,128)}, f32[256,128]{1,0:T(8,128)S(1)}, u32[]{:S(2)}, u32[]{:S(2)}) collective-permute-start(f32[256,128]{1,0:T(8,128)} %get-tuple-element.99), channel_id=1, source_target_pairs={{0,8},{4,12},{8,0},{12,4},{16,24},{20,28},{24,16},{28,20},{1,9},{5... | collective-permute-start | bytes 393224 | tf_op jit(solution)/shard_map/ppermute | solution.py:528
  169.0 11.5 %collective-permute-start.25 = (f32[256,128]{1,0:T(8,128)}, f32[256,128]{1,0:T(8,128)S(1)}, u32[]{:S(2)}, u32[]{:S(2)}) collective-permute-start(f32[256,128]{1,0:T(8,128)} %get-tuple-element.101), channel_id=1, source_target_pairs={{0,16},{4,20},{8,24},{12,28},{16,0},{20,4},{24,8},{28,12},{1,17},{... | collective-permute-start | bytes 393224 | tf_op jit(solution)/shard_map/ppermute | solution.py:528
  181.6 3.7 %collective-permute-start.24 = (f32[256,128]{1,0:T(8,128)S(1)}, f32[256,128]{1,0:T(8,128)S(1)}, u32[]{:S(2)}, u32[]{:S(2)}) collective-permute-start(f32[256,128]{1,0:T(8,128)S(1)} %add.58), channel_id=1, source_target_pairs={{0,16},{4,20},{8,24},{12,28},{16,0},{20,4},{24,8},{28,12},{1,17},{... | collective-permute-start | bytes 393224 | tf_op jit(solution)/shard_map/ppermute | solution.py:528
  207.7 4.4 %shard_map.123 = (f32[672,128]{1,0:T(8,128)S(1)}, f32[672,128]{1,0:T(8,128)S(1)}, f32[672,128]{1,0:T(8,128)S(1)}, f32[672,128]{1,0:T(8,128)S(1)}) custom-call(s32[4]{0:T(128)S(1)} %iota_xor_fusion.place_ref, bf16[1344,1024]{1,0:T(8,128)(2,1)S(1)} %shard_map.110.refs_0_, bf16[1344,1024]{1,0:T(8,128)(2,1)S(1)} %copy-done.2, f32[4,1024,128]{2,1,0:T(8,128)S(1)} %bitcast.12, ...), custom_call_target="tpu_custom_call" | custom-call | flops 2113929216 | bytes 5505024 | tf_op jit(solution)/shard_map/pallas_call | solution.py:154
  226.1 6.8 %collective-permute-done.33 = f32[672,128]{1,0:T(8,128)S(1)} collective-permute-done((f32[672,128]{1,0:T(8,128)S(1)}, f32[672,128]{1,0:T(8,128)S(1)}, u32[]{:S(2)}, u32[]{:S(2)}) %collective-permute-start.33) | collective-permute-done | bytes 344096 | tf_op jit(solution)/shard_map/ppermute | solution.py:528
  238.3 3.9 %all-gather.5.cloned.1.call-done = f32[4096,128]{1,0:T(8,128)} async-done(((f32[1024,128]{1,0:T(8,128)}), f32[4096,128]{1,0:T(8,128)}) %all-gather.5.cloned.1.call-update) | async-done | bytes 2097168 | tf_op jit(solution)/shard_map/all_gather | solution.py:578
  251.4 4.4 %shard_map.128 = (f32[672,128]{1,0:T(8,128)S(1)}, f32[672,128]{1,0:T(8,128)S(1)}, f32[672,128]{1,0:T(8,128)S(1)}, f32[672,128]{1,0:T(8,128)S(1)}) custom-call(s32[4]{0:T(128)S(1)} %iota_xor_fusion.place_ref, bf16[1344,1024]{1,0:T(8,128)(2,1)S(1)} %shard_map.125.refs_0_, bf16[1344,1024]{1,0:T(8,128)(2,1)S(1)} %copy-done.4, f32[4,1024,128]{2,1,0:T(8,128)S(1)} %bitcast.8, ...), custom_call_target="tpu_custom_call" | custom-call | flops 2113929216 | bytes 5505024 | tf_op jit(solution)/shard_map/pallas_call | solution.py:154
  266.9 3.1 %collective-permute-done.39 = f32[672,128]{1,0:T(8,128)S(1)} collective-permute-done((f32[672,128]{1,0:T(8,128)S(1)}, f32[672,128]{1,0:T(8,128)S(1)}, u32[]{:S(2)}, u32[]{:S(2)}) %collective-permute-start.39) | collective-permute-done | bytes 344096 | tf_op jit(solution)/shard_map/ppermute | solution.py:528
  270.1 4.6 %collective-permute-done.42 = f32[672,128]{1,0:T(8,128)S(1)} collective-permute-done((f32[672,128]{1,0:T(8,128)S(1)}, f32[672,128]{1,0:T(8,128)S(1)}, u32[]{:S(2)}, u32[]{:S(2)}) %collective-permute-start.42) | collective-permute-done | bytes 344096 | tf_op jit(solution)/shard_map/ppermute | solution.py:528
  (178 shorter events, 123.8 us)
Async XLA Ops:
  7.2 80.7 %reduce-scatter.4.cloned.1.call-start = ((), (), s32[]{:S(2)}) async-start(), calls=%async_computation.3 | async-start | bytes 2621440 | tf_op jit(solution)/shard_map/reduce_scatter | solution.py:575
  7.7 18.9 %collective-permute-start.3 = (f32[1344,128]{1,0:T(8,128)}, f32[1344,128]{1,0:T(8,128)}, u32[]{:S(2)}, u32[]{:S(2)}) collective-permute-start(f32[1344,128]{1,0:T(8,128)} %refs_2_.2), channel_id=1, source_target_pairs={{0,8},{4,12},{8,0},{12,4},{16,24},{20,28},{24,16},{28,20},{1,9},{5... | collective-permute-start | bytes 2064392 | tf_op jit(solution)/shard_map/ppermute | solution.py:528
  10.3 17.7 %collective-permute-start.4 = (f32[1344,128]{1,0:T(8,128)}, f32[1344,128]{1,0:T(8,128)S(1)}, u32[]{:S(2)}, u32[]{:S(2)}) collective-permute-start(f32[1344,128]{1,0:T(8,128)} %refs_2_.2), channel_id=1, source_target_pairs={{0,16},{4,20},{8,24},{12,28},{16,0},{20,4},{24,8},{28,12},{1,17},{... | collective-permute-start | bytes 2064392 | tf_op jit(solution)/shard_map/ppermute | solution.py:528
  42.8 74.6 %reduce-scatter.6.cloned.1.call-start = ((), (), s32[]{:S(2)}) async-start(), calls=%async_computation.4 | async-start | bytes 1310720 | tf_op jit(solution)/shard_map/reduce_scatter | solution.py:575
  42.9 15.9 %collective-permute-start.14 = (f32[1344,128]{1,0:T(8,128)S(1)}, f32[1344,128]{1,0:T(8,128)S(1)}, u32[]{:S(2)}, u32[]{:S(2)}) collective-permute-start(f32[1344,128]{1,0:T(8,128)S(1)} %copy-done.12), channel_id=1, source_target_pairs={{0,8},{4,12},{8,0},{12,4},{16,24},{20,28},{24,16},{28,20},{1,9},{5... | collective-permute-start | bytes 2064392 | tf_op jit(solution)/shard_map/ppermute | solution.py:528
  44.3 15.2 %collective-permute-start.15 = (f32[1344,128]{1,0:T(8,128)S(1)}, f32[1344,128]{1,0:T(8,128)S(1)}, u32[]{:S(2)}, u32[]{:S(2)}) collective-permute-start(f32[1344,128]{1,0:T(8,128)S(1)} %copy-done.12), channel_id=1, source_target_pairs={{0,16},{4,20},{8,24},{12,28},{16,0},{20,4},{24,8},{28,12},{1,17},{... | collective-permute-start | bytes 2064392 | tf_op jit(solution)/shard_map/ppermute | solution.py:528
  72.7 76.3 %reduce-scatter.8.cloned.1.call-start = ((), (), s32[]{:S(2)}) async-start(), calls=%async_computation.5 | async-start | bytes 1310720 | tf_op jit(solution)/shard_map/reduce_scatter | solution.py:575
  73.4 124.7 %all-gather.7.cloned.1.call-start = ((), (), s32[]{:S(2)}) async-start(), calls=%async_computation.7 | async-start | bytes 2621440 | tf_op jit(solution)/shard_map/all_gather | solution.py:578
  76.0 24.0 %collective-permute-start = (f32[512,256]{1,0:T(8,128)}, f32[512,256]{1,0:T(8,128)}, u32[]{:S(2)}, u32[]{:S(2)}) collective-permute-start(f32[512,256]{1,0:T(8,128)} %get-tuple-element.137), channel_id=1, source_target_pairs={{0,4},{4,0},{8,12},{12,8},{16,20},{20,16},{24,28},{28,24},{1,5},{5... | collective-permute-start | bytes 1572872 | tf_op jit(solution)/shard_map/ppermute | solution.py:528
  77.1 22.9 %collective-permute-start.1 = (f32[512,256]{1,0:T(8,128)}, f32[512,256]{1,0:T(8,128)}, u32[]{:S(2)}, u32[]{:S(2)}) collective-permute-start(f32[512,256]{1,0:T(8,128)} %get-tuple-element.135), channel_id=1, source_target_pairs={{0,4},{4,0},{8,12},{12,8},{16,20},{20,16},{24,28},{28,24},{1,5},{5... | collective-permute-start | bytes 1572872 | tf_op jit(solution)/shard_map/ppermute | solution.py:528
  117.4 16.5 %collective-permute-start.19 = (f32[128,512]{1,0:T(8,128)}, f32[128,512]{1,0:T(8,128)S(1)}, u32[]{:S(2)}, u32[]{:S(2)}) collective-permute-start(f32[128,512]{1,0:T(8,128)} %bitcast.21), channel_id=1, source_target_pairs={{0,16},{4,20},{8,24},{12,28},{16,0},{20,4},{24,8},{28,12},{1,17},{... | collective-permute-start | bytes 786440 | tf_op jit(solution)/shard_map/ppermute | solution.py:528
  130.4 13.1 %collective-permute-start.11 = (f32[512,128]{1,0:T(8,128)}, f32[512,128]{1,0:T(8,128)S(1)}, u32[]{:S(2)}, u32[]{:S(2)}) collective-permute-start(f32[512,128]{1,0:T(8,128)} %get-tuple-element.74), channel_id=1, source_target_pairs={{0,8},{4,12},{8,0},{12,4},{16,24},{20,28},{24,16},{28,20},{1,9},{5... | collective-permute-start | bytes 786440 | tf_op jit(solution)/shard_map/ppermute | solution.py:528
  130.5 16.5 %collective-permute-start.13 = (f32[512,128]{1,0:T(8,128)}, f32[512,128]{1,0:T(8,128)S(1)}, u32[]{:S(2)}, u32[]{:S(2)}) collective-permute-start(f32[512,128]{1,0:T(8,128)} %get-tuple-element.76), channel_id=1, source_target_pairs={{0,24},{4,28},{8,16},{12,20},{16,8},{20,12},{24,0},{28,4},{1,25},{... | collective-permute-start | bytes 786440 | tf_op jit(solution)/shard_map/ppermute | solution.py:528
  134.6 14.4 %collective-permute-start.21 = (f32[128,256]{1,0:T(8,128)}, f32[128,256]{1,0:T(8,128)S(1)}, u32[]{:S(2)}, u32[]{:S(2)}) collective-permute-start(f32[128,256]{1,0:T(8,128)} %slice.69), channel_id=1, source_target_pairs={{0,8},{4,12},{8,0},{12,4},{16,24},{20,28},{24,16},{28,20},{1,9},{5... | collective-permute-start | bytes 393224 | tf_op jit(solution)/shard_map/ppermute | solution.py:528
  149.0 93.2 %all-gather.5.cloned.1.call-start = ((), (), s32[]{:S(2)}) async-start(), calls=%async_computation.6 | async-start | bytes 2621440 | tf_op jit(solution)/shard_map/all_gather | solution.py:578
  162.3 18.4 %collective-permute-start.23 = (f32[256,128]{1,0:T(8,128)}, f32[256,128]{1,0:T(8,128)S(1)}, u32[]{:S(2)}, u32[]{:S(2)}) collective-permute-start(f32[256,128]{1,0:T(8,128)} %get-tuple-element.99), channel_id=1, source_target_pairs={{0,8},{4,12},{8,0},{12,4},{16,24},{20,28},{24,16},{28,20},{1,9},{5... | collective-permute-start | bytes 393224 | tf_op jit(solution)/shard_map/ppermute | solution.py:528
  169.0 16.3 %collective-permute-start.25 = (f32[256,128]{1,0:T(8,128)}, f32[256,128]{1,0:T(8,128)S(1)}, u32[]{:S(2)}, u32[]{:S(2)}) collective-permute-start(f32[256,128]{1,0:T(8,128)} %get-tuple-element.101), channel_id=1, source_target_pairs={{0,16},{4,20},{8,24},{12,28},{16,0},{20,4},{24,8},{28,12},{1,17},{... | collective-permute-start | bytes 393224 | tf_op jit(solution)/shard_map/ppermute | solution.py:528
  196.8 18.2 %collective-permute-start.34 = (f32[512,256]{1,0:T(8,128)}, f32[512,256]{1,0:T(8,128)}, u32[]{:S(2)}, u32[]{:S(2)}) collective-permute-start(f32[512,256]{1,0:T(8,128)} %get-tuple-element.134), channel_id=1, source_target_pairs={{0,4},{4,0},{8,12},{12,8},{16,20},{20,16},{24,28},{28,24},{1,5},{5... | collective-permute-start | bytes 1572872 | tf_op jit(solution)/shard_map/ppermute | solution.py:528
  207.5 17.4 %collective-permute-start.35 = (f32[512,128]{1,0:T(8,128)S(1)}, f32[512,128]{1,0:T(8,128)S(1)}, u32[]{:S(2)}, u32[]{:S(2)}) collective-permute-start(f32[512,128]{1,0:T(8,128)S(1)} %get-tuple-element.142), channel_id=1, source_target_pairs={{0,4},{4,0},{8,12},{12,8},{16,20},{20,16},{24,28},{28,24},{1,5},{5... | collective-permute-start | bytes 786440 | tf_op jit(solution)/shard_map/ppermute | solution.py:528
  207.6 14.7 %collective-permute-start.31 = (f32[672,128]{1,0:T(8,128)S(1)}, f32[672,128]{1,0:T(8,128)S(1)}, u32[]{:S(2)}, u32[]{:S(2)}) collective-permute-start(f32[672,128]{1,0:T(8,128)S(1)} %get-tuple-element.111), channel_id=1, source_target_pairs={{0,16},{4,20},{8,24},{12,28},{16,0},{20,4},{24,8},{28,12},{1,17},{... | collective-permute-start | bytes 1032200 | tf_op jit(solution)/shard_map/ppermute | solution.py:528
  212.2 13.6 %collective-permute-start.28 = (f32[672,128]{1,0:T(8,128)S(1)}, f32[672,128]{1,0:T(8,128)S(1)}, u32[]{:S(2)}, u32[]{:S(2)}) collective-permute-start(f32[672,128]{1,0:T(8,128)S(1)} %get-tuple-element.106), channel_id=1, source_target_pairs={{0,8},{4,12},{8,0},{12,4},{16,24},{20,28},{24,16},{28,20},{1,9},{5... | collective-permute-start | bytes 1032200 | tf_op jit(solution)/shard_map/ppermute | solution.py:528
  217.4 15.4 %collective-permute-start.33 = (f32[672,128]{1,0:T(8,128)S(1)}, f32[672,128]{1,0:T(8,128)S(1)}, u32[]{:S(2)}, u32[]{:S(2)}) collective-permute-start(f32[672,128]{1,0:T(8,128)S(1)} %get-tuple-element.112), channel_id=1, source_target_pairs={{0,16},{4,20},{8,24},{12,28},{16,0},{20,4},{24,8},{28,12},{1,17},{... | collective-permute-start | bytes 1032200 | tf_op jit(solution)/shard_map/ppermute | solution.py:528
  261.0 13.7 %collective-permute-start.42 = (f32[672,128]{1,0:T(8,128)S(1)}, f32[672,128]{1,0:T(8,128)S(1)}, u32[]{:S(2)}, u32[]{:S(2)}) collective-permute-start(f32[672,128]{1,0:T(8,128)S(1)} %get-tuple-element.131), channel_id=1, source_target_pairs={{0,16},{4,20},{8,24},{12,28},{16,0},{20,4},{24,8},{28,12},{1,17},{... | collective-permute-start | bytes 1032200 | tf_op jit(solution)/shard_map/ppermute | solution.py:528
  261.2 13.6 %collective-permute-start.41 = (f32[672,128]{1,0:T(8,128)S(1)}, f32[672,128]{1,0:T(8,128)S(1)}, u32[]{:S(2)}, u32[]{:S(2)}) collective-permute-start(f32[672,128]{1,0:T(8,128)S(1)} %add.69), channel_id=1, source_target_pairs={{0,8},{4,12},{8,0},{12,4},{16,24},{20,28},{24,16},{28,20},{1,9},{5... | collective-permute-start | bytes 1032200 | tf_op jit(solution)/shard_map/ppermute | solution.py:528
  (49 other events, 312.7 us)
Sparse Core Ops, SparseCore 0:
  42.9 44.8 reduce-scatter.3
  90.8 26.5 reduce-scatter.5
  119.7 25.7 reduce-scatter.7
  149.1 46.2 all-gather.6
  197.5 44.6 all-gather.4

commit v5 on v4

--- a/solution.py
+++ b/solution.py
@@ -284,15 +284,35 @@
     return how(value.reshape(SPAN // 8, 8, value.shape[1]), axis=0)
 
 
+def stage_body(tok_ref, live_ref, *refs, nb, group, halves):
+    q_refs, g_refs = refs[:nb], refs[nb : 2 * nb]
+    qt_ref, q_ref, gt_ref, grad_ref = refs[2 * nb :]
+    step = pl.program_id(0)
+    slot, half = lax.div(step, jnp.int32(halves)), lax.rem(step, jnp.int32(halves))
+    live = live_ref[tok_ref[0] ^ slot]
+    for source in range(nb):
+
+        @pl.when(slot == source)
+        def _():
+            for head in range(group):
+                part = slice(head * SPAN, (head + 1) * SPAN)
+                rows = load_rows(q_refs[source], half, head) * logit_scale
+                qt_ref[0, :, part] = transposed_pair(rows)
+                q_ref[0, part, :] = pair_cat(rows, 1)
+                rows = load_rows(g_refs[source], half, head) * live_column(half, live)
+                gt_ref[0, :, part] = transposed_pair(rows)
+                grad_ref[0, part, :] = pair_cat(rows, 1)
+
+
 def soft_body(tok_ref, fork_ref, live_ref, *refs, conf):
     nb, group, owners, layout, sources, outs = conf["nb"], conf["group"], conf["owners"], conf["layout"], conf["sources"], conf["outs"]
     halves = conf["rows"] // SPAN
     lanes = group * SPAN
-    q_refs, g_refs = refs[:nb], refs[nb : 2 * nb]
-    key_refs = refs[2 * nb : 2 * nb + sources]
-    prob_ref = refs[2 * nb + sources]
-    out_refs = refs[2 * nb + sources + 1 : 2 * nb + sources + 1 + outs]
-    keys_ref, sum_ref, scores_ref, qt_ref, grad_ref, offset_ref, limit_ref, many_ref, sems = refs[2 * nb + sources + 1 + outs :]
+    qt_ref, grad_ref = refs[:2]
+    key_refs = refs[2 : 2 + sources]
+    prob_ref = refs[2 + sources]
+    out_refs = refs[3 + sources : 3 + sources + outs]
+    keys_ref, sum_ref, scores_ref, offset_ref, limit_ref, many_ref, sems = refs[3 + sources + outs :]
     step = pl.program_id(0)
     tok = tok_ref[0]
     turn = lax.rem(step, 2)
@@ -319,18 +339,8 @@
     branch, slot, half, count = find_step(many_ref, step, tok, halves)
     place_of = functools.partial(block_offset, offset_ref, owners * SPAN, slot, half, halves)
     live = live_ref[branch]
-    for source in range(nb):
-
-        @pl.when(slot == source)
-        def _():
-            for head in range(group):
-                qt_ref[:, head * SPAN : (head + 1) * SPAN] = transposed_pair(load_rows(q_refs[source], half, head) * logit_scale)
-                grad_ref[head * SPAN : (head + 1) * SPAN, :] = pair_cat(
-                    load_rows(g_refs[source], half, head) * live_column(half, live), 1
-                )
-
     def first(block, largest):
-        value = scores(keys_ref, place_of(block), qt_ref[...], key_limits(limit_ref, slot, half, live, block, lanes))
+        value = scores(keys_ref, place_of(block), qt_ref[0], key_limits(limit_ref, slot, half, live, block, lanes))
         score_ref[slot_rows(block), :] = value
         return jnp.maximum(largest, fold(value, jnp.max))
 
@@ -350,7 +360,7 @@
         score_ref[slot_rows(block), :] = prob
         copy_out(step, block).start()
         high, low = split(prob)
-        grads = grad_ref[...]
+        grads = grad_ref[0]
         both = dot(high, grads) + dot(low, grads)
         offset = place_of(block)
         sum_ref[slot_rows(offset // SPAN), :] += both[:, :HEAD_DIM] + both[:, HEAD_DIM:]
@@ -372,15 +382,15 @@
     nb, group, owners, layout, sources, outs = conf["nb"], conf["group"], conf["owners"], conf["layout"], conf["sources"], conf["outs"]
     halves = conf["rows"] // SPAN
     lanes = group * SPAN
-    q_refs, g_refs = refs[:nb], refs[nb : 2 * nb]
-    at = 2 * nb
+    gt_ref, q_ref = refs[:2]
+    at = 2
     value_sources = conf["value_sources"]
     key_refs, value_refs = refs[at : at + sources], refs[at + sources : at + sources + value_sources]
     at += sources + value_sources
     prob_ref = refs[at]
     dq_ref = refs[at + 1]
     out_refs = refs[at + 2 : at + 2 + outs]
-    (keys_ref, values_ref, sum_ref, probs_ref, dprob_ref, gt_ref, q_ref, dqt_ref, offset_ref, limit_ref, many_ref, sems) = refs[at + 2 + outs :]
+    (keys_ref, values_ref, sum_ref, probs_ref, dprob_ref, dqt_ref, offset_ref, limit_ref, many_ref, sems) = refs[at + 2 + outs :]
     step = pl.program_id(0)
     tok = tok_ref[0]
     held_ref = probs_ref.at[lax.rem(step, 2)]
@@ -411,21 +421,9 @@
 
     branch, slot, half, count = find_step(many_ref, step, tok, halves)
     place_of = functools.partial(block_offset, offset_ref, owners * SPAN, slot, half, halves)
-    live = live_ref[branch]
-    for source in range(nb):
-
-        @pl.when(slot == source)
-        def _():
-            for head in range(group):
-                rows = load_rows(q_refs[source], half, head) * logit_scale
-                q_ref[head * SPAN : (head + 1) * SPAN, :] = pair_cat(rows, 1)
-                gt_ref[:, head * SPAN : (head + 1) * SPAN] = transposed_pair(
-                    load_rows(g_refs[source], half, head) * live_column(half, live)
-                )
-
     def first(block, delta):
         values = block_rows(values_ref, place_of(block))
-        dprob = dot(jnp.concatenate([values, values], axis=1), gt_ref[...])
+        dprob = dot(jnp.concatenate([values, values], axis=1), gt_ref[0])
         dprob_ref[slot_rows(block), :] = dprob
         return delta + fold(held_ref[slot_rows(block), :] * dprob, jnp.sum)
 
@@ -436,7 +434,7 @@
     def second(block, _):
         offset = place_of(block)
         high, low = split(held_ref[slot_rows(block), :] * (dprob_ref[slot_rows(block), :] - delta))
-        rows = q_ref[...]
+        rows = q_ref[0]
         both = dot(high, rows) + dot(low, rows)
         sum_ref[slot_rows(offset // SPAN), :] += both[:, :HEAD_DIM] + both[:, HEAD_DIM:]
         keys = block_rows(keys_ref, offset)
@@ -477,31 +475,49 @@
     table = pltpu.VMEM((table_rows, 2 * HEAD_DIM), bf16)
     table_sum = pltpu.VMEM((table_rows, HEAD_DIM), f32)
     square = pltpu.VMEM((slots, lanes), f32)
-    columns = pltpu.VMEM((4 * HEAD_DIM, lanes), bf16)
+    columns = jax.ShapeDtypeStruct((steps, 4 * HEAD_DIM, lanes), bf16)
+    pairs = jax.ShapeDtypeStruct((steps, lanes, 2 * HEAD_DIM), bf16)
+
+    def by_step(array):
+        return pl.BlockSpec((1, *array.shape[1:]), lambda step: (step, 0, 0))
+
     lists = [pltpu.SMEM((nb, owners + 1), jnp.int32)] * 2 + [pltpu.SMEM((nb,), jnp.int32)]
     params = pltpu.CompilerParams(vmem_limit_bytes=56 * MIB)
     work = 2 * steps * 6 * SPAN * lanes * 2 * HEAD_DIM
 
-    def soft(keys):
+    def stage():
+        return pl.pallas_call(
+            functools.partial(stage_body, nb=nb, group=group, halves=halves),
+            grid=(steps,),
+            in_specs=[smem_spec] * 2 + [whole_spec(a) for a in (*qs, *gs)],
+            out_specs=[by_step(columns), by_step(pairs)] * 2,
+            out_shape=[columns, pairs] * 2,
+            compiler_params=pltpu.CompilerParams(vmem_limit_bytes=56 * MIB),
+            cost_estimate=pl.CostEstimate(flops=8 * steps * lanes * HEAD_DIM, bytes_accessed=16 * steps * lanes * HEAD_DIM, transcendentals=0),
+        )(scalars[0], scalars[2], *qs, *gs)
+
+    def soft(staged, keys):
+        qt, _, _, g_pairs = staged
         return pl.pallas_call(
             functools.partial(soft_body, conf=value_conf),
             grid=(steps,),
-            in_specs=[smem_spec] * 3 + [whole_spec(a) for a in (*qs, *gs, *keys)],
+            in_specs=[smem_spec] * 3 + [by_step(qt), by_step(g_pairs)] + [whole_spec(a) for a in keys],
             out_specs=[probs_spec] + [whole_spec(a) for a in value_sums],
             out_shape=[probs] + value_sums,
-            scratch_shapes=[table, table_sum, two_squares, columns, pltpu.VMEM((lanes, 2 * HEAD_DIM), bf16)]
+            scratch_shapes=[table, table_sum, two_squares]
             + lists
             + [sems],
             compiler_params=params,
             cost_estimate=pl.CostEstimate(flops=2 * work, bytes_accessed=4 * rows * width, transcendentals=0),
-        )(*scalars, *qs, *gs, *keys)
-
-    def grad(keys, values, probs_in):
+        )(*scalars, qt, g_pairs, *keys)
+
+    def grad(staged, keys, values, probs_in):
+        _, q_pairs, gt, _ = staged
         dq = jax.ShapeDtypeStruct((nb * rows, width), f32)
         return pl.pallas_call(
             functools.partial(grad_body, conf=key_conf),
             grid=(steps,),
-            in_specs=[smem_spec] * 3 + [whole_spec(a) for a in (*qs, *gs, *keys, *values)] + [probs_spec],
+            in_specs=[smem_spec] * 3 + [by_step(gt), by_step(q_pairs)] + [whole_spec(a) for a in (*keys, *values)] + [probs_spec],
             out_specs=[pl.BlockSpec((SPAN, width), lambda step: (step, 0))] + [whole_spec(a) for a in key_sums],
             out_shape=[dq] + key_sums,
             scratch_shapes=[
@@ -510,17 +526,15 @@
                 table_sum,
                 two_squares,
                 square,
-                columns,
-                pltpu.VMEM((lanes, 2 * HEAD_DIM), bf16),
                 pltpu.VMEM((2 * HEAD_DIM, lanes), f32),
             ]
             + lists
             + [sems],
             compiler_params=params,
             cost_estimate=pl.CostEstimate(flops=4 * work, bytes_accessed=4 * rows * width, transcendentals=0),
-        )(*scalars, *qs, *gs, *keys, *values, probs_in)
-
-    return soft, grad
+        )(*scalars, gt, q_pairs, *keys, *values, probs_in)
+
+    return stage, soft, grad
 
 
 def flip(array, mask):
@@ -530,6 +544,12 @@
 
 def together(*arrays):
     return lax.optimization_barrier(arrays)
+
+
+def flip_one_way(array, mask, rising):
+    count = lax.axis_size("tok")
+    pairs = [(index, index ^ mask) for index in range(count) if (index < index ^ mask) == rising]
+    return lax.ppermute(array, "tok", pairs)
 
 
 def gather_square(array, cut, axis):
@@ -587,7 +607,7 @@
 
     def returned_at_once(across, down, corner, own):
         plan = tuple((index, slot * SPAN, slot * rows, SPAN) for index in range(3) for slot in range(2))
-        return combine(own, [flip(across, 2), flip(down, 4), flip(corner, 6)], plan)
+        return combine(own, [flip_one_way(across, 2, False), flip_one_way(down, 4, False), flip_one_way(corner, 6, False)], plan)
 
     def weight(every, xs):
         corner = weight_grad(place, (3,), xs, every)
@@ -628,21 +648,25 @@
         (0, 0, 0, 2 * SPAN),
         (1, 0, base + SPAN, SPAN),
         (1, SPAN, base + rows + SPAN, SPAN),
-    ) + tuple((index + 1, *rest) for index, *rest in layout[3:])
+        (2, 0, 2 * SPAN, 2 * SPAN),
+        (3, 0, 4 * SPAN, 2 * SPAN),
+        (4, 0, 6 * SPAN, 2 * SPAN),
+    )
     key_sum_rows = tuple((0, (2 + index) * SPAN, SPAN) for index in range(6))
     value_sum_rows = tuple((0, 2 * (1 + index) * SPAN, 2 * SPAN) for index in range(3))
-    soft, grad = attention_calls(scalars, qs, gs, layout, value_layout, key_sum_rows, value_sum_rows, True, owners)
-
+    stage, soft, grad = attention_calls(scalars, qs, gs, layout, value_layout, key_sum_rows, value_sum_rows, True, owners)
+
+    keys, *staged = together(keys, *stage())
     key_parts = [keys, *gather_square(lead(keys), SPAN, 1)]
-    probs, *value_sums = soft(key_parts)
+    probs, *value_sums = soft(staged, key_parts)
     value_parts = list(together(leading, *value_sums))[:1]
-    value_parts += gather_square(value_parts[0], SPAN, 1)
+    value_parts += [flip_one_way(value_parts[0], mask, True) for mask in (2, 4, 6)]
     value_grads = returned_at_once(*value_sums)
     probs, value_grads, *value_parts = together(probs, value_grads, *value_parts)
     trailing, value_grads = together(trailing, value_grads)
     every_value = all_heads(value_grads)
     value_parts = [value_parts[0], trailing, *value_parts[1:]]
-    grad_query, *key_sums = grad(key_parts, value_parts, probs)
+    grad_query, *key_sums = grad(staged, key_parts, value_parts, probs)
     key_grads = returned(*key_sums)
     every_key = all_heads(key_grads)
     every_value, key_grads = together(every_value, key_grads)
@@ -668,7 +692,7 @@
     keys, values = projected(w_key), projected(w_value)
     layout = ((0, 0, owners * SPAN, hidden.shape[0]), (1, 0, 0, owners * SPAN))
     sums = ((0, 0, owners * SPAN),)
-    soft, grad = attention_calls(scalars, [queries], [out_grad], layout, layout, sums, sums, False, owners)
+    stage, soft, grad = attention_calls(scalars, [queries], [out_grad], layout, layout, sums, sums, False, owners)
 
     def parts(array):
         return [array, lax.all_gather(array[:, :SPAN], "tok", axis=1, tiled=True)]
@@ -681,10 +705,11 @@
         columns = lax.dot_general(hidden, every, (((0,), (0,)), ((), ())), precision=lax.Precision.HIGHEST)
         return lax.psum_scatter(columns, "tok", scatter_dimension=1, tiled=True)
 
+    staged = stage()
     key_parts = parts(keys)
-    probs, *value_sums = soft(key_parts)
+    probs, *value_sums = soft(staged, key_parts)
     value_grads = returned(*value_sums)
-    grad_query, *key_sums = grad(key_parts, parts(values), probs)
+    grad_query, *key_sums = grad(staged, key_parts, parts(values), probs)
     key_grads = returned(*key_sums)
     return grad_query, key_grads, value_grads, weight(key_grads), weight(value_grads)
 

time: 283 us -> 279 us (0.986)
  waiting for transfers between devices: 73.5 us -> 66.4 us
  starting transfers between devices: 82 us -> 85.1 us
    ppermute x0 -> x6, starting transfers between devices: none -> 25.5 us  [flip_one_way(): return lax.ppermute(array, 'tok', pairs)]
    ppermute x43 -> x36, starting transfers between devices: 81.6 us -> 59.2 us  [flip(): lax.ppermute(array, 'tok', [(index, index ^ mask) for index in range(coun...]
    reduce_scatter x3, waiting for transfers between devices: 12.5 us -> 5.38 us  [sum_heads(): return lax.psum_scatter(partial, 'head', scatter_dimension=0, tiled=True)[0]]
    pallas_call x0 -> x1, Pallas kernels: none -> 4.78 us  [stage(): pl.pallas_call(functools.partial(stage_body, nb=nb, group=group, halves=h...]
    ppermute x43 -> x36, waiting for transfers between devices: 56.4 us -> 53.1 us  [flip(): lax.ppermute(array, 'tok', [(index, index ^ mask) for index in range(coun...]
    unnamed x50 -> x46, local copies, waits for them, and re-layouts: 18.4 us -> 17.9 us
  transfers between devices with their start and end apart: 48 -> 47, of which waited for: 22 -> 25; matrix products, arithmetic and copies ran while one was open for 6% -> 6% of each run, Pallas kernels for 25% -> 26%
where the time goes in v5:
time: 279 us; the launch traced here: 278 us
  starting transfers between devices  85.1 us (31%)
  Pallas kernels  77.6 us (28%)
  waiting for transfers between devices  66.4 us (24%)
  local copies, waits for them, and re-layouts  27.7 us (10%)
  between operations  14.2 us (5%)
  other arithmetic  6.83 us (2%)
    ppermute x36, starting transfers between devices, flip(): lax.ppermute(array, 'tok', [(index, index ^ mask) for index in range(coun...  59.2 us
    ppermute x36, waiting for transfers between devices, flip(): lax.ppermute(array, 'tok', [(index, index ^ mask) for index in range(coun...  53.1 us
    ppermute x6, starting transfers between devices, flip_one_way(): return lax.ppermute(array, 'tok', pairs)  25.5 us
    pallas_call x6, Pallas kernels, project(): pl.pallas_call(functools.partial(project_body, row_inputs=len(xs), pieces...  23.1 us
    pallas_call x6, Pallas kernels, weight_grad(): pl.pallas_call(functools.partial(weight_grad_body, row_inputs=len(xs), pa...  20.3 us
    unnamed x46, local copies, waits for them, and re-layouts  17.9 us
    pallas_call x1, Pallas kernels, grad(): pl.pallas_call(functools.partial(grad_body, conf=key_conf), grid=(steps,)...  11.7 us
    pallas_call x1, Pallas kernels, soft(): pl.pallas_call(functools.partial(soft_body, conf=value_conf), grid=(steps...  9.85 us
  transfers between devices with their start and end apart: 47, of which 25 were waited for; matrix products, arithmetic and copies ran while one was open for 6% of the time, Pallas kernels for 26%

profile of v5, /device:TPU:0, one launch (start us, length us, event | category | flops | bytes accessed | tf_op | source)
XLA Modules:
  0.0 277.8 jit_solution(11096937686164167080)
XLA Ops:
  16.7 2.9 %shard_map.112.refs_4_ = f32[4,128,1024]{2,1,0:T(8,128)S(1)} custom-call(s32[4]{0:T(128)S(1)} %iota_xor_fusion.place_ref, bf16[1344,1024]{1,0:T(8,128)(2,1)S(1)} %shard_map.110.refs_0_, bf16[1344,1024]{1,0:T(8,128)(2,1)S(1)} %shard_map.111.refs_1_, f32[1344,128]{1,0:T(8,128)S(1)} %copy-done.13), custom_call_target="tpu_custom_call" | custom-call | flops 1056964608 | bytes 5505024 | tf_op jit(solution)/shard_map/pallas_call | solution.py:96
  19.7 6.9 %collective-permute-done.1.refs_2_ = f32[1344,128]{1,0:T(8,128)} collective-permute-done((f32[1344,128]{1,0:T(8,128)}, f32[1344,128]{1,0:T(8,128)}, u32[]{:S(2)}, u32[]{:S(2)}) %collective-permute-start.1) | collective-permute-done | bytes 688160 | tf_op jit(solution)/shard_map/ppermute | solution.py:542
  31.2 6.2 %shard_map.113.refs_4_ = f32[4,128,1024]{2,1,0:T(8,128)S(1)} custom-call(s32[4]{0:T(128)S(1)} %iota_xor_fusion.place_ref, bf16[1344,1024]{1,0:T(8,128)(2,1)S(1)} %shard_map.110.refs_0_, bf16[1344,1024]{1,0:T(8,128)(2,1)S(1)} %shard_map.111.refs_1_, f32[1344,128]{1,0:T(8,128)} %collective-permute-done.1.refs_2_, ...), custom_call_target="tpu_custom_call", output_to_operand_aliasing={{}: (5, {})} | custom-call | flops 2113929216 | bytes 5505024 | tf_op jit(solution)/shard_map/pallas_call | solution.py:96
  38.6 2.9 %shard_map.114 = f32[4,128,1024]{2,1,0:T(8,128)S(1)} custom-call(s32[4]{0:T(128)S(1)} %iota_xor_fusion.place_ref, bf16[1344,1024]{1,0:T(8,128)(2,1)S(1)} %shard_map.110.refs_0_, bf16[1344,1024]{1,0:T(8,128)(2,1)S(1)} %shard_map.111.refs_1_, f32[640,128]{1,0:T(8,128)S(1)} %collective-permute-done.3.refs_2_, ...), custom_call_target="tpu_custom_call", output_to_operand_aliasing={{}: (5, {})} | custom-call | flops 1056964608 | bytes 5505024 | tf_op jit(solution)/shard_map/pallas_call | solution.py:96
  47.6 2.9 %shard_map.118 = (f32[4,128,512]{2,1,0:T(8,128)S(1)}, f32[4,128,512]{2,1,0:T(8,128)S(1)}) custom-call(s32[4]{0:T(128)S(1)} %iota_xor_fusion.place_ref, bf16[1344,1024]{1,0:T(8,128)(2,1)S(1)} %shard_map.110.refs_0_, bf16[1344,1024]{1,0:T(8,128)(2,1)S(1)} %copy-done.1, f32[1344,128]{1,0:T(8,128)S(1)} %copy-done.12), custom_call_target="tpu_custom_call" | custom-call | flops 1056964608 | bytes 5505024 | tf_op jit(solution)/shard_map/pallas_call | solution.py:96
  50.5 8.2 %collective-permute-done.14.refs_2_ = f32[1344,128]{1,0:T(8,128)S(1)} collective-permute-done((f32[1344,128]{1,0:T(8,128)S(1)}, f32[1344,128]{1,0:T(8,128)S(1)}, u32[]{:S(2)}, u32[]{:S(2)}) %collective-permute-start.14) | collective-permute-done | bytes 688160 | tf_op jit(solution)/shard_map/ppermute | solution.py:542
  62.0 5.1 %shard_map.119 = (f32[4,128,512]{2,1,0:T(8,128)S(1)}, f32[4,128,512]{2,1,0:T(8,128)S(1)}) custom-call(s32[4]{0:T(128)S(1)} %iota_xor_fusion.place_ref, bf16[1344,1024]{1,0:T(8,128)(2,1)S(1)} %shard_map.110.refs_0_, bf16[1344,1024]{1,0:T(8,128)(2,1)S(1)} %copy-done.1, ...), custom_call_target="tpu_custom_call", output_to_operand_aliasing={{0}: (5, {}), {1}: (6, {})} | custom-call | flops 2113929216 | bytes 5505024 | tf_op jit(solution)/shard_map/pallas_call | solution.py:96
  67.8 2.9 %shard_map.120 = (f32[4,128,512]{2,1,0:T(8,128)S(1)}, f32[4,128,512]{2,1,0:T(8,128)S(1)}) custom-call(s32[4]{0:T(128)S(1)} %iota_xor_fusion.place_ref, bf16[1344,1024]{1,0:T(8,128)(2,1)S(1)} %shard_map.110.refs_0_, bf16[1344,1024]{1,0:T(8,128)(2,1)S(1)} %copy-done.1, ...), custom_call_target="tpu_custom_call", output_to_operand_aliasing={{0}: (5, {}), {1}: (6, {})} | custom-call | flops 1056964608 | bytes 5505024 | tf_op jit(solution)/shard_map/pallas_call | solution.py:96
  78.6 4.8 %shard_map.115 = (bf16[4,512,512]{2,1,0:T(8,128)(2,1)}, bf16[4,512,256]{2,1,0:T(8,128)(2,1)}, bf16[4,512,512]{2,1,0:T(8,128)(2,1)}, bf16[4,512,256]{2,1,0:T(8,128)(2,1)}) custom-call(s32[1]{0:T(128)} %bitcast.tok_ref, s32[8]{0:T(128)} %live_ref.5, f32[512,256]{1,0:T(8,128)} %get-tuple-element.154.refs_0_, f32[512,256]{1,0:T(8,128)} %copy-done.20, ...), custom_call_target="tpu_custom_call" | custom-call | flops 2097152 | bytes 4194304 | tf_op jit(solution)/shard_map/pallas_call | solution.py:489
  83.4 4.6 %reduce-scatter.4.cloned.1.call-done = f32[1,128,1024]{2,1,0:T(8,128)} async-done(((f32[4,128,1024]{2,1,0:T(8,128)}), f32[1,128,1024]{2,1,0:T(8,128)}) %reduce-scatter.4.cloned.1.call-update) | async-done | bytes 524304 | tf_op jit(solution)/shard_map/reduce_scatter | solution.py:595
  91.9 4.9 %collective-permute-done.8.refs_4_ = f32[128,512]{1,0:T(8,128)S(1)} collective-permute-done((f32[128,512]{1,0:T(8,128)S(1)}, f32[128,512]{1,0:T(8,128)S(1)}, u32[]{:S(2)}, u32[]{:S(2)}) %collective-permute-start.8) | collective-permute-done | bytes 262176 | tf_op jit(solution)/shard_map/ppermute | solution.py:542
  104.0 9.8 %shard_map.116 = (f32[4,2560,512]{2,1,0:T(8,128)}, f32[512,128]{1,0:T(8,128)}, f32[512,128]{1,0:T(8,128)}, f32[512,128]{1,0:T(8,128)}, f32[1024,128]{1,0:T(8,128)}) custom-call(s32[1]{0:T(128)} %bitcast.tok_ref, s32[7]{0:T(128)} %fork_ref.3, s32[8]{0:T(128)} %live_ref.5, bf16[4,512,512]{2,1,0:T(8,128)(2,1)} %get-tuple-element.87.refs_0_, ...), custom_call_target="tpu_custom_call" | custom-call | flops 3221225472 | bytes 524288 | tf_op jit(solution)/shard_map/pallas_call | solution.py:501
  117.8 17.2 %collective-permute-start.20 = (f32[128,512]{1,0:T(8,128)}, f32[128,512]{1,0:T(8,128)}, u32[]{:S(2)}, u32[]{:S(2)}) collective-permute-start(f32[128,512]{1,0:T(8,128)} %bitcast.21), channel_id=1, source_target_pairs={{0,24},{4,28},{8,16},{12,20},{1,25},{5,29},{9,17},{13,21},{2,26},{... | collective-permute-start | bytes 786440 | tf_op jit(solution)/shard_map/ppermute | solution.py:552
  145.0 11.7 %shard_map.121 = (f32[1024,256]{1,0:T(8,128)}, f32[256,128]{1,0:T(8,128)}, f32[256,128]{1,0:T(8,128)}, f32[256,128]{1,0:T(8,128)}, f32[256,128]{1,0:T(8,128)}, /...) custom-call(s32[1]{0:T(128)} %bitcast.tok_ref, s32[7]{0:T(128)} %fork_ref.3, s32[8]{0:T(128)} %live_ref.5, ...), custom_call_target="tpu_custom_call" | custom-call | flops 6442450944 | bytes 524288 | tf_op jit(solution)/shard_map/pallas_call | solution.py:517
  156.7 6.5 %collective-permute-start.22 = (f32[256,128]{1,0:T(8,128)}, f32[256,128]{1,0:T(8,128)S(1)}, u32[]{:S(2)}, u32[]{:S(2)}) collective-permute-start(f32[256,128]{1,0:T(8,128)} %get-tuple-element.115), channel_id=1, source_target_pairs={{0,8},{4,12},{8,0},{12,4},{16,24},{20,28},{24,16},{28,20},{1,9},{5... | collective-permute-start | bytes 393224 | tf_op jit(solution)/shard_map/ppermute | solution.py:542
  163.3 11.0 %collective-permute-start.24 = (f32[256,128]{1,0:T(8,128)}, f32[256,128]{1,0:T(8,128)S(1)}, u32[]{:S(2)}, u32[]{:S(2)}) collective-permute-start(f32[256,128]{1,0:T(8,128)} %get-tuple-element.117), channel_id=1, source_target_pairs={{0,16},{4,20},{8,24},{12,28},{16,0},{20,4},{24,8},{28,12},{1,17},{... | collective-permute-start | bytes 393224 | tf_op jit(solution)/shard_map/ppermute | solution.py:542
  175.4 4.4 %collective-permute-start.23 = (f32[256,128]{1,0:T(8,128)S(1)}, f32[256,128]{1,0:T(8,128)S(1)}, u32[]{:S(2)}, u32[]{:S(2)}) collective-permute-start(f32[256,128]{1,0:T(8,128)S(1)} %add.58), channel_id=1, source_target_pairs={{0,16},{4,20},{8,24},{12,28},{16,0},{20,4},{24,8},{28,12},{1,17},{... | collective-permute-start | bytes 393224 | tf_op jit(solution)/shard_map/ppermute | solution.py:542
  195.8 2.9 %shard_map.125 = (f32[672,128]{1,0:T(8,128)S(1)}, f32[672,128]{1,0:T(8,128)S(1)}) custom-call(s32[4]{0:T(128)S(1)} %iota_xor_fusion.place_ref, bf16[1344,1024]{1,0:T(8,128)(2,1)S(1)} %shard_map.110.refs_0_, bf16[1344,1024]{1,0:T(8,128)(2,1)S(1)} %copy-done.2, f32[4,1024,128]{2,1,0:T(8,128)S(1)} %bitcast.11), custom_call_target="tpu_custom_call" | custom-call | flops 1056964608 | bytes 5505024 | tf_op jit(solution)/shard_map/pallas_call | solution.py:154
  202.1 4.4 %shard_map.124 = (f32[672,128]{1,0:T(8,128)S(1)}, f32[672,128]{1,0:T(8,128)S(1)}, f32[672,128]{1,0:T(8,128)S(1)}, f32[672,128]{1,0:T(8,128)S(1)}) custom-call(s32[4]{0:T(128)S(1)} %iota_xor_fusion.place_ref, bf16[1344,1024]{1,0:T(8,128)(2,1)S(1)} %shard_map.110.refs_0_, bf16[1344,1024]{1,0:T(8,128)(2,1)S(1)} %copy-done.2, f32[4,1024,128]{2,1,0:T(8,128)S(1)} %bitcast.12, ...), custom_call_target="tpu_custom_call" | custom-call | flops 2113929216 | bytes 5505024 | tf_op jit(solution)/shard_map/pallas_call | solution.py:154
  220.3 6.9 %collective-permute-done.32 = f32[672,128]{1,0:T(8,128)S(1)} collective-permute-done((f32[672,128]{1,0:T(8,128)S(1)}, f32[672,128]{1,0:T(8,128)S(1)}, u32[]{:S(2)}, u32[]{:S(2)}) %collective-permute-start.32) | collective-permute-done | bytes 344096 | tf_op jit(solution)/shard_map/ppermute | solution.py:542
  232.6 5.2 %all-gather.5.cloned.1.call-done = f32[4096,128]{1,0:T(8,128)} async-done(((f32[1024,128]{1,0:T(8,128)}), f32[4096,128]{1,0:T(8,128)}) %all-gather.5.cloned.1.call-update) | async-done | bytes 2097168 | tf_op jit(solution)/shard_map/all_gather | solution.py:598
  247.1 4.4 %shard_map.129 = (f32[672,128]{1,0:T(8,128)S(1)}, f32[672,128]{1,0:T(8,128)S(1)}, f32[672,128]{1,0:T(8,128)S(1)}, f32[672,128]{1,0:T(8,128)S(1)}) custom-call(s32[4]{0:T(128)S(1)} %iota_xor_fusion.place_ref, bf16[1344,1024]{1,0:T(8,128)(2,1)S(1)} %shard_map.126.refs_0_, bf16[1344,1024]{1,0:T(8,128)(2,1)S(1)} %copy-done.4, f32[4,1024,128]{2,1,0:T(8,128)S(1)} %bitcast.8, ...), custom_call_target="tpu_custom_call" | custom-call | flops 2113929216 | bytes 5505024 | tf_op jit(solution)/shard_map/pallas_call | solution.py:154
  262.6 3.1 %collective-permute-done.38 = f32[672,128]{1,0:T(8,128)S(1)} collective-permute-done((f32[672,128]{1,0:T(8,128)S(1)}, f32[672,128]{1,0:T(8,128)S(1)}, u32[]{:S(2)}, u32[]{:S(2)}) %collective-permute-start.38) | collective-permute-done | bytes 344096 | tf_op jit(solution)/shard_map/ppermute | solution.py:542
  265.7 4.6 %collective-permute-done.41 = f32[672,128]{1,0:T(8,128)S(1)} collective-permute-done((f32[672,128]{1,0:T(8,128)S(1)}, f32[672,128]{1,0:T(8,128)S(1)}, u32[]{:S(2)}, u32[]{:S(2)}) %collective-permute-start.41) | collective-permute-done | bytes 344096 | tf_op jit(solution)/shard_map/ppermute | solution.py:542
  (171 shorter events, 118.8 us)
Async XLA Ops:
  7.2 80.8 %reduce-scatter.4.cloned.1.call-start = ((), (), s32[]{:S(2)}) async-start(), calls=%async_computation.3 | async-start | bytes 2621440 | tf_op jit(solution)/shard_map/reduce_scatter | solution.py:595
  7.7 18.9 %collective-permute-start.1 = (f32[1344,128]{1,0:T(8,128)}, f32[1344,128]{1,0:T(8,128)}, u32[]{:S(2)}, u32[]{:S(2)}) collective-permute-start(f32[1344,128]{1,0:T(8,128)} %refs_2_.2), channel_id=1, source_target_pairs={{0,8},{4,12},{8,0},{12,4},{16,24},{20,28},{24,16},{28,20},{1,9},{5... | collective-permute-start | bytes 2064392 | tf_op jit(solution)/shard_map/ppermute | solution.py:542
  10.3 17.7 %collective-permute-start.2 = (f32[1344,128]{1,0:T(8,128)}, f32[1344,128]{1,0:T(8,128)S(1)}, u32[]{:S(2)}, u32[]{:S(2)}) collective-permute-start(f32[1344,128]{1,0:T(8,128)} %refs_2_.2), channel_id=1, source_target_pairs={{0,16},{4,20},{8,24},{12,28},{16,0},{20,4},{24,8},{28,12},{1,17},{... | collective-permute-start | bytes 2064392 | tf_op jit(solution)/shard_map/ppermute | solution.py:542
  42.8 75.0 %reduce-scatter.6.cloned.1.call-start = ((), (), s32[]{:S(2)}) async-start(), calls=%async_computation.4 | async-start | bytes 1310720 | tf_op jit(solution)/shard_map/reduce_scatter | solution.py:595
  42.9 15.9 %collective-permute-start.14 = (f32[1344,128]{1,0:T(8,128)S(1)}, f32[1344,128]{1,0:T(8,128)S(1)}, u32[]{:S(2)}, u32[]{:S(2)}) collective-permute-start(f32[1344,128]{1,0:T(8,128)S(1)} %copy-done.12), channel_id=1, source_target_pairs={{0,8},{4,12},{8,0},{12,4},{16,24},{20,28},{24,16},{28,20},{1,9},{5... | collective-permute-start | bytes 2064392 | tf_op jit(solution)/shard_map/ppermute | solution.py:542
  44.3 15.2 %collective-permute-start.15 = (f32[1344,128]{1,0:T(8,128)S(1)}, f32[1344,128]{1,0:T(8,128)S(1)}, u32[]{:S(2)}, u32[]{:S(2)}) collective-permute-start(f32[1344,128]{1,0:T(8,128)S(1)} %copy-done.12), channel_id=1, source_target_pairs={{0,16},{4,20},{8,24},{12,28},{16,0},{20,4},{24,8},{28,12},{1,17},{... | collective-permute-start | bytes 2064392 | tf_op jit(solution)/shard_map/ppermute | solution.py:542
  72.7 72.2 %reduce-scatter.8.cloned.1.call-start = ((), (), s32[]{:S(2)}) async-start(), calls=%async_computation.5 | async-start | bytes 1310720 | tf_op jit(solution)/shard_map/reduce_scatter | solution.py:595
  76.7 115.7 %all-gather.7.cloned.1.call-start = ((), (), s32[]{:S(2)}) async-start(), calls=%async_computation.7 | async-start | bytes 2621440 | tf_op jit(solution)/shard_map/all_gather | solution.py:598
  113.9 23.1 %collective-permute-start.11 = (f32[512,128]{1,0:T(8,128)}, f32[512,128]{1,0:T(8,128)S(1)}, u32[]{:S(2)}, u32[]{:S(2)}) collective-permute-start(f32[512,128]{1,0:T(8,128)} %get-tuple-element.91), channel_id=1, source_target_pairs={{8,0},{12,4},{24,16},{28,20},{9,1},{13,5},{25,17},{29,21},{10,2},{... | collective-permute-start | bytes 786440 | tf_op jit(solution)/shard_map/ppermute | solution.py:552
  115.2 24.3 %collective-permute-start.12 = (f32[512,128]{1,0:T(8,128)}, f32[512,128]{1,0:T(8,128)S(1)}, u32[]{:S(2)}, u32[]{:S(2)}) collective-permute-start(f32[512,128]{1,0:T(8,128)} %get-tuple-element.92), channel_id=1, source_target_pairs={{16,0},{20,4},{24,8},{28,12},{17,1},{21,5},{25,9},{29,13},{18,2},{... | collective-permute-start | bytes 786440 | tf_op jit(solution)/shard_map/ppermute | solution.py:552
  116.5 23.5 %collective-permute-start.13 = (f32[512,128]{1,0:T(8,128)}, f32[512,128]{1,0:T(8,128)S(1)}, u32[]{:S(2)}, u32[]{:S(2)}) collective-permute-start(f32[512,128]{1,0:T(8,128)} %get-tuple-element.93), channel_id=1, source_target_pairs={{16,8},{20,12},{24,0},{28,4},{17,9},{21,13},{25,1},{29,5},{18,10},... | collective-permute-start | bytes 786440 | tf_op jit(solution)/shard_map/ppermute | solution.py:552
  117.8 24.1 %collective-permute-start.20 = (f32[128,512]{1,0:T(8,128)}, f32[128,512]{1,0:T(8,128)}, u32[]{:S(2)}, u32[]{:S(2)}) collective-permute-start(f32[128,512]{1,0:T(8,128)} %bitcast.21), channel_id=1, source_target_pairs={{0,24},{4,28},{8,16},{12,20},{1,25},{5,29},{9,17},{13,21},{2,26},{... | collective-permute-start | bytes 786440 | tf_op jit(solution)/shard_map/ppermute | solution.py:552
  145.0 92.9 %all-gather.5.cloned.1.call-start = ((), (), s32[]{:S(2)}) async-start(), calls=%async_computation.6 | async-start | bytes 2621440 | tf_op jit(solution)/shard_map/all_gather | solution.py:598
  156.7 17.7 %collective-permute-start.22 = (f32[256,128]{1,0:T(8,128)}, f32[256,128]{1,0:T(8,128)S(1)}, u32[]{:S(2)}, u32[]{:S(2)}) collective-permute-start(f32[256,128]{1,0:T(8,128)} %get-tuple-element.115), channel_id=1, source_target_pairs={{0,8},{4,12},{8,0},{12,4},{16,24},{20,28},{24,16},{28,20},{1,9},{5... | collective-permute-start | bytes 393224 | tf_op jit(solution)/shard_map/ppermute | solution.py:542
  163.3 16.5 %collective-permute-start.24 = (f32[256,128]{1,0:T(8,128)}, f32[256,128]{1,0:T(8,128)S(1)}, u32[]{:S(2)}, u32[]{:S(2)}) collective-permute-start(f32[256,128]{1,0:T(8,128)} %get-tuple-element.117), channel_id=1, source_target_pairs={{0,16},{4,20},{8,24},{12,28},{16,0},{20,4},{24,8},{28,12},{1,17},{... | collective-permute-start | bytes 393224 | tf_op jit(solution)/shard_map/ppermute | solution.py:542
  191.1 18.8 %collective-permute-start.33 = (f32[512,256]{1,0:T(8,128)}, f32[512,256]{1,0:T(8,128)S(1)}, u32[]{:S(2)}, u32[]{:S(2)}) collective-permute-start(f32[512,256]{1,0:T(8,128)} %get-tuple-element.150), channel_id=1, source_target_pairs={{0,4},{4,0},{8,12},{12,8},{16,20},{20,16},{24,28},{28,24},{1,5},{5... | collective-permute-start | bytes 1572872 | tf_op jit(solution)/shard_map/ppermute | solution.py:542
  201.8 15.5 %collective-permute-start.34 = (f32[512,128]{1,0:T(8,128)S(1)}, f32[512,128]{1,0:T(8,128)S(1)}, u32[]{:S(2)}, u32[]{:S(2)}) collective-permute-start(f32[512,128]{1,0:T(8,128)S(1)} %get-tuple-element.158), channel_id=1, source_target_pairs={{0,4},{4,0},{8,12},{12,8},{16,20},{20,16},{24,28},{28,24},{1,5},{5... | collective-permute-start | bytes 786440 | tf_op jit(solution)/shard_map/ppermute | solution.py:542
  201.9 13.2 %collective-permute-start.30 = (f32[672,128]{1,0:T(8,128)S(1)}, f32[672,128]{1,0:T(8,128)S(1)}, u32[]{:S(2)}, u32[]{:S(2)}) collective-permute-start(f32[672,128]{1,0:T(8,128)S(1)} %get-tuple-element.127), channel_id=1, source_target_pairs={{0,16},{4,20},{8,24},{12,28},{16,0},{20,4},{24,8},{28,12},{1,17},{... | collective-permute-start | bytes 1032200 | tf_op jit(solution)/shard_map/ppermute | solution.py:542
  206.5 11.7 %collective-permute-start.27 = (f32[672,128]{1,0:T(8,128)S(1)}, f32[672,128]{1,0:T(8,128)S(1)}, u32[]{:S(2)}, u32[]{:S(2)}) collective-permute-start(f32[672,128]{1,0:T(8,128)S(1)} %get-tuple-element.122), channel_id=1, source_target_pairs={{0,8},{4,12},{8,0},{12,4},{16,24},{20,28},{24,16},{28,20},{1,9},{5... | collective-permute-start | bytes 1032200 | tf_op jit(solution)/shard_map/ppermute | solution.py:542
  211.0 16.1 %collective-permute-start.32 = (f32[672,128]{1,0:T(8,128)S(1)}, f32[672,128]{1,0:T(8,128)S(1)}, u32[]{:S(2)}, u32[]{:S(2)}) collective-permute-start(f32[672,128]{1,0:T(8,128)S(1)} %get-tuple-element.128), channel_id=1, source_target_pairs={{0,16},{4,20},{8,24},{12,28},{16,0},{20,4},{24,8},{28,12},{1,17},{... | collective-permute-start | bytes 1032200 | tf_op jit(solution)/shard_map/ppermute | solution.py:542
  215.2 11.9 %collective-permute-start.31 = (f32[672,128]{1,0:T(8,128)S(1)}, f32[672,128]{1,0:T(8,128)S(1)}, u32[]{:S(2)}, u32[]{:S(2)}) collective-permute-start(f32[672,128]{1,0:T(8,128)S(1)} %add.63), channel_id=1, source_target_pairs={{0,8},{4,12},{8,0},{12,4},{16,24},{20,28},{24,16},{28,20},{1,9},{5... | collective-permute-start | bytes 1032200 | tf_op jit(solution)/shard_map/ppermute | solution.py:542
  254.5 11.2 %collective-permute-start.38 = (f32[672,128]{1,0:T(8,128)S(1)}, f32[672,128]{1,0:T(8,128)S(1)}, u32[]{:S(2)}, u32[]{:S(2)}) collective-permute-start(f32[672,128]{1,0:T(8,128)S(1)} %add.67), channel_id=1, source_target_pairs={{0,16},{4,20},{8,24},{12,28},{16,0},{20,4},{24,8},{28,12},{1,17},{... | collective-permute-start | bytes 1032200 | tf_op jit(solution)/shard_map/ppermute | solution.py:542
  256.7 13.7 %collective-permute-start.41 = (f32[672,128]{1,0:T(8,128)S(1)}, f32[672,128]{1,0:T(8,128)S(1)}, u32[]{:S(2)}, u32[]{:S(2)}) collective-permute-start(f32[672,128]{1,0:T(8,128)S(1)} %get-tuple-element.147), channel_id=1, source_target_pairs={{0,16},{4,20},{8,24},{12,28},{16,0},{20,4},{24,8},{28,12},{1,17},{... | collective-permute-start | bytes 1032200 | tf_op jit(solution)/shard_map/ppermute | solution.py:542
  256.8 13.5 %collective-permute-start.40 = (f32[672,128]{1,0:T(8,128)S(1)}, f32[672,128]{1,0:T(8,128)S(1)}, u32[]{:S(2)}, u32[]{:S(2)}) collective-permute-start(f32[672,128]{1,0:T(8,128)S(1)} %add.69), channel_id=1, source_target_pairs={{0,8},{4,12},{8,0},{12,4},{16,24},{20,28},{24,16},{28,20},{1,9},{5... | collective-permute-start | bytes 1032200 | tf_op jit(solution)/shard_map/ppermute | solution.py:542
  (46 other events, 258.8 us)
Sparse Core Ops, SparseCore 0:
  42.9 44.9 reduce-scatter.3
  90.3 26.4 reduce-scatter.5
  119.1 25.7 reduce-scatter.7
  146.5 44.5 all-gather.6
  193.1 44.6 all-gather.4

commit v6 on v5

--- a/solution.py
+++ b/solution.py
@@ -106,7 +106,7 @@
         ),
         out_shape=[jax.ShapeDtypeStruct((place.shape[0], HEAD_DIM, width * len(xs)), f32)] * outs,
         input_output_aliases={inputs + index: index for index in range(len(before))},
-        compiler_params=pltpu.CompilerParams(vmem_limit_bytes=24 * MIB),
+        compiler_params=pltpu.CompilerParams(vmem_limit_bytes=18 * MIB),
         cost_estimate=pl.CostEstimate(
             flops=6 * rows * len(xs) * depth * len(slots) * HEAD_DIM, bytes_accessed=4 * rows * len(xs) * depth, transcendentals=0
         ),
@@ -162,7 +162,7 @@
             scratch_shapes=[pltpu.VMEM((rows * len(xs), 2 * parts * HEAD_DIM), bf16)],
         ),
         out_shape=[jax.ShapeDtypeStruct((block * half, HEAD_DIM), f32)] * (2 * parts),
-        compiler_params=pltpu.CompilerParams(vmem_limit_bytes=24 * MIB),
+        compiler_params=pltpu.CompilerParams(vmem_limit_bytes=10 * MIB),
         cost_estimate=pl.CostEstimate(
             flops=6 * rows * len(xs) * depth * parts * HEAD_DIM, bytes_accessed=4 * rows * len(xs) * depth, transcendentals=0
         ),
@@ -610,7 +610,8 @@
         return combine(own, [flip_one_way(across, 2, False), flip_one_way(down, 4, False), flip_one_way(corner, 6, False)], plan)
 
     def weight(every, xs):
-        corner = weight_grad(place, (3,), xs, every)
+        first = lax.dynamic_index_in_dim(every, place[3], 0, keepdims=True)
+        corner = weight_grad(jnp.zeros_like(place), (0,), xs, first)
         across_head, across_tail, down_head, down_tail = weight_grad(place, (1, 2), xs, every)
         kept = weight_grad(place, (0,), xs, every)
         arrivals = scatter_square((across_head, across_tail), (down_head, down_tail), corner)

time: 279 us -> 278 us (level)
  starting transfers between devices: 85.1 us -> 80.1 us
    unnamed x46 -> x50, local copies, waits for them, and re-layouts: 17.9 us -> 15.7 us
  transfers between devices with their start and end apart: 47 -> 47, of which waited for: 25 -> 25; matrix products, arithmetic and copies ran while one was open for 6% -> 7% of each run, Pallas kernels for 26% -> 26%
where the time goes in v6:
time: 278 us; the launch traced here: 277 us
  starting transfers between devices  80.1 us (29%)
  Pallas kernels  77.1 us (28%)
  waiting for transfers between devices  67.4 us (24%)
  local copies, waits for them, and re-layouts  28.3 us (10%)
  between operations  16.2 us (6%)
  other arithmetic  8.02 us (3%)
    ppermute x36, starting transfers between devices, flip(): lax.ppermute(array, 'tok', [(index, index ^ mask) for index in range(coun...  56.5 us
    ppermute x36, waiting for transfers between devices, flip(): lax.ppermute(array, 'tok', [(index, index ^ mask) for index in range(coun...  51.1 us
    ppermute x6, starting transfers between devices, flip_one_way(): return lax.ppermute(array, 'tok', pairs)  23.2 us
    pallas_call x6, Pallas kernels, project(): pl.pallas_call(functools.partial(project_body, row_inputs=len(xs), pieces...  22.8 us
    pallas_call x6, Pallas kernels, weight_grad(): pl.pallas_call(functools.partial(weight_grad_body, row_inputs=len(xs), pa...  20.2 us
    unnamed x50, local copies, waits for them, and re-layouts  15.7 us
    pallas_call x1, Pallas kernels, grad(): pl.pallas_call(functools.partial(grad_body, conf=key_conf), grid=(steps,)...  11.6 us
    pallas_call x1, Pallas kernels, soft(): pl.pallas_call(functools.partial(soft_body, conf=value_conf), grid=(steps...  9.82 us
  transfers between devices with their start and end apart: 47, of which 25 were waited for; matrix products, arithmetic and copies ran while one was open for 7% of the time, Pallas kernels for 26%

profile of v6, /device:TPU:0, one launch (start us, length us, event | category | flops | bytes accessed | tf_op | source)
XLA Modules:
  0.0 277.1 jit_solution(10904530616779241039)
XLA Ops:
  16.7 2.9 %shard_map.112.refs_4_ = f32[4,128,1024]{2,1,0:T(8,128)S(1)} custom-call(s32[4]{0:T(128)S(1)} %iota_xor_fusion.place_ref, bf16[1344,1024]{1,0:T(8,128)(2,1)S(1)} %shard_map.110.refs_0_, bf16[1344,1024]{1,0:T(8,128)(2,1)S(1)} %shard_map.111.refs_1_, f32[1344,128]{1,0:T(8,128)S(1)} %copy-done.15), custom_call_target="tpu_custom_call" | custom-call | flops 1056964608 | bytes 5505024 | tf_op jit(solution)/shard_map/pallas_call | solution.py:96
  19.6 7.0 %collective-permute-done.1.refs_2_ = f32[1344,128]{1,0:T(8,128)} collective-permute-done((f32[1344,128]{1,0:T(8,128)}, f32[1344,128]{1,0:T(8,128)}, u32[]{:S(2)}, u32[]{:S(2)}) %collective-permute-start.1) | collective-permute-done | bytes 688160 | tf_op jit(solution)/shard_map/ppermute | solution.py:542
  31.2 6.2 %shard_map.113.refs_4_ = f32[4,128,1024]{2,1,0:T(8,128)S(1)} custom-call(s32[4]{0:T(128)S(1)} %iota_xor_fusion.place_ref, bf16[1344,1024]{1,0:T(8,128)(2,1)S(1)} %shard_map.110.refs_0_, bf16[1344,1024]{1,0:T(8,128)(2,1)S(1)} %shard_map.111.refs_1_, f32[1344,128]{1,0:T(8,128)} %collective-permute-done.1.refs_2_, ...), custom_call_target="tpu_custom_call", output_to_operand_aliasing={{}: (5, {})} | custom-call | flops 2113929216 | bytes 5505024 | tf_op jit(solution)/shard_map/pallas_call | solution.py:96
  38.6 2.9 %shard_map.114 = f32[4,128,1024]{2,1,0:T(8,128)S(1)} custom-call(s32[4]{0:T(128)S(1)} %iota_xor_fusion.place_ref, bf16[1344,1024]{1,0:T(8,128)(2,1)S(1)} %shard_map.110.refs_0_, bf16[1344,1024]{1,0:T(8,128)(2,1)S(1)} %shard_map.111.refs_1_, f32[640,128]{1,0:T(8,128)S(1)} %collective-permute-done.3.refs_2_, ...), custom_call_target="tpu_custom_call", output_to_operand_aliasing={{}: (5, {})} | custom-call | flops 1056964608 | bytes 5505024 | tf_op jit(solution)/shard_map/pallas_call | solution.py:96
  48.4 2.9 %shard_map.118 = (f32[4,128,512]{2,1,0:T(8,128)S(1)}, f32[4,128,512]{2,1,0:T(8,128)S(1)}) custom-call(s32[4]{0:T(128)S(1)} %iota_xor_fusion.place_ref, bf16[1344,1024]{1,0:T(8,128)(2,1)S(1)} %shard_map.110.refs_0_, bf16[1344,1024]{1,0:T(8,128)(2,1)S(1)} %copy-done.1, f32[1344,128]{1,0:T(8,128)S(1)} %copy-done.14), custom_call_target="tpu_custom_call" | custom-call | flops 1056964608 | bytes 5505024 | tf_op jit(solution)/shard_map/pallas_call | solution.py:96
  51.3 8.3 %collective-permute-done.14.refs_2_ = f32[1344,128]{1,0:T(8,128)S(1)} collective-permute-done((f32[1344,128]{1,0:T(8,128)S(1)}, f32[1344,128]{1,0:T(8,128)S(1)}, u32[]{:S(2)}, u32[]{:S(2)}) %collective-permute-start.14) | collective-permute-done | bytes 688160 | tf_op jit(solution)/shard_map/ppermute | solution.py:542
  62.9 5.1 %shard_map.119 = (f32[4,128,512]{2,1,0:T(8,128)S(1)}, f32[4,128,512]{2,1,0:T(8,128)S(1)}) custom-call(s32[4]{0:T(128)S(1)} %iota_xor_fusion.place_ref, bf16[1344,1024]{1,0:T(8,128)(2,1)S(1)} %shard_map.110.refs_0_, bf16[1344,1024]{1,0:T(8,128)(2,1)S(1)} %copy-done.1, ...), custom_call_target="tpu_custom_call", output_to_operand_aliasing={{0}: (5, {}), {1}: (6, {})} | custom-call | flops 2113929216 | bytes 5505024 | tf_op jit(solution)/shard_map/pallas_call | solution.py:96
  68.7 2.9 %shard_map.120 = (f32[4,128,512]{2,1,0:T(8,128)S(1)}, f32[4,128,512]{2,1,0:T(8,128)S(1)}) custom-call(s32[4]{0:T(128)S(1)} %iota_xor_fusion.place_ref, bf16[1344,1024]{1,0:T(8,128)(2,1)S(1)} %shard_map.110.refs_0_, bf16[1344,1024]{1,0:T(8,128)(2,1)S(1)} %copy-done.1, ...), custom_call_target="tpu_custom_call", output_to_operand_aliasing={{0}: (5, {}), {1}: (6, {})} | custom-call | flops 1056964608 | bytes 5505024 | tf_op jit(solution)/shard_map/pallas_call | solution.py:96
  79.5 4.8 %shard_map.115 = (bf16[4,512,512]{2,1,0:T(8,128)(2,1)}, bf16[4,512,256]{2,1,0:T(8,128)(2,1)}, bf16[4,512,512]{2,1,0:T(8,128)(2,1)}, bf16[4,512,256]{2,1,0:T(8,128)(2,1)}) custom-call(s32[1]{0:T(128)} %bitcast.tok_ref, s32[8]{0:T(128)} %live_ref.5, f32[512,256]{1,0:T(8,128)} %get-tuple-element.154.refs_0_, f32[512,256]{1,0:T(8,128)} %copy-done.22, ...), custom_call_target="tpu_custom_call" | custom-call | flops 2097152 | bytes 4194304 | tf_op jit(solution)/shard_map/pallas_call | solution.py:489
  84.2 3.6 %reduce-scatter.4.cloned.1.call-done = f32[1,128,1024]{2,1,0:T(8,128)} async-done(((f32[4,128,1024]{2,1,0:T(8,128)}), f32[1,128,1024]{2,1,0:T(8,128)}) %reduce-scatter.4.cloned.1.call-update) | async-done | bytes 524304 | tf_op jit(solution)/shard_map/reduce_scatter | solution.py:595
  91.9 4.9 %collective-permute-done.8.refs_4_ = f32[128,512]{1,0:T(8,128)S(1)} collective-permute-done((f32[128,512]{1,0:T(8,128)S(1)}, f32[128,512]{1,0:T(8,128)S(1)}, u32[]{:S(2)}, u32[]{:S(2)}) %collective-permute-start.8) | collective-permute-done | bytes 262176 | tf_op jit(solution)/shard_map/ppermute | solution.py:542
  104.1 9.8 %shard_map.116 = (f32[4,2560,512]{2,1,0:T(8,128)}, f32[512,128]{1,0:T(8,128)}, f32[512,128]{1,0:T(8,128)}, f32[512,128]{1,0:T(8,128)}, f32[1024,128]{1,0:T(8,128)}) custom-call(s32[1]{0:T(128)} %bitcast.tok_ref, s32[7]{0:T(128)} %fork_ref.3, s32[8]{0:T(128)} %live_ref.5, bf16[4,512,512]{2,1,0:T(8,128)(2,1)} %get-tuple-element.87.refs_0_, ...), custom_call_target="tpu_custom_call" | custom-call | flops 3221225472 | bytes 524288 | tf_op jit(solution)/shard_map/pallas_call | solution.py:501
  117.8 14.9 %collective-permute-start.20 = (f32[128,512]{1,0:T(8,128)}, f32[128,512]{1,0:T(8,128)}, u32[]{:S(2)}, u32[]{:S(2)}) collective-permute-start(f32[128,512]{1,0:T(8,128)} %bitcast.22), channel_id=1, source_target_pairs={{0,24},{4,28},{8,16},{12,20},{1,25},{5,29},{9,17},{13,21},{2,26},{... | collective-permute-start | bytes 786440 | tf_op jit(solution)/shard_map/ppermute | solution.py:552
  141.8 3.1 %reduce-scatter.8.cloned.1.call-done = f32[1,128,512]{2,1,0:T(8,128)} async-done(((f32[4,128,512]{2,1,0:T(8,128)}), f32[1,128,512]{2,1,0:T(8,128)}) %reduce-scatter.8.cloned.1.call-update) | async-done | bytes 262160 | tf_op jit(solution)/shard_map/reduce_scatter | solution.py:595
  144.9 11.6 %shard_map.121 = (f32[1024,256]{1,0:T(8,128)}, f32[256,128]{1,0:T(8,128)}, f32[256,128]{1,0:T(8,128)}, f32[256,128]{1,0:T(8,128)}, f32[256,128]{1,0:T(8,128)}, /...) custom-call(s32[1]{0:T(128)} %bitcast.tok_ref, s32[7]{0:T(128)} %fork_ref.3, s32[8]{0:T(128)} %live_ref.5, ...), custom_call_target="tpu_custom_call" | custom-call | flops 6442450944 | bytes 524288 | tf_op jit(solution)/shard_map/pallas_call | solution.py:517
  156.6 6.3 %collective-permute-start.22 = (f32[256,128]{1,0:T(8,128)}, f32[256,128]{1,0:T(8,128)S(1)}, u32[]{:S(2)}, u32[]{:S(2)}) collective-permute-start(f32[256,128]{1,0:T(8,128)} %get-tuple-element.115), channel_id=1, source_target_pairs={{0,8},{4,12},{8,0},{12,4},{16,24},{20,28},{24,16},{28,20},{1,9},{5... | collective-permute-start | bytes 393224 | tf_op jit(solution)/shard_map/ppermute | solution.py:542
  162.9 8.7 %collective-permute-start.24 = (f32[256,128]{1,0:T(8,128)}, f32[256,128]{1,0:T(8,128)S(1)}, u32[]{:S(2)}, u32[]{:S(2)}) collective-permute-start(f32[256,128]{1,0:T(8,128)} %get-tuple-element.117), channel_id=1, source_target_pairs={{0,16},{4,20},{8,24},{12,28},{16,0},{20,4},{24,8},{28,12},{1,17},{... | collective-permute-start | bytes 393224 | tf_op jit(solution)/shard_map/ppermute | solution.py:542
  172.6 4.5 %collective-permute-start.23 = (f32[256,128]{1,0:T(8,128)S(1)}, f32[256,128]{1,0:T(8,128)S(1)}, u32[]{:S(2)}, u32[]{:S(2)}) collective-permute-start(f32[256,128]{1,0:T(8,128)S(1)} %add.63), channel_id=1, source_target_pairs={{0,16},{4,20},{8,24},{12,28},{16,0},{20,4},{24,8},{28,12},{1,17},{... | collective-permute-start | bytes 393224 | tf_op jit(solution)/shard_map/ppermute | solution.py:542
  201.3 4.4 %shard_map.124 = (f32[672,128]{1,0:T(8,128)S(1)}, f32[672,128]{1,0:T(8,128)S(1)}, f32[672,128]{1,0:T(8,128)S(1)}, f32[672,128]{1,0:T(8,128)S(1)}) custom-call(s32[4]{0:T(128)S(1)} %iota_xor_fusion.place_ref, bf16[1344,1024]{1,0:T(8,128)(2,1)S(1)} %shard_map.110.refs_0_, bf16[1344,1024]{1,0:T(8,128)(2,1)S(1)} %copy-done.3, f32[4,1024,128]{2,1,0:T(8,128)S(1)} %bitcast.13, ...), custom_call_target="tpu_custom_call" | custom-call | flops 2113929216 | bytes 5505024 | tf_op jit(solution)/shard_map/pallas_call | solution.py:154
  219.4 5.9 %collective-permute-done.32 = f32[672,128]{1,0:T(8,128)S(1)} collective-permute-done((f32[672,128]{1,0:T(8,128)S(1)}, f32[672,128]{1,0:T(8,128)S(1)}, u32[]{:S(2)}, u32[]{:S(2)}) %collective-permute-start.32) | collective-permute-done | bytes 344096 | tf_op jit(solution)/shard_map/ppermute | solution.py:542
  230.8 6.8 %all-gather.5.cloned.1.call-done = f32[4096,128]{1,0:T(8,128)} async-done(((f32[1024,128]{1,0:T(8,128)}), f32[4096,128]{1,0:T(8,128)}) %all-gather.5.cloned.1.call-update) | async-done | bytes 2097168 | tf_op jit(solution)/shard_map/all_gather | solution.py:598
  246.6 4.4 %shard_map.129 = (f32[672,128]{1,0:T(8,128)S(1)}, f32[672,128]{1,0:T(8,128)S(1)}, f32[672,128]{1,0:T(8,128)S(1)}, f32[672,128]{1,0:T(8,128)S(1)}) custom-call(s32[4]{0:T(128)S(1)} %iota_xor_fusion.place_ref, bf16[1344,1024]{1,0:T(8,128)(2,1)S(1)} %shard_map.126.refs_0_, bf16[1344,1024]{1,0:T(8,128)(2,1)S(1)} %copy-done.6, f32[4,1024,128]{2,1,0:T(8,128)S(1)} %bitcast.9, ...), custom_call_target="tpu_custom_call" | custom-call | flops 2113929216 | bytes 5505024 | tf_op jit(solution)/shard_map/pallas_call | solution.py:154
  262.1 2.9 %collective-permute-done.38 = f32[672,128]{1,0:T(8,128)S(1)} collective-permute-done((f32[672,128]{1,0:T(8,128)S(1)}, f32[672,128]{1,0:T(8,128)S(1)}, u32[]{:S(2)}, u32[]{:S(2)}) %collective-permute-start.38) | collective-permute-done | bytes 344096 | tf_op jit(solution)/shard_map/ppermute | solution.py:542
  265.0 4.6 %collective-permute-done.41 = f32[672,128]{1,0:T(8,128)S(1)} collective-permute-done((f32[672,128]{1,0:T(8,128)S(1)}, f32[672,128]{1,0:T(8,128)S(1)}, u32[]{:S(2)}, u32[]{:S(2)}) %collective-permute-start.41) | collective-permute-done | bytes 344096 | tf_op jit(solution)/shard_map/ppermute | solution.py:542
  (179 shorter events, 121.7 us)
Async XLA Ops:
  7.2 80.7 %reduce-scatter.4.cloned.1.call-start = ((), (), s32[]{:S(2)}) async-start(), calls=%async_computation.3 | async-start | bytes 2621440 | tf_op jit(solution)/shard_map/reduce_scatter | solution.py:595
  7.7 18.9 %collective-permute-start.1 = (f32[1344,128]{1,0:T(8,128)}, f32[1344,128]{1,0:T(8,128)}, u32[]{:S(2)}, u32[]{:S(2)}) collective-permute-start(f32[1344,128]{1,0:T(8,128)} %refs_2_.2), channel_id=1, source_target_pairs={{0,8},{4,12},{8,0},{12,4},{16,24},{20,28},{24,16},{28,20},{1,9},{5... | collective-permute-start | bytes 2064392 | tf_op jit(solution)/shard_map/ppermute | solution.py:542
  10.3 17.7 %collective-permute-start.2 = (f32[1344,128]{1,0:T(8,128)}, f32[1344,128]{1,0:T(8,128)S(1)}, u32[]{:S(2)}, u32[]{:S(2)}) collective-permute-start(f32[1344,128]{1,0:T(8,128)} %refs_2_.2), channel_id=1, source_target_pairs={{0,16},{4,20},{8,24},{12,28},{16,0},{20,4},{24,8},{28,12},{1,17},{... | collective-permute-start | bytes 2064392 | tf_op jit(solution)/shard_map/ppermute | solution.py:542
  42.8 75.0 %reduce-scatter.6.cloned.1.call-start = ((), (), s32[]{:S(2)}) async-start(), calls=%async_computation.4 | async-start | bytes 1310720 | tf_op jit(solution)/shard_map/reduce_scatter | solution.py:595
  43.8 15.8 %collective-permute-start.14 = (f32[1344,128]{1,0:T(8,128)S(1)}, f32[1344,128]{1,0:T(8,128)S(1)}, u32[]{:S(2)}, u32[]{:S(2)}) collective-permute-start(f32[1344,128]{1,0:T(8,128)S(1)} %copy-done.14), channel_id=1, source_target_pairs={{0,8},{4,12},{8,0},{12,4},{16,24},{20,28},{24,16},{28,20},{1,9},{5... | collective-permute-start | bytes 2064392 | tf_op jit(solution)/shard_map/ppermute | solution.py:542
  45.1 15.2 %collective-permute-start.15 = (f32[1344,128]{1,0:T(8,128)S(1)}, f32[1344,128]{1,0:T(8,128)S(1)}, u32[]{:S(2)}, u32[]{:S(2)}) collective-permute-start(f32[1344,128]{1,0:T(8,128)S(1)} %copy-done.14), channel_id=1, source_target_pairs={{0,16},{4,20},{8,24},{12,28},{16,0},{20,4},{24,8},{28,12},{1,17},{... | collective-permute-start | bytes 2064392 | tf_op jit(solution)/shard_map/ppermute | solution.py:542
  73.6 71.3 %reduce-scatter.8.cloned.1.call-start = ((), (), s32[]{:S(2)}) async-start(), calls=%async_computation.5 | async-start | bytes 1310720 | tf_op jit(solution)/shard_map/reduce_scatter | solution.py:595
  77.6 114.7 %all-gather.7.cloned.1.call-start = ((), (), s32[]{:S(2)}) async-start(), calls=%async_computation.7 | async-start | bytes 2621440 | tf_op jit(solution)/shard_map/all_gather | solution.py:598
  113.9 20.8 %collective-permute-start.11 = (f32[512,128]{1,0:T(8,128)}, f32[512,128]{1,0:T(8,128)S(1)}, u32[]{:S(2)}, u32[]{:S(2)}) collective-permute-start(f32[512,128]{1,0:T(8,128)} %get-tuple-element.91), channel_id=1, source_target_pairs={{8,0},{12,4},{24,16},{28,20},{9,1},{13,5},{25,17},{29,21},{10,2},{... | collective-permute-start | bytes 786440 | tf_op jit(solution)/shard_map/ppermute | solution.py:552
  115.2 22.0 %collective-permute-start.12 = (f32[512,128]{1,0:T(8,128)}, f32[512,128]{1,0:T(8,128)S(1)}, u32[]{:S(2)}, u32[]{:S(2)}) collective-permute-start(f32[512,128]{1,0:T(8,128)} %get-tuple-element.92), channel_id=1, source_target_pairs={{16,0},{20,4},{24,8},{28,12},{17,1},{21,5},{25,9},{29,13},{18,2},{... | collective-permute-start | bytes 786440 | tf_op jit(solution)/shard_map/ppermute | solution.py:552
  116.5 21.2 %collective-permute-start.13 = (f32[512,128]{1,0:T(8,128)}, f32[512,128]{1,0:T(8,128)S(1)}, u32[]{:S(2)}, u32[]{:S(2)}) collective-permute-start(f32[512,128]{1,0:T(8,128)} %get-tuple-element.93), channel_id=1, source_target_pairs={{16,8},{20,12},{24,0},{28,4},{17,9},{21,13},{25,1},{29,5},{18,10},... | collective-permute-start | bytes 786440 | tf_op jit(solution)/shard_map/ppermute | solution.py:552
  117.8 21.8 %collective-permute-start.20 = (f32[128,512]{1,0:T(8,128)}, f32[128,512]{1,0:T(8,128)}, u32[]{:S(2)}, u32[]{:S(2)}) collective-permute-start(f32[128,512]{1,0:T(8,128)} %bitcast.22), channel_id=1, source_target_pairs={{0,24},{4,28},{8,16},{12,20},{1,25},{5,29},{9,17},{13,21},{2,26},{... | collective-permute-start | bytes 786440 | tf_op jit(solution)/shard_map/ppermute | solution.py:552
  144.9 92.8 %all-gather.5.cloned.1.call-start = ((), (), s32[]{:S(2)}) async-start(), calls=%async_computation.6 | async-start | bytes 2621440 | tf_op jit(solution)/shard_map/all_gather | solution.py:598
  156.6 15.1 %collective-permute-start.22 = (f32[256,128]{1,0:T(8,128)}, f32[256,128]{1,0:T(8,128)S(1)}, u32[]{:S(2)}, u32[]{:S(2)}) collective-permute-start(f32[256,128]{1,0:T(8,128)} %get-tuple-element.115), channel_id=1, source_target_pairs={{0,8},{4,12},{8,0},{12,4},{16,24},{20,28},{24,16},{28,20},{1,9},{5... | collective-permute-start | bytes 393224 | tf_op jit(solution)/shard_map/ppermute | solution.py:542
  162.9 14.2 %collective-permute-start.24 = (f32[256,128]{1,0:T(8,128)}, f32[256,128]{1,0:T(8,128)S(1)}, u32[]{:S(2)}, u32[]{:S(2)}) collective-permute-start(f32[256,128]{1,0:T(8,128)} %get-tuple-element.117), channel_id=1, source_target_pairs={{0,16},{4,20},{8,24},{12,28},{16,0},{20,4},{24,8},{28,12},{1,17},{... | collective-permute-start | bytes 393224 | tf_op jit(solution)/shard_map/ppermute | solution.py:542
  190.9 18.0 %collective-permute-start.33 = (f32[512,256]{1,0:T(8,128)}, f32[512,256]{1,0:T(8,128)}, u32[]{:S(2)}, u32[]{:S(2)}) collective-permute-start(f32[512,256]{1,0:T(8,128)} %get-tuple-element.150), channel_id=1, source_target_pairs={{0,4},{4,0},{8,12},{12,8},{16,20},{20,16},{24,28},{28,24},{1,5},{5... | collective-permute-start | bytes 1572872 | tf_op jit(solution)/shard_map/ppermute | solution.py:542
  200.0 15.6 %collective-permute-start.30 = (f32[672,128]{1,0:T(8,128)S(1)}, f32[672,128]{1,0:T(8,128)S(1)}, u32[]{:S(2)}, u32[]{:S(2)}) collective-permute-start(f32[672,128]{1,0:T(8,128)S(1)} %get-tuple-element.127), channel_id=1, source_target_pairs={{0,16},{4,20},{8,24},{12,28},{16,0},{20,4},{24,8},{28,12},{1,17},{... | collective-permute-start | bytes 1032200 | tf_op jit(solution)/shard_map/ppermute | solution.py:542
  201.2 16.7 %collective-permute-start.34 = (f32[512,128]{1,0:T(8,128)S(1)}, f32[512,128]{1,0:T(8,128)S(1)}, u32[]{:S(2)}, u32[]{:S(2)}) collective-permute-start(f32[512,128]{1,0:T(8,128)S(1)} %get-tuple-element.158), channel_id=1, source_target_pairs={{0,4},{4,0},{8,12},{12,8},{16,20},{20,16},{24,28},{28,24},{1,5},{5... | collective-permute-start | bytes 786440 | tf_op jit(solution)/shard_map/ppermute | solution.py:542
  205.7 13.0 %collective-permute-start.27 = (f32[672,128]{1,0:T(8,128)S(1)}, f32[672,128]{1,0:T(8,128)S(1)}, u32[]{:S(2)}, u32[]{:S(2)}) collective-permute-start(f32[672,128]{1,0:T(8,128)S(1)} %get-tuple-element.122), channel_id=1, source_target_pairs={{0,8},{4,12},{8,0},{12,4},{16,24},{20,28},{24,16},{28,20},{1,9},{5... | collective-permute-start | bytes 1032200 | tf_op jit(solution)/shard_map/ppermute | solution.py:542
  211.3 14.0 %collective-permute-start.32 = (f32[672,128]{1,0:T(8,128)S(1)}, f32[672,128]{1,0:T(8,128)S(1)}, u32[]{:S(2)}, u32[]{:S(2)}) collective-permute-start(f32[672,128]{1,0:T(8,128)S(1)} %get-tuple-element.128), channel_id=1, source_target_pairs={{0,16},{4,20},{8,24},{12,28},{16,0},{20,4},{24,8},{28,12},{1,17},{... | collective-permute-start | bytes 1032200 | tf_op jit(solution)/shard_map/ppermute | solution.py:542
  244.9 11.1 %collective-permute-start.39 = (f32[672,128]{1,0:T(8,128)S(1)}, f32[672,128]{1,0:T(8,128)S(1)}, u32[]{:S(2)}, u32[]{:S(2)}) collective-permute-start(f32[672,128]{1,0:T(8,128)S(1)} %get-tuple-element.146), channel_id=1, source_target_pairs={{0,16},{4,20},{8,24},{12,28},{16,0},{20,4},{24,8},{28,12},{1,17},{... | collective-permute-start | bytes 1032200 | tf_op jit(solution)/shard_map/ppermute | solution.py:542
  253.5 11.4 %collective-permute-start.38 = (f32[672,128]{1,0:T(8,128)S(1)}, f32[672,128]{1,0:T(8,128)S(1)}, u32[]{:S(2)}, u32[]{:S(2)}) collective-permute-start(f32[672,128]{1,0:T(8,128)S(1)} %add.73), channel_id=1, source_target_pairs={{0,16},{4,20},{8,24},{12,28},{16,0},{20,4},{24,8},{28,12},{1,17},{... | collective-permute-start | bytes 1032200 | tf_op jit(solution)/shard_map/ppermute | solution.py:542
  256.0 13.7 %collective-permute-start.41 = (f32[672,128]{1,0:T(8,128)S(1)}, f32[672,128]{1,0:T(8,128)S(1)}, u32[]{:S(2)}, u32[]{:S(2)}) collective-permute-start(f32[672,128]{1,0:T(8,128)S(1)} %get-tuple-element.147), channel_id=1, source_target_pairs={{0,16},{4,20},{8,24},{12,28},{16,0},{20,4},{24,8},{28,12},{1,17},{... | collective-permute-start | bytes 1032200 | tf_op jit(solution)/shard_map/ppermute | solution.py:542
  256.1 13.5 %collective-permute-start.40 = (f32[672,128]{1,0:T(8,128)S(1)}, f32[672,128]{1,0:T(8,128)S(1)}, u32[]{:S(2)}, u32[]{:S(2)}) collective-permute-start(f32[672,128]{1,0:T(8,128)S(1)} %add.75), channel_id=1, source_target_pairs={{0,8},{4,12},{8,0},{12,4},{16,24},{20,28},{24,16},{28,20},{1,9},{5... | collective-permute-start | bytes 1032200 | tf_op jit(solution)/shard_map/ppermute | solution.py:542
  (48 other events, 268.9 us)
Sparse Core Ops, SparseCore 0:
  42.9 44.9 reduce-scatter.3
  90.2 26.4 reduce-scatter.5
  119.0 25.7 reduce-scatter.7
  146.4 44.5 all-gather.6
  193.1 44.5 all-gather.4

commit v7 on v6

--- a/solution.py
+++ b/solution.py
@@ -142,7 +142,7 @@
     depth, rows = xs[0].shape
     rows = rows // 2
     parts = len(slots)
-    steps = 4
+    steps = 2
     half = steps // 2
     block = depth // steps
 
@@ -162,7 +162,7 @@
             scratch_shapes=[pltpu.VMEM((rows * len(xs), 2 * parts * HEAD_DIM), bf16)],
         ),
         out_shape=[jax.ShapeDtypeStruct((block * half, HEAD_DIM), f32)] * (2 * parts),
-        compiler_params=pltpu.CompilerParams(vmem_limit_bytes=10 * MIB),
+        compiler_params=pltpu.CompilerParams(vmem_limit_bytes=16 * MIB),
         cost_estimate=pl.CostEstimate(
             flops=6 * rows * len(xs) * depth * parts * HEAD_DIM, bytes_accessed=4 * rows * len(xs) * depth, transcendentals=0
         ),
@@ -600,11 +600,6 @@
     def lead(array):
         return jnp.concatenate([array[:, :SPAN], array[:, rows : rows + SPAN]], axis=1)
 
-    def returned(across_head, across_tail, down_head, down_tail, corner_head, corner_tail, own):
-        arrivals = scatter_square((across_head, across_tail), (down_head, down_tail), (corner_head, corner_tail))
-        plan = tuple((index, 0, rows * (index // 2), SPAN) for index in range(4))
-        return combine(own, arrivals, plan)
-
     def returned_at_once(across, down, corner, own):
         plan = tuple((index, slot * SPAN, slot * rows, SPAN) for index in range(3) for slot in range(2))
         return combine(own, [flip_one_way(across, 2, False), flip_one_way(down, 4, False), flip_one_way(corner, 6, False)], plan)
@@ -653,9 +648,8 @@
         (3, 0, 4 * SPAN, 2 * SPAN),
         (4, 0, 6 * SPAN, 2 * SPAN),
     )
-    key_sum_rows = tuple((0, (2 + index) * SPAN, SPAN) for index in range(6))
     value_sum_rows = tuple((0, 2 * (1 + index) * SPAN, 2 * SPAN) for index in range(3))
-    stage, soft, grad = attention_calls(scalars, qs, gs, layout, value_layout, key_sum_rows, value_sum_rows, True, owners)
+    stage, soft, grad = attention_calls(scalars, qs, gs, layout, value_layout, value_sum_rows, value_sum_rows, True, owners)
 
     keys, *staged = together(keys, *stage())
     key_parts = [keys, *gather_square(lead(keys), SPAN, 1)]
@@ -668,7 +662,7 @@
     every_value = all_heads(value_grads)
     value_parts = [value_parts[0], trailing, *value_parts[1:]]
     grad_query, *key_sums = grad(staged, key_parts, value_parts, probs)
-    key_grads = returned(*key_sums)
+    key_grads = returned_at_once(*key_sums)
     every_key = all_heads(key_grads)
     every_value, key_grads = together(every_value, key_grads)
     grad_w_value = finish(*weight(every_value, xs))

time: 278 us -> 278 us (level)
  waiting for transfers between devices: 67.4 us -> 92.3 us
  starting transfers between devices: 80.1 us -> 59 us
    ppermute x36 -> x30, starting transfers between devices: 56.5 us -> 31.3 us  [flip(): lax.ppermute(array, 'tok', [(index, index ^ mask) for index in range(coun...]
    ppermute x6 -> x9, waiting for transfers between devices: 2.69 us -> 26.1 us  [flip_one_way(): return lax.ppermute(array, 'tok', pairs)]
    ppermute x6 -> x9, starting transfers between devices: 23.2 us -> 27.3 us  [flip_one_way(): return lax.ppermute(array, 'tok', pairs)]
    ppermute x36 -> x30, waiting for transfers between devices: 51.1 us -> 52.6 us  [flip(): lax.ppermute(array, 'tok', [(index, index ^ mask) for index in range(coun...]
  transfers between devices with their start and end apart: 47 -> 44, of which waited for: 25 -> 26; matrix products, arithmetic and copies ran while one was open for 7% -> 6% of each run, Pallas kernels for 26% -> 25%
where the time goes in v7:
time: 278 us; the launch traced here: 277 us
  waiting for transfers between devices  92.3 us (33%)
  Pallas kernels  74.7 us (27%)
  starting transfers between devices  59 us (21%)
  local copies, waits for them, and re-layouts  28.2 us (10%)
  between operations  16.3 us (6%)
  other arithmetic  6.19 us (2%)
    ppermute x30, waiting for transfers between devices, flip(): lax.ppermute(array, 'tok', [(index, index ^ mask) for index in range(coun...  52.6 us
    ppermute x30, starting transfers between devices, flip(): lax.ppermute(array, 'tok', [(index, index ^ mask) for index in range(coun...  31.3 us
    ppermute x9, starting transfers between devices, flip_one_way(): return lax.ppermute(array, 'tok', pairs)  27.3 us
    ppermute x9, waiting for transfers between devices, flip_one_way(): return lax.ppermute(array, 'tok', pairs)  26.1 us
    pallas_call x6, Pallas kernels, project(): pl.pallas_call(functools.partial(project_body, row_inputs=len(xs), pieces...  22.8 us
    pallas_call x6, Pallas kernels, weight_grad(): pl.pallas_call(functools.partial(weight_grad_body, row_inputs=len(xs), pa...  17.8 us
    unnamed x50, local copies, waits for them, and re-layouts  15.7 us
    pallas_call x1, Pallas kernels, grad(): pl.pallas_call(functools.partial(grad_body, conf=key_conf), grid=(steps,)...  11.6 us
  transfers between devices with their start and end apart: 44, of which 26 were waited for; matrix products, arithmetic and copies ran while one was open for 6% of the time, Pallas kernels for 25%

profile of v7, /device:TPU:0, one launch (start us, length us, event | category | flops | bytes accessed | tf_op | source)
XLA Modules:
  0.0 276.7 jit_solution(8692797437540825021)
XLA Ops:
  19.6 7.0 %collective-permute-done.1.refs_2_ = f32[1344,128]{1,0:T(8,128)} collective-permute-done((f32[1344,128]{1,0:T(8,128)}, f32[1344,128]{1,0:T(8,128)}, u32[]{:S(2)}, u32[]{:S(2)}) %collective-permute-start.1) | collective-permute-done | bytes 688160 | tf_op jit(solution)/shard_map/ppermute | solution.py:542
  31.2 6.2 %shard_map.113.refs_4_ = f32[4,128,1024]{2,1,0:T(8,128)S(1)} custom-call(s32[4]{0:T(128)S(1)} %iota_xor_fusion.place_ref, bf16[1344,1024]{1,0:T(8,128)(2,1)S(1)} %shard_map.110.refs_0_, bf16[1344,1024]{1,0:T(8,128)(2,1)S(1)} %shard_map.111.refs_1_, f32[1344,128]{1,0:T(8,128)} %collective-permute-done.1.refs_2_, ...), custom_call_target="tpu_custom_call", output_to_operand_aliasing={{}: (5, {})} | custom-call | flops 2113929216 | bytes 5505024 | tf_op jit(solution)/shard_map/pallas_call | solution.py:96
  51.3 8.3 %collective-permute-done.14.refs_2_ = f32[1344,128]{1,0:T(8,128)S(1)} collective-permute-done((f32[1344,128]{1,0:T(8,128)S(1)}, f32[1344,128]{1,0:T(8,128)S(1)}, u32[]{:S(2)}, u32[]{:S(2)}) %collective-permute-start.14) | collective-permute-done | bytes 688160 | tf_op jit(solution)/shard_map/ppermute | solution.py:542
  62.9 5.1 %shard_map.119 = (f32[4,128,512]{2,1,0:T(8,128)S(1)}, f32[4,128,512]{2,1,0:T(8,128)S(1)}) custom-call(s32[4]{0:T(128)S(1)} %iota_xor_fusion.place_ref, bf16[1344,1024]{1,0:T(8,128)(2,1)S(1)} %shard_map.110.refs_0_, bf16[1344,1024]{1,0:T(8,128)(2,1)S(1)} %copy-done.1, ...), custom_call_target="tpu_custom_call", output_to_operand_aliasing={{0}: (5, {}), {1}: (6, {})} | custom-call | flops 2113929216 | bytes 5505024 | tf_op jit(solution)/shard_map/pallas_call | solution.py:96
  68.7 2.9 %shard_map.120 = (f32[4,128,512]{2,1,0:T(8,128)S(1)}, f32[4,128,512]{2,1,0:T(8,128)S(1)}) custom-call(s32[4]{0:T(128)S(1)} %iota_xor_fusion.place_ref, bf16[1344,1024]{1,0:T(8,128)(2,1)S(1)} %shard_map.110.refs_0_, bf16[1344,1024]{1,0:T(8,128)(2,1)S(1)} %copy-done.1, ...), custom_call_target="tpu_custom_call", output_to_operand_aliasing={{0}: (5, {}), {1}: (6, {})} | custom-call | flops 1056964608 | bytes 5505024 | tf_op jit(solution)/shard_map/pallas_call | solution.py:96
  79.4 4.8 %shard_map.115 = (bf16[4,512,512]{2,1,0:T(8,128)(2,1)}, bf16[4,512,256]{2,1,0:T(8,128)(2,1)}, bf16[4,512,512]{2,1,0:T(8,128)(2,1)}, bf16[4,512,256]{2,1,0:T(8,128)(2,1)}) custom-call(s32[1]{0:T(128)} %bitcast.tok_ref, s32[8]{0:T(128)} %live_ref.5, f32[512,256]{1,0:T(8,128)} %get-tuple-element.148.refs_0_, f32[512,256]{1,0:T(8,128)} %copy-done.22, ...), custom_call_target="tpu_custom_call" | custom-call | flops 2097152 | bytes 4194304 | tf_op jit(solution)/shard_map/pallas_call | solution.py:489
  84.2 3.7 %reduce-scatter.4.cloned.1.call-done = f32[1,128,1024]{2,1,0:T(8,128)} async-done(((f32[4,128,1024]{2,1,0:T(8,128)}), f32[1,128,1024]{2,1,0:T(8,128)}) %reduce-scatter.4.cloned.1.call-update) | async-done | bytes 524304 | tf_op jit(solution)/shard_map/reduce_scatter | solution.py:595
  91.9 4.9 %collective-permute-done.8.refs_4_ = f32[128,512]{1,0:T(8,128)S(1)} collective-permute-done((f32[128,512]{1,0:T(8,128)S(1)}, f32[128,512]{1,0:T(8,128)S(1)}, u32[]{:S(2)}, u32[]{:S(2)}) %collective-permute-start.8) | collective-permute-done | bytes 262176 | tf_op jit(solution)/shard_map/ppermute | solution.py:542
  104.1 9.8 %shard_map.116 = (f32[4,2560,512]{2,1,0:T(8,128)}, f32[512,128]{1,0:T(8,128)}, f32[512,128]{1,0:T(8,128)}, f32[512,128]{1,0:T(8,128)}, f32[1024,128]{1,0:T(8,128)}) custom-call(s32[1]{0:T(128)} %bitcast.tok_ref, s32[7]{0:T(128)} %fork_ref.3, s32[8]{0:T(128)} %live_ref.5, bf16[4,512,512]{2,1,0:T(8,128)(2,1)} %get-tuple-element.84.refs_0_, ...), custom_call_target="tpu_custom_call" | custom-call | flops 3221225472 | bytes 524288 | tf_op jit(solution)/shard_map/pallas_call | solution.py:501
  117.8 14.9 %collective-permute-start.20 = (f32[128,512]{1,0:T(8,128)}, f32[128,512]{1,0:T(8,128)}, u32[]{:S(2)}, u32[]{:S(2)}) collective-permute-start(f32[128,512]{1,0:T(8,128)} %bitcast.22), channel_id=1, source_target_pairs={{0,24},{4,28},{8,16},{12,20},{1,25},{5,29},{9,17},{13,21},{2,26},{... | collective-permute-start | bytes 786440 | tf_op jit(solution)/shard_map/ppermute | solution.py:552
  141.8 3.1 %reduce-scatter.8.cloned.1.call-done = f32[1,128,512]{2,1,0:T(8,128)} async-done(((f32[4,128,512]{2,1,0:T(8,128)}), f32[1,128,512]{2,1,0:T(8,128)}) %reduce-scatter.8.cloned.1.call-update) | async-done | bytes 262160 | tf_op jit(solution)/shard_map/reduce_scatter | solution.py:595
  144.9 11.6 %shard_map.121 = (f32[1024,256]{1,0:T(8,128)}, f32[512,128]{1,0:T(8,128)}, f32[512,128]{1,0:T(8,128)}, f32[512,128]{1,0:T(8,128)}, f32[1024,128]{1,0:T(8,128)}) custom-call(s32[1]{0:T(128)} %bitcast.tok_ref, s32[7]{0:T(128)} %fork_ref.3, s32[8]{0:T(128)} %live_ref.5, bf16[4,512,512]{2,1,0:T(8,128)(2,1)} %get-tuple-element.81.refs_0_, ...), custom_call_target="tpu_custom_call" | custom-call | flops 6442450944 | bytes 524288 | tf_op jit(solution)/shard_map/pallas_call | solution.py:517
  160.7 7.3 %collective-permute-done.21.refs_0_ = f32[512,128]{1,0:T(8,128)S(1)} collective-permute-done((f32[512,128]{1,0:T(8,128)}, f32[512,128]{1,0:T(8,128)S(1)}, u32[]{:S(2)}, u32[]{:S(2)}) %collective-permute-start.21) | collective-permute-done | bytes 262176 | tf_op jit(solution)/shard_map/ppermute | solution.py:552
  168.0 6.1 %collective-permute-done.22.refs_1_ = f32[512,128]{1,0:T(8,128)S(1)} collective-permute-done((f32[512,128]{1,0:T(8,128)}, f32[512,128]{1,0:T(8,128)S(1)}, u32[]{:S(2)}, u32[]{:S(2)}) %collective-permute-start.22) | collective-permute-done | bytes 262176 | tf_op jit(solution)/shard_map/ppermute | solution.py:552
  174.1 10.0 %collective-permute-done.23.refs_2_ = f32[512,128]{1,0:T(8,128)S(1)} collective-permute-done((f32[512,128]{1,0:T(8,128)}, f32[512,128]{1,0:T(8,128)S(1)}, u32[]{:S(2)}, u32[]{:S(2)}) %collective-permute-start.23) | collective-permute-done | bytes 262176 | tf_op jit(solution)/shard_map/ppermute | solution.py:552
  200.5 4.0 %shard_map.124 = (f32[672,128]{1,0:T(8,128)S(1)}, f32[672,128]{1,0:T(8,128)S(1)}, f32[672,128]{1,0:T(8,128)S(1)}, f32[672,128]{1,0:T(8,128)S(1)}) custom-call(s32[4]{0:T(128)S(1)} %iota_xor_fusion.place_ref, bf16[1344,1024]{1,0:T(8,128)(2,1)S(1)} %shard_map.110.refs_0_, bf16[1344,1024]{1,0:T(8,128)(2,1)S(1)} %copy-done.2, f32[4,1024,128]{2,1,0:T(8,128)S(1)} %bitcast.13, ...), custom_call_target="tpu_custom_call" | custom-call | flops 2113929216 | bytes 5505024 | tf_op jit(solution)/shard_map/pallas_call | solution.py:154
  206.0 3.6 %collective-permute-done.25 = f32[672,128]{1,0:T(8,128)S(1)} collective-permute-done((f32[672,128]{1,0:T(8,128)S(1)}, f32[672,128]{1,0:T(8,128)S(1)}, u32[]{:S(2)}, u32[]{:S(2)}) %collective-permute-start.25) | collective-permute-done | bytes 344096 | tf_op jit(solution)/shard_map/ppermute | solution.py:542
  217.5 3.2 %collective-permute-done.26 = f32[672,128]{1,0:T(8,128)S(1)} collective-permute-done((f32[672,128]{1,0:T(8,128)S(1)}, f32[672,128]{1,0:T(8,128)S(1)}, u32[]{:S(2)}, u32[]{:S(2)}) %collective-permute-start.26) | collective-permute-done | bytes 344096 | tf_op jit(solution)/shard_map/ppermute | solution.py:542
  220.8 4.6 %collective-permute-done.29 = f32[672,128]{1,0:T(8,128)S(1)} collective-permute-done((f32[672,128]{1,0:T(8,128)S(1)}, f32[672,128]{1,0:T(8,128)S(1)}, u32[]{:S(2)}, u32[]{:S(2)}) %collective-permute-start.29) | collective-permute-done | bytes 344096 | tf_op jit(solution)/shard_map/ppermute | solution.py:542
  230.9 6.8 %all-gather.5.cloned.1.call-done = f32[4096,128]{1,0:T(8,128)} async-done(((f32[1024,128]{1,0:T(8,128)}), f32[4096,128]{1,0:T(8,128)}) %all-gather.5.cloned.1.call-update) | async-done | bytes 2097168 | tf_op jit(solution)/shard_map/all_gather | solution.py:598
  246.0 4.0 %shard_map.129 = (f32[672,128]{1,0:T(8,128)S(1)}, f32[672,128]{1,0:T(8,128)S(1)}, f32[672,128]{1,0:T(8,128)S(1)}, f32[672,128]{1,0:T(8,128)S(1)}) custom-call(s32[4]{0:T(128)S(1)} %iota_xor_fusion.place_ref, bf16[1344,1024]{1,0:T(8,128)(2,1)S(1)} %shard_map.126.refs_0_, bf16[1344,1024]{1,0:T(8,128)(2,1)S(1)} %copy-done.6, f32[4,1024,128]{2,1,0:T(8,128)S(1)} %bitcast.9, ...), custom_call_target="tpu_custom_call" | custom-call | flops 2113929216 | bytes 5505024 | tf_op jit(solution)/shard_map/pallas_call | solution.py:154
  250.7 3.0 %collective-permute-done.34 = f32[672,128]{1,0:T(8,128)S(1)} collective-permute-done((f32[672,128]{1,0:T(8,128)S(1)}, f32[672,128]{1,0:T(8,128)S(1)}, u32[]{:S(2)}, u32[]{:S(2)}) %collective-permute-start.34) | collective-permute-done | bytes 344096 | tf_op jit(solution)/shard_map/ppermute | solution.py:542
  261.1 3.7 %collective-permute-done.35 = f32[672,128]{1,0:T(8,128)S(1)} collective-permute-done((f32[672,128]{1,0:T(8,128)S(1)}, f32[672,128]{1,0:T(8,128)S(1)}, u32[]{:S(2)}, u32[]{:S(2)}) %collective-permute-start.35) | collective-permute-done | bytes 344096 | tf_op jit(solution)/shard_map/ppermute | solution.py:542
  264.8 4.4 %collective-permute-done.38 = f32[672,128]{1,0:T(8,128)S(1)} collective-permute-done((f32[672,128]{1,0:T(8,128)S(1)}, f32[672,128]{1,0:T(8,128)S(1)}, u32[]{:S(2)}, u32[]{:S(2)}) %collective-permute-start.38) | collective-permute-done | bytes 344096 | tf_op jit(solution)/shard_map/ppermute | solution.py:542
  (171 shorter events, 117.4 us)
Async XLA Ops:
  7.2 80.7 %reduce-scatter.4.cloned.1.call-start = ((), (), s32[]{:S(2)}) async-start(), calls=%async_computation.3 | async-start | bytes 2621440 | tf_op jit(solution)/shard_map/reduce_scatter | solution.py:595
  7.7 18.9 %collective-permute-start.1 = (f32[1344,128]{1,0:T(8,128)}, f32[1344,128]{1,0:T(8,128)}, u32[]{:S(2)}, u32[]{:S(2)}) collective-permute-start(f32[1344,128]{1,0:T(8,128)} %refs_2_.2), channel_id=1, source_target_pairs={{0,8},{4,12},{8,0},{12,4},{16,24},{20,28},{24,16},{28,20},{1,9},{5... | collective-permute-start | bytes 2064392 | tf_op jit(solution)/shard_map/ppermute | solution.py:542
  10.3 17.7 %collective-permute-start.2 = (f32[1344,128]{1,0:T(8,128)}, f32[1344,128]{1,0:T(8,128)S(1)}, u32[]{:S(2)}, u32[]{:S(2)}) collective-permute-start(f32[1344,128]{1,0:T(8,128)} %refs_2_.2), channel_id=1, source_target_pairs={{0,16},{4,20},{8,24},{12,28},{16,0},{20,4},{24,8},{28,12},{1,17},{... | collective-permute-start | bytes 2064392 | tf_op jit(solution)/shard_map/ppermute | solution.py:542
  42.8 75.0 %reduce-scatter.6.cloned.1.call-start = ((), (), s32[]{:S(2)}) async-start(), calls=%async_computation.4 | async-start | bytes 1310720 | tf_op jit(solution)/shard_map/reduce_scatter | solution.py:595
  43.8 15.8 %collective-permute-start.14 = (f32[1344,128]{1,0:T(8,128)S(1)}, f32[1344,128]{1,0:T(8,128)S(1)}, u32[]{:S(2)}, u32[]{:S(2)}) collective-permute-start(f32[1344,128]{1,0:T(8,128)S(1)} %copy-done.14), channel_id=1, source_target_pairs={{0,8},{4,12},{8,0},{12,4},{16,24},{20,28},{24,16},{28,20},{1,9},{5... | collective-permute-start | bytes 2064392 | tf_op jit(solution)/shard_map/ppermute | solution.py:542
  45.1 15.2 %collective-permute-start.15 = (f32[1344,128]{1,0:T(8,128)S(1)}, f32[1344,128]{1,0:T(8,128)S(1)}, u32[]{:S(2)}, u32[]{:S(2)}) collective-permute-start(f32[1344,128]{1,0:T(8,128)S(1)} %copy-done.14), channel_id=1, source_target_pairs={{0,16},{4,20},{8,24},{12,28},{16,0},{20,4},{24,8},{28,12},{1,17},{... | collective-permute-start | bytes 2064392 | tf_op jit(solution)/shard_map/ppermute | solution.py:542
  73.6 71.3 %reduce-scatter.8.cloned.1.call-start = ((), (), s32[]{:S(2)}) async-start(), calls=%async_computation.5 | async-start | bytes 1310720 | tf_op jit(solution)/shard_map/reduce_scatter | solution.py:595
  77.6 115.7 %all-gather.7.cloned.1.call-start = ((), (), s32[]{:S(2)}) async-start(), calls=%async_computation.7 | async-start | bytes 2621440 | tf_op jit(solution)/shard_map/all_gather | solution.py:598
  113.9 20.8 %collective-permute-start.11 = (f32[512,128]{1,0:T(8,128)}, f32[512,128]{1,0:T(8,128)S(1)}, u32[]{:S(2)}, u32[]{:S(2)}) collective-permute-start(f32[512,128]{1,0:T(8,128)} %get-tuple-element.88), channel_id=1, source_target_pairs={{8,0},{12,4},{24,16},{28,20},{9,1},{13,5},{25,17},{29,21},{10,2},{... | collective-permute-start | bytes 786440 | tf_op jit(solution)/shard_map/ppermute | solution.py:552
  115.2 22.0 %collective-permute-start.12 = (f32[512,128]{1,0:T(8,128)}, f32[512,128]{1,0:T(8,128)S(1)}, u32[]{:S(2)}, u32[]{:S(2)}) collective-permute-start(f32[512,128]{1,0:T(8,128)} %get-tuple-element.89), channel_id=1, source_target_pairs={{16,0},{20,4},{24,8},{28,12},{17,1},{21,5},{25,9},{29,13},{18,2},{... | collective-permute-start | bytes 786440 | tf_op jit(solution)/shard_map/ppermute | solution.py:552
  116.5 21.2 %collective-permute-start.13 = (f32[512,128]{1,0:T(8,128)}, f32[512,128]{1,0:T(8,128)S(1)}, u32[]{:S(2)}, u32[]{:S(2)}) collective-permute-start(f32[512,128]{1,0:T(8,128)} %get-tuple-element.90), channel_id=1, source_target_pairs={{16,8},{20,12},{24,0},{28,4},{17,9},{21,13},{25,1},{29,5},{18,10},... | collective-permute-start | bytes 786440 | tf_op jit(solution)/shard_map/ppermute | solution.py:552
  117.8 21.8 %collective-permute-start.20 = (f32[128,512]{1,0:T(8,128)}, f32[128,512]{1,0:T(8,128)}, u32[]{:S(2)}, u32[]{:S(2)}) collective-permute-start(f32[128,512]{1,0:T(8,128)} %bitcast.22), channel_id=1, source_target_pairs={{0,24},{4,28},{8,16},{12,20},{1,25},{5,29},{9,17},{13,21},{2,26},{... | collective-permute-start | bytes 786440 | tf_op jit(solution)/shard_map/ppermute | solution.py:552
  144.9 92.8 %all-gather.5.cloned.1.call-start = ((), (), s32[]{:S(2)}) async-start(), calls=%async_computation.6 | async-start | bytes 2621440 | tf_op jit(solution)/shard_map/all_gather | solution.py:598
  156.6 11.5 %collective-permute-start.21 = (f32[512,128]{1,0:T(8,128)}, f32[512,128]{1,0:T(8,128)S(1)}, u32[]{:S(2)}, u32[]{:S(2)}) collective-permute-start(f32[512,128]{1,0:T(8,128)} %get-tuple-element.110), channel_id=1, source_target_pairs={{8,0},{12,4},{24,16},{28,20},{9,1},{13,5},{25,17},{29,21},{10,2},{... | collective-permute-start | bytes 786440 | tf_op jit(solution)/shard_map/ppermute | solution.py:552
  157.9 16.2 %collective-permute-start.22 = (f32[512,128]{1,0:T(8,128)}, f32[512,128]{1,0:T(8,128)S(1)}, u32[]{:S(2)}, u32[]{:S(2)}) collective-permute-start(f32[512,128]{1,0:T(8,128)} %get-tuple-element.111), channel_id=1, source_target_pairs={{16,0},{20,4},{24,8},{28,12},{17,1},{21,5},{25,9},{29,13},{18,2},{... | collective-permute-start | bytes 786440 | tf_op jit(solution)/shard_map/ppermute | solution.py:552
  159.2 24.9 %collective-permute-start.23 = (f32[512,128]{1,0:T(8,128)}, f32[512,128]{1,0:T(8,128)S(1)}, u32[]{:S(2)}, u32[]{:S(2)}) collective-permute-start(f32[512,128]{1,0:T(8,128)} %get-tuple-element.112), channel_id=1, source_target_pairs={{16,8},{20,12},{24,0},{28,4},{17,9},{21,13},{25,1},{29,5},{18,10},... | collective-permute-start | bytes 786440 | tf_op jit(solution)/shard_map/ppermute | solution.py:552
  192.0 17.8 %collective-permute-start.30 = (f32[512,256]{1,0:T(8,128)}, f32[512,256]{1,0:T(8,128)}, u32[]{:S(2)}, u32[]{:S(2)}) collective-permute-start(f32[512,256]{1,0:T(8,128)} %get-tuple-element.144), channel_id=1, source_target_pairs={{0,4},{4,0},{8,12},{12,8},{16,20},{20,16},{24,28},{28,24},{1,5},{5... | collective-permute-start | bytes 1572872 | tf_op jit(solution)/shard_map/ppermute | solution.py:542
  198.7 17.9 %collective-permute-start.27 = (f32[672,128]{1,0:T(8,128)S(1)}, f32[672,128]{1,0:T(8,128)S(1)}, u32[]{:S(2)}, u32[]{:S(2)}) collective-permute-start(f32[672,128]{1,0:T(8,128)S(1)} %get-tuple-element.121), channel_id=1, source_target_pairs={{0,16},{4,20},{8,24},{12,28},{16,0},{20,4},{24,8},{28,12},{1,17},{... | collective-permute-start | bytes 1032200 | tf_op jit(solution)/shard_map/ppermute | solution.py:542
  200.4 16.3 %collective-permute-start.31 = (f32[512,128]{1,0:T(8,128)S(1)}, f32[512,128]{1,0:T(8,128)S(1)}, u32[]{:S(2)}, u32[]{:S(2)}) collective-permute-start(f32[512,128]{1,0:T(8,128)S(1)} %get-tuple-element.152), channel_id=1, source_target_pairs={{0,4},{4,0},{8,12},{12,8},{16,20},{20,16},{24,28},{28,24},{1,5},{5... | collective-permute-start | bytes 786440 | tf_op jit(solution)/shard_map/ppermute | solution.py:542
  204.5 13.0 %collective-permute-start.24 = (f32[672,128]{1,0:T(8,128)S(1)}, f32[672,128]{1,0:T(8,128)S(1)}, u32[]{:S(2)}, u32[]{:S(2)}) collective-permute-start(f32[672,128]{1,0:T(8,128)S(1)} %get-tuple-element.116), channel_id=1, source_target_pairs={{0,8},{4,12},{8,0},{12,4},{16,24},{20,28},{24,16},{28,20},{1,9},{5... | collective-permute-start | bytes 1032200 | tf_op jit(solution)/shard_map/ppermute | solution.py:542
  212.1 13.3 %collective-permute-start.29 = (f32[672,128]{1,0:T(8,128)S(1)}, f32[672,128]{1,0:T(8,128)S(1)}, u32[]{:S(2)}, u32[]{:S(2)}) collective-permute-start(f32[672,128]{1,0:T(8,128)S(1)} %get-tuple-element.122), channel_id=1, source_target_pairs={{0,16},{4,20},{8,24},{12,28},{16,0},{20,4},{24,8},{28,12},{1,17},{... | collective-permute-start | bytes 1032200 | tf_op jit(solution)/shard_map/ppermute | solution.py:542
  244.5 11.3 %collective-permute-start.36 = (f32[672,128]{1,0:T(8,128)S(1)}, f32[672,128]{1,0:T(8,128)S(1)}, u32[]{:S(2)}, u32[]{:S(2)}) collective-permute-start(f32[672,128]{1,0:T(8,128)S(1)} %get-tuple-element.140), channel_id=1, source_target_pairs={{0,16},{4,20},{8,24},{12,28},{16,0},{20,4},{24,8},{28,12},{1,17},{... | collective-permute-start | bytes 1032200 | tf_op jit(solution)/shard_map/ppermute | solution.py:542
  255.6 13.7 %collective-permute-start.38 = (f32[672,128]{1,0:T(8,128)S(1)}, f32[672,128]{1,0:T(8,128)S(1)}, u32[]{:S(2)}, u32[]{:S(2)}) collective-permute-start(f32[672,128]{1,0:T(8,128)S(1)} %get-tuple-element.141), channel_id=1, source_target_pairs={{0,16},{4,20},{8,24},{12,28},{16,0},{20,4},{24,8},{28,12},{1,17},{... | collective-permute-start | bytes 1032200 | tf_op jit(solution)/shard_map/ppermute | solution.py:542
  255.9 13.4 %collective-permute-start.37 = (f32[672,128]{1,0:T(8,128)S(1)}, f32[672,128]{1,0:T(8,128)S(1)}, u32[]{:S(2)}, u32[]{:S(2)}) collective-permute-start(f32[672,128]{1,0:T(8,128)S(1)} %add.67), channel_id=1, source_target_pairs={{0,8},{4,12},{8,0},{12,4},{16,24},{20,28},{24,16},{28,20},{1,9},{5... | collective-permute-start | bytes 1032200 | tf_op jit(solution)/shard_map/ppermute | solution.py:542
  (45 other events, 253.3 us)
Sparse Core Ops, SparseCore 0:
  42.9 44.9 reduce-scatter.3
  90.2 26.4 reduce-scatter.5
  119.0 25.7 reduce-scatter.7
  146.4 44.5 all-gather.6
  193.1 44.5 all-gather.4
